TPU v7x, 32 devices: a whole 2x2x4 slice. The times are simulated.
32 devices in a mesh: dp: 2 (over x), expert: 16 (over z, y, core).
Axes of the slice: x: 2, y: 2, z: 4, core: 2. Of those that a mesh axis runs over, the one named last changes fastest.
Arguments:
- tokens: bfloat16 [2048, 4096], P('expert', 'dp'), may hold values from -6 to 6
- routing: int32 [2048, 8], P('expert'), may hold values from 0 to 15, all different within a row; in each aligned block of 128 rows (0 to 127, 128 to 255, ...) at most 80 rows name the same one
- gate_probs: float32 [2048, 8], P('expert'), may hold values from 0.05 to 0.3
- paired: int32 [16], P('expert'), may hold values from 0 to 1, as said below
- w_gate: bfloat16 [16, 4096, 768], P('expert', 'dp'), may hold values from -0.09375 to 0.09375
- w_up: bfloat16 [16, 4096, 768], P('expert', 'dp'), may hold values from -0.09375 to 0.09375
- w_down: bfloat16 [16, 768, 4096], P('expert', None, 'dp'), may hold values from -0.21875 to 0.21875
- cotangent: bfloat16 [2048, 4096], P('expert', 'dp'), may hold values from -6 to 6
Outputs:
- output: bfloat16 [2048, 4096], P('expert', 'dp')
- grad_tokens: bfloat16 [2048, 4096], P('expert', 'dp')
- grad_gate: float32 [16, 4096, 768], P('expert', 'dp')
- grad_up: float32 [16, 4096, 768], P('expert', 'dp')
- grad_down: float32 [16, 768, 4096], P('expert', None, 'dp')
Inputs may be any that keep to these rules, and one draw needn't show every extreme that they name: `routing`: each token names 8 different copies; among the tokens of one source (aligned blocks of 128 tokens) no copy is named more than 80 times, a bound that some block reaches. paired[c] equals paired[(c + 8) mod 16]; paired[0] and paired[15] are 1.
All inputs are finite; a program needn't handle non-finite values.
Results may differ from a plain program's by a relative error of at most 0.029.
Values may be sent and summed in bfloat16 or wider, within the bound.
No kernel may reach another device: no remote copies, remote signals or barrier semaphores. Data moves between devices by JAX's collectives and lax.ppermute only.
A program may use at most 128 MiB of HBM per device.

v0:
```python
import jax
import jax.numpy as jnp
from jax import lax
from jax.sharding import PartitionSpec as P


def swapped(value, axis, stride):
    mask = 2**stride
    pairs = [(source, source ^ mask) for source in range(lax.axis_size(axis))]
    return lax.ppermute(value, axis, pairs)


def product(left, right):
    return jnp.dot(left, right, preferred_element_type=jnp.float32)


def inner_rows(left, right):
    return lax.dot_general(
        left, right, (((0,), (0,)), ((), ())), preferred_element_type=jnp.float32
    )


def outer_cols(left, right):
    return lax.dot_general(
        left, right, (((1,), (1,)), ((), ())), preferred_element_type=jnp.float32
    )


def rounded(value):
    return lax.optimization_barrier(value.astype(jnp.bfloat16)).astype(jnp.float32)


def per_device(tokens, routing, gate_probs, paired, w_gate, w_up, w_down, cotangent):
    n_expert = lax.axis_size("expert")
    n_data = lax.axis_size("dp")
    token_count, top_count = routing.shape
    slab = tokens.shape[1]
    hidden = w_gate.shape[2]
    capacity = max(2, 5 * token_count * top_count // (4 * n_expert))
    all_rows = n_expert * capacity
    own_rows = all_rows // n_data
    gate_slab = w_gate[0]
    up_slab = w_up[0]
    down_slab = w_down[0]
    flat_route = routing.reshape(token_count * top_count)
    onehot = (flat_route[:, None] == jnp.arange(n_expert, dtype=jnp.int32)[None, :]).astype(
        jnp.int32
    )
    earlier = jnp.cumsum(onehot, axis=0) - onehot
    target = flat_route * capacity + jnp.sum(earlier * onehot, axis=1)
    select = jnp.arange(all_rows, dtype=jnp.int32)[:, None] == target[None, :]
    select_grid = select.reshape(all_rows, token_count, top_count)
    token_select = jnp.any(select_grid, axis=2).astype(jnp.bfloat16)
    weight_select = jnp.sum(select_grid.astype(jnp.float32) * gate_probs[None, :, :], axis=2)
    weight_high = weight_select.astype(jnp.bfloat16)
    weight_low = (weight_select - weight_high.astype(jnp.float32)).astype(jnp.bfloat16)
    send_tokens = product(token_select, tokens).astype(jnp.bfloat16)
    scaled = (gate_probs[:, :, None] * cotangent.astype(jnp.float32)[:, None, :]).astype(
        jnp.bfloat16
    )
    send_grads = product(
        select.astype(jnp.bfloat16), scaled.reshape(token_count * top_count, slab)
    ).astype(jnp.bfloat16)
    arrived = (
        lax.all_to_all(
            send_tokens.reshape(n_expert, capacity, slab),
            "expert",
            split_axis=0,
            concat_axis=0,
            tiled=True,
        ),
        lax.all_to_all(
            send_grads.reshape(n_expert, capacity, slab),
            "expert",
            split_axis=0,
            concat_axis=0,
            tiled=True,
        ),
    )
    token_slab = arrived[0].reshape(all_rows, slab)
    grad_slab = arrived[1].reshape(all_rows, slab)
    block_rows = token_slab
    summed = lax.psum_scatter(
        rounded(
            jnp.concatenate([product(block_rows, gate_slab), product(block_rows, up_slab)], axis=1)
        ).astype(jnp.bfloat16),
        "dp",
        scatter_dimension=0,
        tiled=True,
    ).astype(jnp.float32)
    gate_own = summed[:, :hidden]
    up_own = summed[:, hidden:]
    hid_own = (jax.nn.silu(gate_own) * up_own).astype(jnp.bfloat16)
    piece = lax.all_gather(hid_own, "dp", axis=0, tiled=True)
    answer_acc = product(piece, down_slab)
    grad_down = inner_rows(piece, grad_slab)
    answer_slab = answer_acc.astype(jnp.bfloat16)
    answer_back = lax.all_to_all(
        answer_slab.reshape(n_expert, capacity, slab),
        "expert",
        split_axis=0,
        concat_axis=0,
        tiled=True,
    )
    hidden_parts = (
        outer_cols(grad_slab, down_slab).astype(jnp.bfloat16).reshape(n_data, own_rows, hidden)
    )
    arrived_parts = lax.all_to_all(hidden_parts, "dp", split_axis=0, concat_axis=0, tiled=True)
    grad_hidden = jnp.sum(arrived_parts.astype(jnp.float32), axis=0)
    sigma = jax.nn.sigmoid(gate_own)
    activated = gate_own * sigma
    grad_gate_rows = (grad_hidden * up_own * sigma * (1.0 + gate_own * (1.0 - sigma))).astype(
        jnp.bfloat16
    )
    grad_up_rows = (grad_hidden * activated).astype(jnp.bfloat16)
    piece_gate = lax.all_gather(grad_gate_rows, "dp", axis=0, tiled=True)
    piece_up = lax.all_gather(grad_up_rows, "dp", axis=0, tiled=True)
    block_rows = token_slab
    gate_acc = inner_rows(block_rows, piece_gate)
    up_acc = inner_rows(block_rows, piece_up)
    back_rows = outer_cols(piece_gate, gate_slab) + outer_cols(piece_up, up_slab)
    grad_gate = gate_acc
    grad_up = up_acc
    back_slab = back_rows.astype(jnp.bfloat16)
    back_rows_home = lax.all_to_all(
        back_slab.reshape(n_expert, capacity, slab),
        "expert",
        split_axis=0,
        concat_axis=0,
        tiled=True,
    )
    answer_home = answer_back.reshape(all_rows, slab)
    output = (inner_rows(weight_high, answer_home) + inner_rows(weight_low, answer_home)).astype(
        jnp.bfloat16
    )
    grad_tokens = inner_rows(token_select, back_rows_home.reshape(all_rows, slab)).astype(
        jnp.bfloat16
    )
    other = (
        swapped(grad_gate.astype(jnp.bfloat16), "expert", n_expert.bit_length() - 2).astype(
            grad_gate.dtype
        ),
        swapped(grad_up.astype(jnp.bfloat16), "expert", n_expert.bit_length() - 2).astype(
            grad_up.dtype
        ),
        swapped(grad_down.astype(jnp.bfloat16), "expert", n_expert.bit_length() - 2).astype(
            grad_down.dtype
        ),
    )
    keep = paired.astype(jnp.float32)[0]
    grad_gate = (grad_gate + keep * other[0])[None]
    grad_up = (grad_up + keep * other[1])[None]
    grad_down = (grad_down + keep * other[2])[None]
    return (output, grad_tokens, grad_gate, grad_up, grad_down)


def solution(mesh):
    return jax.shard_map(
        per_device,
        mesh=mesh,
        in_specs=(
            P("expert", "dp"),
            P("expert", None),
            P("expert", None),
            P("expert"),
            P("expert", "dp", None),
            P("expert", "dp", None),
            P("expert", None, "dp"),
            P("expert", "dp"),
        ),
        out_specs=(
            P("expert", "dp"),
            P("expert", "dp"),
            P("expert", "dp", None),
            P("expert", "dp", None),
            P("expert", None, "dp"),
        ),
        check_vma=False,
    )
```

profile of v0, /device:TPU:0, one launch (start us, length us, event | category | flops | bytes accessed | tf_op | source)
XLA Modules:
  0.0 1016.5 jit_solution(943002692804698102)
XLA Ops:
  7.2 0.0 copy-start
  7.2 0.9 copy.43
  8.1 0.1 eq.50
  8.2 0.1 eq.46
  8.3 4.5 reduce-window.6
  12.8 0.1 slice.16
  12.9 0.1 copy.45
  13.1 0.1 copy.46
  13.2 0.1 broadcast_add_fusion
  13.3 0.1 reduce_sum.30
  13.4 0.7 multiply_add_fusion.1
  14.1 4.6 fusion.1
  18.8 4.9 convolution_convert_fusion.2
  23.7 7.6 all-to-all-start
  31.3 2.1 convert_element_type.96
  33.4 0.1 copy.49
  33.5 0.1 mul.92
  33.6 8.5 convolution_convert_fusion
  42.1 85.1 %all-to-all-done = bf16[16,80,2048]{2,1,0:T(8,128)(2,1)} async-done(((bf16[16,80,2048]{2,1,0:T(8,128)(2,1)}), bf16[16,80,2048]{2,1,0:T(8,128)(2,1)}, u32[]{:S(2)}, u32[]{:S(2)}) %all-to-all-start) | async-done | bytes 5242912 | tf_op jit(solution)/shard_map/all_to_all | solution.py:65
  127.2 23.9 %all-to-all-start.2 = ((bf16[16,80,2048]{2,1,0:T(8,128)(2,1)}), bf16[16,80,2048]{2,1,0:T(8,128)(2,1)}, u32[]{:S(2)}, u32[]{:S(2)}) async-start(bf16[16,80,2048]{2,1,0:T(8,128)(2,1)} %bitcast.76), calls=%async_computation.2 | async-start | bytes 10485760 | tf_op jit(solution)/shard_map/all_to_all | solution.py:72
  151.1 0.5 reduce-scatter.4.cloned.1.call-start
  151.6 0.0 copy-start.5
  151.6 7.9 convolution_convert_fusion.4
  159.5 6.8 convolution_convert_fusion.5
  166.3 2.2 pad_maximum_fusion
  168.5 6.3 copy.50
  174.8 0.0 reduce-scatter.4.cloned.1.call-update
  174.8 0.2 all-gather.4.cloned.1.call-start
  175.0 72.0 %all-to-all-done.2 = bf16[16,80,2048]{2,1,0:T(8,128)(2,1)} async-done(((bf16[16,80,2048]{2,1,0:T(8,128)(2,1)}), bf16[16,80,2048]{2,1,0:T(8,128)(2,1)}, u32[]{:S(2)}, u32[]{:S(2)}) %all-to-all-start.2) | async-done | bytes 5242912 | tf_op jit(solution)/shard_map/all_to_all | solution.py:72
  247.1 6.8 convolution_convert_fusion.3
  253.8 27.2 %all_to_all.25 = bf16[2,640,768]{2,1,0:T(8,128)(2,1)S(1)} all-to-all(bf16[2,640,768]{2,1,0:T(8,128)(2,1)S(1)} %bitcast.77), channel_id=1, replica_groups=mesh['dp'=2,'expert'=16] {'dp'}, dimensions={0} | all-to-all | bytes 3932160 | tf_op jit(solution)/shard_map/all_to_all | solution.py:108
  281.0 1.6 convert_reduce_fusion
  282.6 2.2 convert_element_type.90
  284.9 3.0 multiply_convert_fusion
  287.8 0.0 all-gather.4.cloned.1.call-update
  287.8 49.6 %all-gather.4.cloned.1.call-done = bf16[1280,768]{1,0:T(8,128)(2,1)} async-done(((bf16[640,768]{1,0:T(8,128)(2,1)}), bf16[1280,768]{1,0:T(8,128)(2,1)}) %all-gather.4.cloned.1.call-update) | async-done | bytes 1966096 | tf_op jit(solution)/shard_map/all_gather | solution.py:94
  337.4 7.5 convolution_convert_fusion.1
  344.9 5.9 all-to-all-start.1
  350.8 0.0 all-gather.6.cloned.1.call-start
  350.9 0.7 all-gather.6.cloned.1.call-update
  351.5 0.0 all-gather.8.cloned.1.call-start
  351.6 0.5 all-gather.8.cloned.1.call-update
  352.1 33.7 %all-gather.6.cloned.1.call-done = bf16[1280,768]{1,0:T(8,128)(2,1)} async-done(((bf16[640,768]{1,0:T(8,128)(2,1)}), bf16[1280,768]{1,0:T(8,128)(2,1)}) %all-gather.6.cloned.1.call-update) | async-done | bytes 1966096 | tf_op jit(solution)/shard_map/all_gather | solution.py:116
  385.9 8.4 fusion.9
  394.2 25.4 %all-gather.8.cloned.1.call-done = bf16[1280,768]{1,0:T(8,128)(2,1)} async-done(((bf16[640,768]{1,0:T(8,128)(2,1)}), bf16[1280,768]{1,0:T(8,128)(2,1)}) %all-gather.8.cloned.1.call-update) | async-done | bytes 1966096 | tf_op jit(solution)/shard_map/all_gather | solution.py:117
  419.6 12.2 %add_convert_fusion = bf16[1280,2048]{1,0:T(8,128)(2,1)} fusion(f32[1280,2048]{1,0:T(8,128)} %fusion.9, bf16[1280,768]{1,0:T(8,128)(2,1)} %all-gather.8.cloned.1.call-done, bf16[1,2048,768]{2,1,0:T(8,128)(2,1)} %param.13), kind=kOutput, calls=%fused_computation | convolution fusion | flops 4031774720 | bytes 20840448 | tf_op jit(solution)/shard_map/dot_general | solution.py:24
  431.8 14.9 %all-to-all-done.1 = bf16[16,80,2048]{2,1,0:T(8,128)(2,1)} async-done(((bf16[16,80,2048]{2,1,0:T(8,128)(2,1)}), bf16[16,80,2048]{2,1,0:T(8,128)(2,1)}, u32[]{:S(2)}, u32[]{:S(2)}) %all-to-all-start.1) | async-done | bytes 5242912 | tf_op jit(solution)/shard_map/all_to_all | solution.py:98
  446.8 24.3 %all-to-all-start.4 = ((bf16[16,80,2048]{2,1,0:T(8,128)(2,1)}), bf16[16,80,2048]{2,1,0:T(8,128)(2,1)}, u32[]{:S(2)}, u32[]{:S(2)}) async-start(bf16[16,80,2048]{2,1,0:T(8,128)(2,1)} %bitcast.74), calls=%async_computation.4 | async-start | bytes 10485760 | tf_op jit(solution)/shard_map/all_to_all | solution.py:125
  471.0 6.5 fusion.22
  477.5 3.0 collective-permute-start
  480.5 8.5 fusion.23
  489.0 0.2 collective-permute-start.1
  489.2 8.4 fusion.24
  497.6 2.8 collective-permute-start.2
  501.0 7.0 select_reduce_fusion
  508.0 349.6 %collective-permute-done = bf16[2048,768]{1,0:T(8,128)(2,1)S(1)} collective-permute-done((bf16[2048,768]{1,0:T(8,128)(2,1)S(1)}, bf16[2048,768]{1,0:T(8,128)(2,1)S(1)}, u32[]{:S(2)}, u32[]{:S(2)}) %collective-permute-start) | collective-permute-done | bytes 3145760 | tf_op jit(solution)/shard_map/ppermute | solution.py:10
  857.6 3.3 add_bitcast_fusion.2
  860.9 64.2 %collective-permute-done.1 = bf16[2048,768]{1,0:T(8,128)(2,1)} collective-permute-done((bf16[2048,768]{1,0:T(8,128)(2,1)}, bf16[2048,768]{1,0:T(8,128)(2,1)}, u32[]{:S(2)}, u32[]{:S(2)}) %collective-permute-start.1) | collective-permute-done | bytes 3145760 | tf_op jit(solution)/shard_map/ppermute | solution.py:10
  925.1 5.2 add_bitcast_fusion.1
  930.3 61.7 %collective-permute-done.2 = bf16[768,2048]{1,0:T(8,128)(2,1)} collective-permute-done((bf16[768,2048]{1,0:T(8,128)(2,1)}, bf16[768,2048]{1,0:T(8,128)(2,1)}, u32[]{:S(2)}, u32[]{:S(2)}) %collective-permute-start.2) | collective-permute-done | bytes 3145760 | tf_op jit(solution)/shard_map/ppermute | solution.py:10
  992.1 5.6 add_bitcast_fusion
  997.6 3.4 fusion.16
  1001.0 4.3 fusion.13
  1005.3 4.2 convolution_convert_fusion.6
  (24 shorter events, 0.2 us)
Async XLA Ops:
  7.2 239.9 %copy-start = (bf16[1,768,2048]{2,1,0:T(8,128)(2,1)S(1)}, bf16[1,768,2048]{2,1,0:T(8,128)(2,1)}, u32[]{:S(2)}) copy-start(bf16[1,768,2048]{2,1,0:T(8,128)(2,1)} %param.14) | copy-start | bytes 9437188
  23.7 9.7 copy-start.4
  23.7 103.5 %all-to-all-start = ((bf16[16,80,2048]{2,1,0:T(8,128)(2,1)}), bf16[16,80,2048]{2,1,0:T(8,128)(2,1)}, u32[]{:S(2)}, u32[]{:S(2)}) async-start(bf16[16,80,2048]{2,1,0:T(8,128)(2,1)} %bitcast.73), calls=%async_computation | async-start | bytes 10485760 | tf_op jit(solution)/shard_map/all_to_all | solution.py:65
  127.2 119.8 %all-to-all-start.2 = ((bf16[16,80,2048]{2,1,0:T(8,128)(2,1)}), bf16[16,80,2048]{2,1,0:T(8,128)(2,1)}, u32[]{:S(2)}, u32[]{:S(2)}) async-start(bf16[16,80,2048]{2,1,0:T(8,128)(2,1)} %bitcast.76), calls=%async_computation.2 | async-start | bytes 10485760 | tf_op jit(solution)/shard_map/all_to_all | solution.py:72
  151.1 131.5 %reduce-scatter.4.cloned.1.call-start = ((), (), s32[]{:S(2)}) async-start(), calls=%async_computation.9 | async-start | bytes 5898240 | tf_op jit(solution)/shard_map/reduce_scatter | solution.py:83
  151.6 7.9 copy-start.5
  174.8 162.6 %all-gather.4.cloned.1.call-start = ((), (), s32[]{:S(2)}) async-start(), calls=%async_computation.6 | async-start | bytes 2949120 | tf_op jit(solution)/shard_map/all_gather | solution.py:94
  282.6 2.2 copy-start.2
  344.9 41.0 %copy-start.6 = (bf16[1,2048,768]{2,1,0:T(8,128)(2,1)S(1)}, bf16[1,2048,768]{2,1,0:T(8,128)(2,1)}, u32[]{:S(2)}) copy-start(bf16[1,2048,768]{2,1,0:T(8,128)(2,1)} %param.12) | copy-start | bytes 9437188
  344.9 101.9 %all-to-all-start.1 = ((bf16[16,80,2048]{2,1,0:T(8,128)(2,1)}), bf16[16,80,2048]{2,1,0:T(8,128)(2,1)}, u32[]{:S(2)}, u32[]{:S(2)}) async-start(bf16[16,80,2048]{2,1,0:T(8,128)(2,1)} %bitcast.75), calls=%async_computation.1 | async-start | bytes 10485760 | tf_op jit(solution)/shard_map/all_to_all | solution.py:98
  350.8 35.1 %all-gather.6.cloned.1.call-start = ((), (), s32[]{:S(2)}) async-start(), calls=%async_computation.7 | async-start | bytes 2949120 | tf_op jit(solution)/shard_map/all_gather | solution.py:116
  351.5 68.0 %all-gather.8.cloned.1.call-start = ((), (), s32[]{:S(2)}) async-start(), calls=%async_computation.8 | async-start | bytes 2949120 | tf_op jit(solution)/shard_map/all_gather | solution.py:117
  446.7 24.3 %copy-start.7 = (bf16[1280,768]{1,0:T(8,128)(2,1)S(1)}, bf16[1280,768]{1,0:T(8,128)(2,1)}, u32[]{:S(2)}) copy-start(bf16[1280,768]{1,0:T(8,128)(2,1)} %all-gather.6.cloned.1.call-done) | copy-start | bytes 5898244
  446.8 558.6 %all-to-all-start.4 = ((bf16[16,80,2048]{2,1,0:T(8,128)(2,1)}), bf16[16,80,2048]{2,1,0:T(8,128)(2,1)}, u32[]{:S(2)}, u32[]{:S(2)}) async-start(bf16[16,80,2048]{2,1,0:T(8,128)(2,1)} %bitcast.74), calls=%async_computation.4 | async-start | bytes 10485760 | tf_op jit(solution)/shard_map/all_to_all | solution.py:125
  471.0 9.5 copy-start.8
  477.5 11.7 %copy-start.3 = (bf16[1280,768]{1,0:T(8,128)(2,1)S(1)}, bf16[1280,768]{1,0:T(8,128)(2,1)}, u32[]{:S(2)}) copy-start(bf16[1280,768]{1,0:T(8,128)(2,1)} %all-gather.4.cloned.1.call-done) | copy-start | bytes 5898244
  477.5 380.1 %collective-permute-start = (bf16[2048,768]{1,0:T(8,128)(2,1)S(1)}, bf16[2048,768]{1,0:T(8,128)(2,1)S(1)}, u32[]{:S(2)}, u32[]{:S(2)}) collective-permute-start(bf16[2048,768]{1,0:T(8,128)(2,1)S(1)} %get-tuple-element.8), channel_id=1, source_target_pairs={{0,8},{1,9},{2,10},{3,11},{4,12},{5,13},{6,14},{7,15},{8,0},{9,1},... | collective-permute-start | bytes 9437192 | tf_op jit(solution)/shard_map/ppermute | solution.py:10
  489.0 436.1 %collective-permute-start.1 = (bf16[2048,768]{1,0:T(8,128)(2,1)}, bf16[2048,768]{1,0:T(8,128)(2,1)}, u32[]{:S(2)}, u32[]{:S(2)}) collective-permute-start(bf16[2048,768]{1,0:T(8,128)(2,1)} %get-tuple-element.10), channel_id=1, source_target_pairs={{0,8},{1,9},{2,10},{3,11},{4,12},{5,13},{6,14},{7,15},{8,0},{9,1},... | collective-permute-start | bytes 9437192 | tf_op jit(solution)/shard_map/ppermute | solution.py:10
  497.6 494.5 %collective-permute-start.2 = (bf16[768,2048]{1,0:T(8,128)(2,1)}, bf16[768,2048]{1,0:T(8,128)(2,1)}, u32[]{:S(2)}, u32[]{:S(2)}) collective-permute-start(bf16[768,2048]{1,0:T(8,128)(2,1)} %get-tuple-element.12), channel_id=1, source_target_pairs={{0,8},{1,9},{2,10},{3,11},{4,12},{5,13},{6,14},{7,15},{8,0},{9,1},... | collective-permute-start | bytes 9437192 | tf_op jit(solution)/shard_map/ppermute | solution.py:10
  1001.0 8.5 copy-start.1
Sparse Core Ops, SparseCore 0:
  174.9 53.2 reduce-scatter.3
  288.0 49.3 all-gather.3
  353.8 31.9 all-gather.5
  387.9 31.6 all-gather.7
where the time goes:
time: 1020 us
  waiting for transfers between devices  757 us (74%)
  matrix products  98.2 us (10%)
  starting transfers between devices  68.3 us (7%)
  other arithmetic  42.2 us (4%)
  blocking collectives  27.2 us (3%)
  between operations  15.1 us (1%)
    ppermute x3, waiting for transfers between devices, swapped(): return lax.ppermute(value, axis, pairs)  476 us
    all_to_all x1, waiting for transfers between devices, per_device(): lax.all_to_all(send_tokens.reshape(n_expert, capacity, slab), 'expert', s...  85.1 us
    all_to_all x1, waiting for transfers between devices, per_device(): lax.all_to_all(send_grads.reshape(n_expert, capacity, slab), 'expert', sp...  72 us
    all_gather x1, waiting for transfers between devices, per_device(): piece = lax.all_gather(hid_own, 'dp', axis=0, tiled=True)  49.6 us
    dot_general x5, matrix products, product(): return jnp.dot(left, right, preferred_element_type=jnp.float32)  35.6 us
    dot_general x6, matrix products, inner_rows(): lax.dot_general(left, right, (((0,), (0,)), ((), ())), preferred_element_...  35.3 us
    all_gather x1, waiting for transfers between devices, per_device(): piece_gate = lax.all_gather(grad_gate_rows, 'dp', axis=0, tiled=True)  33.7 us
    dot_general x3, matrix products, outer_cols(): lax.dot_general(left, right, (((1,), (1,)), ((), ())), preferred_element_...  27.4 us
  transfers between devices with their start and end apart: 11, of which 9 were waited for; matrix products, arithmetic and copies ran while one was open for 11% of the time, Pallas kernels for 0%

commit v1 on v0

v1 whole, which is shorter than its diff:
```python
import jax
import jax.numpy as jnp
from jax import lax
from jax.sharding import PartitionSpec as P

BF = jnp.bfloat16
F32 = jnp.float32


def exchange(value, axis, bit):
    pairs = [(source, source ^ bit) for source in range(lax.axis_size(axis))]
    return lax.ppermute(value, axis, pairs)


def product(left, right):
    return jnp.dot(left, right, preferred_element_type=F32)


def contract(left, right, dims):
    return lax.dot_general(left, right, (dims, ((), ())), preferred_element_type=F32)


def batched(left, right, dims):
    return lax.dot_general(left, right, (dims, ((0,), (0,))), preferred_element_type=F32)


def split_exact(value):
    high = lax.reduce_precision(value, 8, 7)
    rest = value - high
    middle = lax.reduce_precision(rest, 8, 7)
    return [high.astype(BF), middle.astype(BF), (rest - middle).astype(BF)]


def bits_of(count):
    return [1 << place for place in reversed(range(count.bit_length() - 1))]


def gather_sources(block, order, bits, flip):
    current = block.reshape((1,) * len(bits) + block.shape)
    for bit in order:
        place = bits.index(bit)
        other = exchange(current, "expert", bit)
        if flip is not None and place == 0:
            first, second = jnp.where(flip, other, current), jnp.where(flip, current, other)
        else:
            first, second = current, other
        current = jnp.concatenate([first, second], axis=place)
    return current.reshape((2 ** len(bits),) + block.shape)


def scatter_sources(blocks, order, bits, flip):
    current = blocks.reshape((2,) * len(bits) + blocks.shape[1:])
    for bit in order:
        place = bits.index(bit)
        first = lax.slice_in_dim(current, 0, 1, axis=place)
        second = lax.slice_in_dim(current, 1, 2, axis=place)
        if flip is not None and place == 0:
            first, second = jnp.where(flip, second, first), jnp.where(flip, first, second)
        other = exchange(second, "expert", bit)
        current = (first.astype(F32) + other.astype(F32)).astype(BF)
    return current.reshape(blocks.shape[1:])


def per_device(tokens, routing, gate_probs, paired, w_gate, w_up, w_down, cotangent):
    n_expert = lax.axis_size("expert")
    n_data = lax.axis_size("dp")
    token_count, top_count = routing.shape
    slab = tokens.shape[1]
    hidden = w_gate.shape[2]
    capacity = max(2, 5 * token_count * top_count // (4 * n_expert))
    all_rows = n_expert * capacity
    own_rows = all_rows // n_data
    half = slab // 2
    bits = bits_of(n_expert)
    top = bits[0]
    paired_dp = n_data == 2
    flip = (lax.axis_index("dp") == 1) if paired_dp else None
    copy = lax.axis_index("expert")
    gate_slab, up_slab, down_slab = w_gate[0], w_up[0], w_down[0]
    order_a = list(bits)
    order_b = [bits[0], bits[2], bits[1]] + list(bits[3:])

    meta = jnp.concatenate([routing.astype(BF)] + split_exact(gate_probs), axis=1)
    head = gather_sources(
        jnp.concatenate([tokens[:, :half], meta], axis=1), order_a, bits, flip
    )
    tail = gather_sources(tokens[:, half:], order_b, bits, flip)
    cot_head = gather_sources(cotangent[:, :half], order_a, bits, flip)
    cot_tail = gather_sources(cotangent[:, half:], order_b, bits, flip)

    named = head[:, :, half : half + top_count].astype(F32)
    parts = [
        head[:, :, half + (1 + i) * top_count : half + (2 + i) * top_count].astype(F32)
        for i in range(3)
    ]
    probs = parts[0] + parts[1] + parts[2]
    before = (
        jnp.arange(token_count)[:, None] < jnp.arange(token_count)[None, :]
    ).astype(BF)

    def selection(index):
        hit = named == index.astype(F32)
        member = jnp.any(hit, axis=2)
        slot = product(member.astype(BF), before).astype(jnp.int32)
        slot = jnp.where(member, slot, -1)
        select = jnp.arange(capacity, dtype=jnp.int32)[None, :, None] == slot[:, None, :]
        return select, jnp.sum(jnp.where(hit, probs, 0.0), axis=2)

    select, prob = selection(copy)
    select_pair, _ = selection(copy ^ top)
    row_prob = jnp.sum(jnp.where(select, prob[:, None, :], 0.0), axis=2).reshape(all_rows, 1)
    pick = select.astype(BF)
    keep = paired.astype(F32)[0]
    pick_both = jnp.concatenate(
        [pick, (select_pair.astype(F32) * keep).astype(BF)], axis=1
    )

    def rows_of(blocks):
        return batched(pick, blocks, ((2,), (1,))).astype(BF).reshape(all_rows, -1)

    def to_tokens(chooser, rows):
        rows = rows.reshape(n_expert, -1, rows.shape[-1])
        spread = batched(chooser, rows, ((1,), (1,))).astype(BF)
        return spread.reshape(n_expert * token_count, -1)

    def sum_dp(rows):
        if paired_dp:
            other = exchange(rows[own_rows:], "dp", 1)
            return rows[:own_rows].astype(F32) + other.astype(F32)
        return lax.psum_scatter(rows, "dp", scatter_dimension=0, tiled=True).astype(F32)

    def gather_dp(rows):
        if paired_dp:
            return jnp.concatenate([rows, exchange(rows, "dp", 1)], axis=0)
        return lax.all_gather(rows, "dp", axis=0, tiled=True)

    def gather_pair(rows):
        crossed = exchange(rows, "expert", top)
        if paired_dp:
            return jnp.concatenate([exchange(crossed, "dp", 1), crossed], axis=0)
        everything = lax.all_gather(crossed, "dp", axis=0, tiled=True)
        middle = all_rows // 2
        return jnp.concatenate([everything[middle:], everything[:middle]], axis=0)

    if paired_dp:
        prob_own = row_prob[:own_rows]
    else:
        prob_own = lax.dynamic_slice_in_dim(row_prob, lax.axis_index("dp") * own_rows, own_rows)

    token_all = jnp.concatenate([head[:, :, :half], tail], axis=2)
    cot_all = jnp.concatenate([cot_head, cot_tail], axis=2)
    token_rows = rows_of(token_all)
    gate_up = jnp.concatenate(
        [product(token_rows, gate_slab).astype(BF), product(token_rows, up_slab).astype(BF)],
        axis=1,
    )
    summed = sum_dp(gate_up)
    gate_own, up_own = summed[:, :hidden], summed[:, hidden:]
    cot_rows = rows_of(cot_all)
    grad_hidden = sum_dp(contract(cot_rows, down_slab, ((1,), (1,))).astype(BF)) * prob_own

    sigma = jax.nn.sigmoid(gate_own)
    activated = gate_own * sigma
    hid = (activated * up_own * prob_own).astype(BF)
    grad_rows = jnp.concatenate(
        [
            (grad_hidden * up_own * sigma * (1.0 + gate_own * (1.0 - sigma))).astype(BF),
            (grad_hidden * activated).astype(BF),
        ],
        axis=1,
    )
    hid_all = gather_dp(hid)
    hid_pair = gather_pair(hid)
    grad_all = gather_dp(grad_rows)
    grad_pair = gather_pair(grad_rows)

    out_part = product(to_tokens(pick, hid_all), down_slab).astype(BF)
    output = scatter_halves(out_part, n_expert, bits, flip)
    grad_spread = to_tokens(pick, grad_all)
    back_part = (
        contract(grad_spread[:, :hidden], gate_slab, ((1,), (1,)))
        + contract(grad_spread[:, hidden:], up_slab, ((1,), (1,)))
    ).astype(BF)
    grad_tokens = scatter_halves(back_part, n_expert, bits, flip)

    def both(own, pair):
        return jnp.concatenate(
            [
                own.reshape(n_expert, capacity, -1),
                pair.reshape(n_expert, capacity, -1),
            ],
            axis=1,
        )

    hid_both = to_tokens(pick_both, both(hid_all, hid_pair))
    grad_both = to_tokens(pick_both, both(grad_all, grad_pair))
    token_flat = token_all.reshape(n_expert * token_count, slab)
    cot_flat = cot_all.reshape(n_expert * token_count, slab)
    grad_gate = contract(token_flat, grad_both[:, :hidden], ((0,), (0,)))
    grad_up = contract(token_flat, grad_both[:, hidden:], ((0,), (0,)))
    grad_down = contract(hid_both, cot_flat, ((0,), (0,)))
    return (output, grad_tokens, grad_gate[None], grad_up[None], grad_down[None])


def scatter_halves(part, n_expert, bits, flip):
    half = part.shape[1] // 2
    blocks = part.reshape(n_expert, -1, part.shape[1])
    up = list(reversed(bits))
    first = scatter_sources(blocks[:, :, :half], up, bits, flip)
    other_order = [up[0], up[2], up[1]] + up[3:]
    second = scatter_sources(blocks[:, :, half:], other_order, bits, flip)
    return jnp.concatenate([first, second], axis=1)


def solution(mesh):
    return jax.shard_map(
        per_device,
        mesh=mesh,
        in_specs=(
            P("expert", "dp"),
            P("expert", None),
            P("expert", None),
            P("expert"),
            P("expert", "dp", None),
            P("expert", "dp", None),
            P("expert", None, "dp"),
            P("expert", "dp"),
        ),
        out_specs=(
            P("expert", "dp"),
            P("expert", "dp"),
            P("expert", "dp", None),
            P("expert", "dp", None),
            P("expert", None, "dp"),
        ),
        check_vma=False,
    )
```

time: 1020 us -> 607 us (0.60)
  waiting for transfers between devices: 757 us -> 309 us
  local copies, waits for them, and re-layouts: 8.04 us -> 56.1 us
  other arithmetic: 42.2 us -> 75.2 us
  blocking collectives: 27.2 us -> 0 us
  starting transfers between devices: 68.3 us -> 46.3 us
  matrix products: 98.2 us -> 112 us
  between operations: 15.1 us -> 2.5 us
    all_to_all x4 -> x0, waiting for transfers between devices: 172 us -> none  [the longest x1 85.1 us: per_device(): lax.all_to_all(send_tokens.reshape(n_expert, capacity, slab), 'expert', s...]
    ppermute x3 -> x40, waiting for transfers between devices: 476 us -> 309 us  [exchange(): return lax.ppermute(value, axis, pairs)]
    all_gather x3 -> x0, waiting for transfers between devices: 109 us -> none  [the longest x1 49.6 us: per_device(): piece = lax.all_gather(hid_own, 'dp', axis=0, tiled=True)]
    all_to_all x4 -> x0, starting transfers between devices: 61.6 us -> none  [the longest x1 24.3 us: per_device(): lax.all_to_all(back_slab.reshape(n_expert, capacity, slab), 'expert', spl...]
    concatenate x1 -> x25, other arithmetic: 2.18 us -> 47.1 us  [the longest x16 22.8 us: gather_sources(): current = jnp.concatenate([first, second], axis=place)]
    ppermute x3 -> x40, starting transfers between devices: 5.91 us -> 46.3 us  [exchange(): return lax.ppermute(value, axis, pairs)]
    all_to_all x1 -> x0, blocking collectives: 27.2 us -> none  [per_device(): lax.all_to_all(hidden_parts, 'dp', split_axis=0, concat_axis=0, tiled=True)]
    concatenate x0 -> x5, local copies, waits for them, and re-layouts: none -> 25.9 us  [the longest x2 10.5 us: gather_dp(): return jnp.concatenate([rows, exchange(rows, 'dp', 1)], axis=0)]
  transfers between devices with their start and end apart: 11 -> 40, of which waited for: 9 -> 23; matrix products, arithmetic and copies ran while one was open for 11% -> 38% of each run, Pallas kernels for 0% -> 0%
where the time goes in v1:
time: 607 us; the launch traced here: 601 us
  waiting for transfers between devices  309 us (51%)
  matrix products  112 us (18%)
  other arithmetic  75.2 us (12%)
  local copies, waits for them, and re-layouts  56.1 us (9%)
  starting transfers between devices  46.3 us (8%)
    ppermute x40, waiting for transfers between devices, exchange(): return lax.ppermute(value, axis, pairs)  309 us
    dot_general x6, matrix products, contract(): lax.dot_general(left, right, (dims, ((), ())), preferred_element_type=F32)  69.6 us
    ppermute x40, starting transfers between devices, exchange(): return lax.ppermute(value, axis, pairs)  46.3 us
    concatenate x16, other arithmetic, gather_sources(): current = jnp.concatenate([first, second], axis=place)  22.8 us
    dot_general x5, matrix products, batched(): lax.dot_general(left, right, (dims, ((0,), (0,))), preferred_element_type...  22.2 us
    dot_general x5, matrix products, product(): return jnp.dot(left, right, preferred_element_type=F32)  20 us
    convert_element_type x12, other arithmetic, scatter_sources(): current = (first.astype(F32) + other.astype(F32)).astype(BF)  14.2 us
    concatenate x2, other arithmetic, gather_dp(): return jnp.concatenate([rows, exchange(rows, 'dp', 1)], axis=0)  13.4 us
  transfers between devices with their start and end apart: 40, of which 23 were waited for; matrix products, arithmetic and copies ran while one was open for 38% of the time, Pallas kernels for 0%

profile of v1, /device:TPU:0, one launch (start us, length us, event | category | flops | bytes accessed | tf_op | source)
XLA Modules:
  0.0 601.0 jit_solution(14952022648132586204)
XLA Ops:
  2.6 4.0 collective-permute-start.4
  8.5 2.9 collective-permute-start.22
  16.0 20.7 %collective-permute-done.4 = bf16[1,1,1,1,128,1024]{5,4,3,2,1,0:T(8,128)(2,1)} collective-permute-done((bf16[1,1,1,1,128,1024]{5,4,3,2,1,0:T(8,128)(2,1)}, bf16[1,1,1,1,128,1024]{5,4,3,2,1,0:T(8,128)(2,1)}, u32[]{:S(2)}, u32[]{:S(2)}) %collective-permute-start.4) | collective-permute-done | bytes 262176 | tf_op jit(solution)/shard_map/ppermute | solution.py:12
  36.7 5.6 collective-permute-done.18
  42.3 5.6 collective-permute-done.22
  54.7 9.7 %collective-permute-done.5 = bf16[2,1,1,1,128,1024]{5,4,3,2,1,0:T(8,128)(2,1)S(1)} collective-permute-done((bf16[2,1,1,1,128,1024]{5,4,3,2,1,0:T(8,128)(2,1)S(1)}, bf16[2,1,1,1,128,1024]{5,4,3,2,1,0:T(8,128)(2,1)S(1)}, u32[]{:S(2)}, u32[]{:S(2)}) %collective-permute-start.5) | collective-permute-done | bytes 524320 | tf_op jit(solution)/shard_map/ppermute | solution.py:12
  64.6 8.5 %collective-permute-done.23 = bf16[2,1,1,1,128,1024]{5,4,3,2,1,0:T(8,128)(2,1)S(1)} collective-permute-done((bf16[2,1,1,1,128,1024]{5,4,3,2,1,0:T(8,128)(2,1)S(1)}, bf16[2,1,1,1,128,1024]{5,4,3,2,1,0:T(8,128)(2,1)S(1)}, u32[]{:S(2)}, u32[]{:S(2)}) %collective-permute-start.23) | collective-permute-done | bytes 524320 | tf_op jit(solution)/shard_map/ppermute | solution.py:12
  76.9 14.9 %collective-permute-done.6 = bf16[2,1,2,1,128,1024]{5,4,3,2,1,0:T(8,128)(2,1)S(1)} collective-permute-done((bf16[2,1,2,1,128,1024]{5,4,3,2,1,0:T(8,128)(2,1)S(1)}, bf16[2,1,2,1,128,1024]{5,4,3,2,1,0:T(8,128)(2,1)S(1)}, u32[]{:S(2)}, u32[]{:S(2)}) %collective-permute-start.6) | collective-permute-done | bytes 1048608 | tf_op jit(solution)/shard_map/ppermute | solution.py:12
  93.5 20.8 %collective-permute-done.24 = bf16[2,1,2,1,128,1024]{5,4,3,2,1,0:T(8,128)(2,1)S(1)} collective-permute-done((bf16[2,1,2,1,128,1024]{5,4,3,2,1,0:T(8,128)(2,1)S(1)}, bf16[2,1,2,1,128,1024]{5,4,3,2,1,0:T(8,128)(2,1)S(1)}, u32[]{:S(2)}, u32[]{:S(2)}) %collective-permute-start.24) | collective-permute-done | bytes 1048608 | tf_op jit(solution)/shard_map/ppermute | solution.py:12
  116.0 7.7 %collective-permute-done.19 = bf16[2,1,1,1,128,1024]{5,4,3,2,1,0:T(8,128)(2,1)S(1)} collective-permute-done((bf16[2,1,1,1,128,1024]{5,4,3,2,1,0:T(8,128)(2,1)S(1)}, bf16[2,1,1,1,128,1024]{5,4,3,2,1,0:T(8,128)(2,1)S(1)}, u32[]{:S(2)}, u32[]{:S(2)}) %collective-permute-start.19) | collective-permute-done | bytes 524320 | tf_op jit(solution)/shard_map/ppermute | solution.py:12
  128.0 20.6 %collective-permute-done.20 = bf16[2,2,1,1,128,1024]{5,4,3,2,1,0:T(8,128)(2,1)} collective-permute-done((bf16[2,2,1,1,128,1024]{5,4,3,2,1,0:T(8,128)(2,1)}, bf16[2,2,1,1,128,1024]{5,4,3,2,1,0:T(8,128)(2,1)}, u32[]{:S(2)}, u32[]{:S(2)}) %collective-permute-start.20) | collective-permute-done | bytes 1048608 | tf_op jit(solution)/shard_map/ppermute | solution.py:12
  148.7 3.0 pad_maximum_fusion.22
  151.8 3.6 pad_maximum_fusion.7
  155.4 3.6 pad_maximum_fusion.9
  159.1 3.5 pad_maximum_fusion.6
  162.6 6.4 %copy.30 = bf16[2,2,2,2,128,1056]{5,4,3,2,1,0:T(8,128)(2,1)} copy(bf16[2,2,2,2,128,1056]{4,5,3,2,1,0:T(8,128)(2,1)} %pad_maximum_fusion.6) | data formatting | bytes 8650752 | tf_op jit(solution)/shard_map/concatenate | solution.py:47
  168.9 2.8 slice.226
  174.5 3.5 fusion.16
  178.0 7.9 %convolution_convert_fusion.3 = bf16[1280,768]{0,1:T(8,128)(2,1)S(1)} fusion(bf16[1280,2048]{1,0:T(8,128)(2,1)} %bitcast.109, bf16[1,2048,768]{2,1,0:T(8,128)(2,1)} %param.13), kind=kOutput, calls=%fused_computation.41 | convolution fusion | flops 4027514880 | bytes 10354688 | tf_op jit(solution)/shard_map/dot_general | solution.py:16
  185.9 4.7 convolution_convert_fusion.4
  193.3 2.3 pad_maximum_fusion.8
  195.7 4.1 fusion.15
  199.8 6.7 %convolution_convert_fusion.2 = bf16[1280,768]{0,1:T(8,128)(2,1)S(1)} fusion(bf16[1280,2048]{1,0:T(8,128)(2,1)} %bitcast.111, bf16[1,768,2048]{2,1,0:T(8,128)(2,1)S(1)} %copy-done), kind=kOutput, calls=%fused_computation.40 | convolution fusion | flops 4027514880 | bytes 10354688 | tf_op jit(solution)/shard_map/dot_general | solution.py:20
  210.2 27.8 %collective-permute-done.8 = bf16[640,1536]{0,1:T(8,128)(2,1)} collective-permute-done((bf16[640,1536]{0,1:T(8,128)(2,1)}, bf16[640,1536]{0,1:T(8,128)(2,1)}, u32[]{:S(2)}, u32[]{:S(2)}) %collective-permute-start.8) | collective-permute-done | bytes 1966112 | tf_op jit(solution)/shard_map/ppermute | solution.py:12
  238.0 2.5 convert_add_fusion
  240.5 18.0 %collective-permute-done.26 = bf16[640,768]{0,1:T(8,128)(2,1)} collective-permute-done((bf16[640,768]{0,1:T(8,128)(2,1)}, bf16[640,768]{0,1:T(8,128)(2,1)}, u32[]{:S(2)}, u32[]{:S(2)}) %collective-permute-start.26) | collective-permute-done | bytes 983072 | tf_op jit(solution)/shard_map/ppermute | solution.py:12
  258.5 3.5 multiply_convert_fusion.1
  264.1 4.6 collective-permute-start.38
  271.5 15.4 %collective-permute-done.9 = bf16[640,768]{0,1:T(8,128)(2,1)S(1)} collective-permute-done((bf16[640,768]{0,1:T(8,128)(2,1)}, bf16[640,768]{0,1:T(8,128)(2,1)S(1)}, u32[]{:S(2)}, u32[]{:S(2)}) %collective-permute-start.9) | collective-permute-done | bytes 983072 | tf_op jit(solution)/shard_map/ppermute | solution.py:12
  286.9 2.6 pad_maximum_fusion.25
  289.6 4.0 copy.31
  293.6 2.6 convolution_convert_fusion.5
  296.2 58.2 %collective-permute-done.38 = bf16[640,768]{0,1:T(8,128)(2,1)} collective-permute-done((bf16[640,768]{0,1:T(8,128)(2,1)}, bf16[640,768]{0,1:T(8,128)(2,1)}, u32[]{:S(2)}, u32[]{:S(2)}) %collective-permute-start.38) | collective-permute-done | bytes 983072 | tf_op jit(solution)/shard_map/ppermute | solution.py:12
  355.0 7.2 %convolution_convert_fusion = bf16[2048,2048]{1,0:T(8,128)(2,1)S(1)} fusion(bf16[2048,768]{1,0:T(8,128)(2,1)S(1)} %bitcast.113, bf16[1,768,2048]{2,1,0:T(8,128)(2,1)S(1)} %copy-done), kind=kOutput, calls=%fused_computation.11 | convolution fusion | flops 6446645248 | bytes 14680064 | tf_op jit(solution)/shard_map/dot_general | solution.py:16
  365.1 2.1 slice.237
  368.5 7.8 %collective-permute-done.39 = bf16[640,768]{0,1:T(8,128)(2,1)S(1)} collective-permute-done((bf16[640,768]{0,1:T(8,128)(2,1)}, bf16[640,768]{0,1:T(8,128)(2,1)S(1)}, u32[]{:S(2)}, u32[]{:S(2)}) %collective-permute-start.39) | collective-permute-done | bytes 983072 | tf_op jit(solution)/shard_map/ppermute | solution.py:12
  377.7 2.7 copy.34
  380.5 15.2 %fusion.23 = f32[1,768,2048]{2,1,0:T(8,128)} fusion(bf16[16,128,1024]{2,1,0:T(8,128)(2,1)} %bitcast.89, bf16[16,128,1024]{2,1,0:T(8,128)(2,1)} %bitcast.92, bf16[16,80,768]{2,1,0:T(8,128)(2,1)} %bitcast.114, bf16[16,80,768]{2,1,0:T(8,128)(2,1)} %bitcast.106, bf16[16,80,128]{2,1,0:T(8,128)(2,1)S(1)} %copy-done.59, bf16[16,80,128]{2,1,0:T(8,128)(2,1)S(1)} %fusion.47), kind=kOutput, calls=%fused_computation.37 | convolution fusion | flops 6973292544 | bytes 19267584 | tf_op jit(solution)/shard_map/dot_general | solution.py:20
  395.6 10.7 %pad_maximum_fusion.12 = bf16[1280,1536]{0,1:T(8,128)(2,1)} fusion(bf16[640,1536]{0,1:T(8,128)(2,1)} %collective-permute-done.27, bf16[640,768]{0,1:T(8,128)(2,1)S(1)} %copy-done.20, bf16[640,768]{0,1:T(8,128)(2,1)S(1)} %copy-done.18), kind=kLoop, calls=%fused_computation.30 | loop fusion | flops 11796480 | bytes 7864320 | tf_op jit(solution)/shard_map/concatenate | solution.py:134
  406.4 6.5 %copy.32 = bf16[1280,1536]{1,0:T(8,128)(2,1)} copy(bf16[1280,1536]{0,1:T(8,128)(2,1)} %pad_maximum_fusion.12) | data formatting | bytes 7864320 | tf_op jit(solution)/shard_map/concatenate | solution.py:134
  412.9 4.1 convolution_convert_fusion.1
  417.0 9.6 %fusion.29 = f32[2048,2048]{1,0:T(8,128)} fusion(bf16[2048,1536]{1,0:T(8,128)(2,1)S(1)} %bitcast.107, bf16[1,2048,768]{2,1,0:T(8,128)(2,1)S(1)} %copy-done.62), kind=kOutput, calls=%fused_computation.46 | convolution fusion | flops 6442450944 | bytes 23068672 | tf_op jit(solution)/shard_map/dot_general | solution.py:20
  427.2 13.2 %add_convert_fusion = bf16[2048,2048]{1,0:T(8,128)(2,1)} fusion(f32[2048,2048]{1,0:T(8,128)} %fusion.29, bf16[2048,1536]{1,0:T(8,128)(2,1)S(1)} %bitcast.108, bf16[1,2048,768]{2,1,0:T(8,128)(2,1)} %param.13), kind=kOutput, calls=%fused_computation | convolution fusion | flops 6450839552 | bytes 31457280 | tf_op jit(solution)/shard_map/dot_general | solution.py:20
  440.4 4.0 fusion.65
  450.4 2.8 add_convert_fusion.4
  455.9 2.6 add_convert_fusion.3
  461.6 7.3 %collective-permute-done.37 = bf16[640,1536]{0,1:T(8,128)(2,1)} collective-permute-done((bf16[640,1536]{0,1:T(8,128)(2,1)}, bf16[640,1536]{0,1:T(8,128)(2,1)}, u32[]{:S(2)}, u32[]{:S(2)}) %collective-permute-start.37) | collective-permute-done | bytes 1966112 | tf_op jit(solution)/shard_map/ppermute | solution.py:12
  469.0 4.3 pad_maximum_fusion.13
  473.3 6.3 %copy.33 = bf16[1280,1536]{1,0:T(8,128)(2,1)} copy(bf16[1280,1536]{0,1:T(8,128)(2,1)} %pad_maximum_fusion.13) | data formatting | bytes 7864320 | tf_op jit(solution)/shard_map/concatenate | solution.py:140
  479.7 7.9 %fusion.12 = bf16[16,128,1536]{2,1,0:T(8,128)(2,1)} fusion(bf16[16,80,1536]{2,1,0:T(8,128)(2,1)} %bitcast.112, bf16[16,80,1536]{2,1,0:T(8,128)(2,1)} %bitcast.102, bf16[16,80,128]{2,1,0:T(8,128)(2,1)S(1)} %copy-done.60, bf16[16,80,128]{2,1,0:T(8,128)(2,1)S(1)} %fusion.47), kind=kOutput, calls=%fused_computation.16 | convolution fusion | flops 1026818048 | bytes 14811136 | tf_op jit(solution)/shard_map/dot_general | solution.py:24
  487.6 12.5 %fusion.25 = f32[1,2048,768]{2,1,0:T(8,128)} fusion(bf16[2048,1024]{1,0:T(8,128)(2,1)S(1)} %bitcast.85, bf16[2048,1024]{1,0:T(8,128)(2,1)S(1)} %bitcast.87, bf16[2048,1536]{1,0:T(8,128)(2,1)} %bitcast.116), kind=kOutput, calls=%fused_computation.39 | convolution fusion | flops 6459228160 | bytes 17825792 | tf_op jit(solution)/shard_map/dot_general | solution.py:20
  500.1 12.4 %fusion.24 = f32[1,2048,768]{2,1,0:T(8,128)} fusion(bf16[2048,1024]{1,0:T(8,128)(2,1)S(1)} %bitcast.86, bf16[2048,1024]{1,0:T(8,128)(2,1)S(1)} %bitcast.88, bf16[2048,1536]{1,0:T(8,128)(2,1)} %bitcast.117), kind=kOutput, calls=%fused_computation.38 | convolution fusion | flops 6459228160 | bytes 17825792 | tf_op jit(solution)/shard_map/dot_general | solution.py:20
  512.5 2.7 add_convert_fusion.2
  517.3 3.3 collective-permute-start.12
  522.8 2.6 add_convert_fusion.1
  526.2 10.0 %collective-permute-done.12 = bf16[2,1,1,1,128,1024]{5,4,3,2,1,0:T(8,128)(2,1)S(1)} collective-permute-done((bf16[2,1,1,1,128,1024]{5,4,3,2,1,0:T(8,128)(2,1)S(1)}, bf16[2,1,1,1,128,1024]{5,4,3,2,1,0:T(8,128)(2,1)S(1)}, u32[]{:S(2)}, u32[]{:S(2)}) %collective-permute-start.12) | collective-permute-done | bytes 524320 | tf_op jit(solution)/shard_map/ppermute | solution.py:12
  536.5 3.1 collective-permute-start.13
  539.6 8.5 %collective-permute-done.16 = bf16[2,1,1,1,128,1024]{5,4,3,2,1,0:T(8,128)(2,1)S(1)} collective-permute-done((bf16[2,1,1,1,128,1024]{5,4,3,2,1,0:T(8,128)(2,1)S(1)}, bf16[2,1,1,1,128,1024]{5,4,3,2,1,0:T(8,128)(2,1)S(1)}, u32[]{:S(2)}, u32[]{:S(2)}) %collective-permute-start.16) | collective-permute-done | bytes 524320 | tf_op jit(solution)/shard_map/ppermute | solution.py:12
  548.4 12.8 %collective-permute-done.13 = bf16[1,1,1,1,128,1024]{5,4,3,2,1,0:T(8,128)(2,1)S(1)} collective-permute-done((bf16[1,1,1,1,128,1024]{5,4,3,2,1,0:T(8,128)(2,1)S(1)}, bf16[1,1,1,1,128,1024]{5,4,3,2,1,0:T(8,128)(2,1)S(1)}, u32[]{:S(2)}, u32[]{:S(2)}) %collective-permute-start.13) | collective-permute-done | bytes 262176 | tf_op jit(solution)/shard_map/ppermute | solution.py:12
  561.7 4.0 collective-permute-start.30
  568.2 7.2 %collective-permute-done.30 = bf16[2,1,1,1,128,1024]{5,4,3,2,1,0:T(8,128)(2,1)S(1)} collective-permute-done((bf16[2,1,1,1,128,1024]{5,4,3,2,1,0:T(8,128)(2,1)S(1)}, bf16[2,1,1,1,128,1024]{5,4,3,2,1,0:T(8,128)(2,1)S(1)}, u32[]{:S(2)}, u32[]{:S(2)}) %collective-permute-start.30) | collective-permute-done | bytes 524320 | tf_op jit(solution)/shard_map/ppermute | solution.py:12
  575.6 3.7 collective-permute-start.31
  580.5 14.9 %collective-permute-done.31 = bf16[1,1,1,1,128,1024]{5,4,3,2,1,0:T(8,128)(2,1)S(1)} collective-permute-done((bf16[1,1,1,1,128,1024]{5,4,3,2,1,0:T(8,128)(2,1)S(1)}, bf16[1,1,1,1,128,1024]{5,4,3,2,1,0:T(8,128)(2,1)S(1)}, u32[]{:S(2)}, u32[]{:S(2)}) %collective-permute-start.31) | collective-permute-done | bytes 262176 | tf_op jit(solution)/shard_map/ppermute | solution.py:12
  595.6 4.3 collective-permute-done.35
  (242 shorter events, 69.7 us)
Async XLA Ops:
  0.6 199.2 %copy-start = (bf16[1,768,2048]{2,1,0:T(8,128)(2,1)S(1)}, bf16[1,768,2048]{2,1,0:T(8,128)(2,1)}, u32[]{:S(2)}) copy-start(bf16[1,768,2048]{2,1,0:T(8,128)(2,1)} %param.14) | copy-start | bytes 9437188
  2.6 34.1 %collective-permute-start.4 = (bf16[1,1,1,1,128,1024]{5,4,3,2,1,0:T(8,128)(2,1)}, bf16[1,1,1,1,128,1024]{5,4,3,2,1,0:T(8,128)(2,1)}, u32[]{:S(2)}, u32[]{:S(2)}) collective-permute-start(bf16[1,1,1,1,128,1024]{5,4,3,2,1,0:T(8,128)(2,1)} %get-tuple-element.27), channel_id=1, source_target_pairs={{0,8},{1,9},{2,10},{3,11},{4,12},{5,13},{6,14},{7,15},{8,0},{9,1},... | collective-permute-start | bytes 786440 | tf_op jit(solution)/shard_map/ppermute | solution.py:12
  8.5 33.9 %collective-permute-start.18 = (bf16[1,1,1,1,128,1024]{5,4,3,2,1,0:T(8,128)(2,1)}, bf16[1,1,1,1,128,1024]{5,4,3,2,1,0:T(8,128)(2,1)}, u32[]{:S(2)}, u32[]{:S(2)}) collective-permute-start(bf16[1,1,1,1,128,1024]{5,4,3,2,1,0:T(8,128)(2,1)} %get-tuple-element.24), channel_id=1, source_target_pairs={{0,8},{1,9},{2,10},{3,11},{4,12},{5,13},{6,14},{7,15},{8,0},{9,1},... | collective-permute-start | bytes 786440 | tf_op jit(solution)/shard_map/ppermute | solution.py:12
  8.5 39.5 %collective-permute-start.22 = (bf16[1,1,1,1,128,1024]{5,4,3,2,1,0:T(8,128)(2,1)}, bf16[1,1,1,1,128,1024]{5,4,3,2,1,0:T(8,128)(2,1)}, u32[]{:S(2)}, u32[]{:S(2)}) collective-permute-start(bf16[1,1,1,1,128,1024]{5,4,3,2,1,0:T(8,128)(2,1)} %get-tuple-element.25), channel_id=1, source_target_pairs={{0,8},{1,9},{2,10},{3,11},{4,12},{5,13},{6,14},{7,15},{8,0},{9,1},... | collective-permute-start | bytes 786440 | tf_op jit(solution)/shard_map/ppermute | solution.py:12
  16.0 35.7 %copy-start.58 = (bf16[128,1056]{0,1:T(8,128)(2,1)}, bf16[128,1056]{0,1:T(8,128)(2,1)S(1)}, u32[]{:S(2)}) copy-start(bf16[128,1056]{0,1:T(8,128)(2,1)S(1)} %constant_dynamic-update-slice_fusion) | copy-start | bytes 811012
  16.0 36.9 %collective-permute-start = (bf16[1,1,1,1,128,1056]{4,5,3,2,1,0:T(8,128)(2,1)S(1)}, bf16[1,1,1,1,128,1056]{4,5,3,2,1,0:T(8,128)(2,1)}, u32[]{:S(2)}, u32[]{:S(2)}) collective-permute-start(bf16[1,1,1,1,128,1056]{4,5,3,2,1,0:T(8,128)(2,1)S(1)} %bitcast.115), channel_id=1, source_target_pairs={{0,8},{1,9},{2,10},{3,11},{4,12},{5,13},{6,14},{7,15},{8,0},{9,1},... | collective-permute-start | bytes 811016 | tf_op jit(solution)/shard_map/ppermute | solution.py:12
  49.4 42.4 %copy-start.37 = (bf16[1,1,1,1,128,1024]{5,4,3,2,1,0:T(8,128)(2,1)}, bf16[1,1,1,1,128,1024]{5,4,3,2,1,0:T(8,128)(2,1)S(1)}, u32[]{:S(2)}) copy-start(bf16[1,1,1,1,128,1024]{5,4,3,2,1,0:T(8,128)(2,1)S(1)} %get-tuple-element.28) | copy-start | bytes 786436
  49.4 42.4 %copy-start.39 = (bf16[1,1,1,1,128,1024]{5,4,3,2,1,0:T(8,128)(2,1)}, bf16[1,1,1,1,128,1024]{5,4,3,2,1,0:T(8,128)(2,1)S(1)}, u32[]{:S(2)}) copy-start(bf16[1,1,1,1,128,1024]{5,4,3,2,1,0:T(8,128)(2,1)S(1)} %get-tuple-element.29) | copy-start | bytes 786436
  49.4 64.9 %copy-start.33 = (bf16[1,1,1,1,128,1024]{5,4,3,2,1,0:T(8,128)(2,1)}, bf16[1,1,1,1,128,1024]{5,4,3,2,1,0:T(8,128)(2,1)S(1)}, u32[]{:S(2)}) copy-start(bf16[1,1,1,1,128,1024]{5,4,3,2,1,0:T(8,128)(2,1)S(1)} %get-tuple-element.22) | copy-start | bytes 786436
  49.4 64.9 %copy-start.35 = (bf16[1,1,1,1,128,1024]{5,4,3,2,1,0:T(8,128)(2,1)}, bf16[1,1,1,1,128,1024]{5,4,3,2,1,0:T(8,128)(2,1)S(1)}, u32[]{:S(2)}) copy-start(bf16[1,1,1,1,128,1024]{5,4,3,2,1,0:T(8,128)(2,1)S(1)} %get-tuple-element.23) | copy-start | bytes 786436
  49.4 74.3 %copy-start.29 = (bf16[1,1,1,1,128,1024]{5,4,3,2,1,0:T(8,128)(2,1)}, bf16[1,1,1,1,128,1024]{5,4,3,2,1,0:T(8,128)(2,1)S(1)}, u32[]{:S(2)}) copy-start(bf16[1,1,1,1,128,1024]{5,4,3,2,1,0:T(8,128)(2,1)S(1)} %get-tuple-element.14) | copy-start | bytes 786436
  49.4 74.3 %copy-start.31 = (bf16[1,1,1,1,128,1024]{5,4,3,2,1,0:T(8,128)(2,1)}, bf16[1,1,1,1,128,1024]{5,4,3,2,1,0:T(8,128)(2,1)S(1)}, u32[]{:S(2)}) copy-start(bf16[1,1,1,1,128,1024]{5,4,3,2,1,0:T(8,128)(2,1)S(1)} %get-tuple-element.15) | copy-start | bytes 786436
  49.5 14.9 %collective-permute-start.5 = (bf16[2,1,1,1,128,1024]{5,4,3,2,1,0:T(8,128)(2,1)S(1)}, bf16[2,1,1,1,128,1024]{5,4,3,2,1,0:T(8,128)(2,1)S(1)}, u32[]{:S(2)}, u32[]{:S(2)}) collective-permute-start(bf16[2,1,1,1,128,1024]{5,4,3,2,1,0:T(8,128)(2,1)S(1)} %pad_maximum_fusion.34), channel_id=1, source_target_pairs={{0,2},{1,3},{2,0},{3,1},{4,6},{5,7},{6,4},{7,5},{8,10},{9,11},{10,... | collective-permute-start | bytes 1572872 | tf_op jit(solution)/shard_map/ppermute | solution.py:12
  51.5 21.6 %collective-permute-start.23 = (bf16[2,1,1,1,128,1024]{5,4,3,2,1,0:T(8,128)(2,1)S(1)}, bf16[2,1,1,1,128,1024]{5,4,3,2,1,0:T(8,128)(2,1)S(1)}, u32[]{:S(2)}, u32[]{:S(2)}) collective-permute-start(bf16[2,1,1,1,128,1024]{5,4,3,2,1,0:T(8,128)(2,1)S(1)} %pad_maximum_fusion.37), channel_id=1, source_target_pairs={{0,2},{1,3},{2,0},{3,1},{4,6},{5,7},{6,4},{7,5},{8,10},{9,11},{10,... | collective-permute-start | bytes 1572872 | tf_op jit(solution)/shard_map/ppermute | solution.py:12
  54.0 72.2 %copy-start.27 = (bf16[1,1,1,1,128,1056]{4,5,3,2,1,0:T(8,128)(2,1)}, bf16[1,1,1,1,128,1056]{4,5,3,2,1,0:T(8,128)(2,1)S(1)}, u32[]{:S(2)}) copy-start(bf16[1,1,1,1,128,1056]{4,5,3,2,1,0:T(8,128)(2,1)S(1)} %get-tuple-element.21) | copy-start | bytes 811012
  54.0 20.7 %collective-permute-start.1 = (bf16[2,1,1,1,128,1056]{4,5,3,2,1,0:T(8,128)(2,1)S(1)}, bf16[2,1,1,1,128,1056]{4,5,3,2,1,0:T(8,128)(2,1)S(1)}, u32[]{:S(2)}, u32[]{:S(2)}) collective-permute-start(bf16[2,1,1,1,128,1056]{4,5,3,2,1,0:T(8,128)(2,1)S(1)} %pad_maximum_fusion.33), channel_id=1, source_target_pairs={{0,4},{1,5},{2,6},{3,7},{4,0},{5,1},{6,2},{7,3},{8,12},{9,13},{10,... | collective-permute-start | bytes 1622024 | tf_op jit(solution)/shard_map/ppermute | solution.py:12
  64.4 29.0 %copy-start.46 = (bf16[2,1,1,1,128,1024]{5,4,3,2,1,0:T(8,128)(2,1)}, bf16[2,1,1,1,128,1024]{5,4,3,2,1,0:T(8,128)(2,1)S(1)}, u32[]{:S(2)}) copy-start(bf16[2,1,1,1,128,1024]{5,4,3,2,1,0:T(8,128)(2,1)S(1)} %collective-permute-done.5) | copy-start | bytes 1572868
  64.5 27.3 %collective-permute-start.6 = (bf16[2,1,2,1,128,1024]{5,4,3,2,1,0:T(8,128)(2,1)S(1)}, bf16[2,1,2,1,128,1024]{5,4,3,2,1,0:T(8,128)(2,1)S(1)}, u32[]{:S(2)}, u32[]{:S(2)}) collective-permute-start(bf16[2,1,2,1,128,1024]{5,4,3,2,1,0:T(8,128)(2,1)S(1)} %pad_maximum_fusion.29), channel_id=1, source_target_pairs={{0,4},{1,5},{2,6},{3,7},{4,0},{5,1},{6,2},{7,3},{8,12},{9,13},{10,... | collective-permute-start | bytes 3145736 | tf_op jit(solution)/shard_map/ppermute | solution.py:12
  73.1 41.2 %copy-start.44 = (bf16[2,1,1,1,128,1024]{5,4,3,2,1,0:T(8,128)(2,1)}, bf16[2,1,1,1,128,1024]{5,4,3,2,1,0:T(8,128)(2,1)S(1)}, u32[]{:S(2)}) copy-start(bf16[2,1,1,1,128,1024]{5,4,3,2,1,0:T(8,128)(2,1)S(1)} %collective-permute-done.23) | copy-start | bytes 1572868
  73.2 41.1 %collective-permute-start.24 = (bf16[2,1,2,1,128,1024]{5,4,3,2,1,0:T(8,128)(2,1)S(1)}, bf16[2,1,2,1,128,1024]{5,4,3,2,1,0:T(8,128)(2,1)S(1)}, u32[]{:S(2)}, u32[]{:S(2)}) collective-permute-start(bf16[2,1,2,1,128,1024]{5,4,3,2,1,0:T(8,128)(2,1)S(1)} %pad_maximum_fusion.31), channel_id=1, source_target_pairs={{0,4},{1,5},{2,6},{3,7},{4,0},{5,1},{6,2},{7,3},{8,12},{9,13},{10,... | collective-permute-start | bytes 3145736 | tf_op jit(solution)/shard_map/ppermute | solution.py:12
  74.7 51.5 %copy-start.42 = (bf16[2,1,1,1,128,1056]{4,5,3,2,1,0:T(8,128)(2,1)}, bf16[2,1,1,1,128,1056]{4,5,3,2,1,0:T(8,128)(2,1)S(1)}, u32[]{:S(2)}) copy-start(bf16[2,1,1,1,128,1056]{4,5,3,2,1,0:T(8,128)(2,1)S(1)} %collective-permute-done.1) | copy-start | bytes 1622020
  74.8 51.4 %collective-permute-start.2 = (bf16[2,2,1,1,128,1056]{4,5,3,2,1,0:T(8,128)(2,1)S(1)}, bf16[2,2,1,1,128,1056]{4,5,3,2,1,0:T(8,128)(2,1)S(1)}, u32[]{:S(2)}, u32[]{:S(2)}) collective-permute-start(bf16[2,2,1,1,128,1056]{4,5,3,2,1,0:T(8,128)(2,1)S(1)} %pad_maximum_fusion.28), channel_id=1, source_target_pairs={{0,2},{1,3},{2,0},{3,1},{4,6},{5,7},{6,4},{7,5},{8,10},{9,11},{10,... | collective-permute-start | bytes 3244040 | tf_op jit(solution)/shard_map/ppermute | solution.py:12
  76.5 47.3 %collective-permute-start.19 = (bf16[2,1,1,1,128,1024]{5,4,3,2,1,0:T(8,128)(2,1)S(1)}, bf16[2,1,1,1,128,1024]{5,4,3,2,1,0:T(8,128)(2,1)S(1)}, u32[]{:S(2)}, u32[]{:S(2)}) collective-permute-start(bf16[2,1,1,1,128,1024]{5,4,3,2,1,0:T(8,128)(2,1)S(1)} %pad_maximum_fusion.36), channel_id=1, source_target_pairs={{0,4},{1,5},{2,6},{3,7},{4,0},{5,1},{6,2},{7,3},{8,12},{9,13},{10,... | collective-permute-start | bytes 1572872 | tf_op jit(solution)/shard_map/ppermute | solution.py:12
  91.8 24.2 %copy-start.54 = (bf16[2,1,2,1,128,1024]{5,4,3,2,1,0:T(8,128)(2,1)}, bf16[2,1,2,1,128,1024]{5,4,3,2,1,0:T(8,128)(2,1)S(1)}, u32[]{:S(2)}) copy-start(bf16[2,1,2,1,128,1024]{5,4,3,2,1,0:T(8,128)(2,1)S(1)} %collective-permute-done.6) | copy-start | bytes 3145732
  93.5 58.3 %collective-permute-start.7 = (bf16[2,2,2,1,128,1024]{5,4,3,2,1,0:T(8,128)(2,1)}, bf16[2,2,2,1,128,1024]{5,4,3,2,1,0:T(8,128)(2,1)}, u32[]{:S(2)}, u32[]{:S(2)}) collective-permute-start(bf16[2,2,2,1,128,1024]{5,4,3,2,1,0:T(8,128)(2,1)} %pad_maximum_fusion.21), channel_id=1, source_target_pairs={{0,1},{1,0},{2,3},{3,2},{4,5},{5,4},{6,7},{7,6},{8,9},{9,8},{10,11... | collective-permute-start | bytes 6291464 | tf_op jit(solution)/shard_map/ppermute | solution.py:12
  114.3 13.6 %copy-start.52 = (bf16[2,1,2,1,128,1024]{5,4,3,2,1,0:T(8,128)(2,1)}, bf16[2,1,2,1,128,1024]{5,4,3,2,1,0:T(8,128)(2,1)S(1)}, u32[]{:S(2)}) copy-start(bf16[2,1,2,1,128,1024]{5,4,3,2,1,0:T(8,128)(2,1)S(1)} %collective-permute-done.24) | copy-start | bytes 3145732
  116.0 39.4 %collective-permute-start.25 = (bf16[2,2,2,1,128,1024]{5,4,3,2,1,0:T(8,128)(2,1)}, bf16[2,2,2,1,128,1024]{5,4,3,2,1,0:T(8,128)(2,1)}, u32[]{:S(2)}, u32[]{:S(2)}) collective-permute-start(bf16[2,2,2,1,128,1024]{5,4,3,2,1,0:T(8,128)(2,1)} %pad_maximum_fusion.23), channel_id=1, source_target_pairs={{0,1},{1,0},{2,3},{3,2},{4,5},{5,4},{6,7},{7,6},{8,9},{9,8},{10,11... | collective-permute-start | bytes 6291464 | tf_op jit(solution)/shard_map/ppermute | solution.py:12
  124.9 23.7 %collective-permute-start.20 = (bf16[2,2,1,1,128,1024]{5,4,3,2,1,0:T(8,128)(2,1)}, bf16[2,2,1,1,128,1024]{5,4,3,2,1,0:T(8,128)(2,1)}, u32[]{:S(2)}, u32[]{:S(2)}) collective-permute-start(bf16[2,2,1,1,128,1024]{5,4,3,2,1,0:T(8,128)(2,1)} %pad_maximum_fusion.30), channel_id=1, source_target_pairs={{0,2},{1,3},{2,0},{3,1},{4,6},{5,7},{6,4},{7,5},{8,10},{9,11},{10,... | collective-permute-start | bytes 3145736 | tf_op jit(solution)/shard_map/ppermute | solution.py:12
  127.9 31.1 %collective-permute-start.3 = (bf16[2,2,2,1,128,1056]{4,5,3,2,1,0:T(8,128)(2,1)}, bf16[2,2,2,1,128,1056]{4,5,3,2,1,0:T(8,128)(2,1)}, u32[]{:S(2)}, u32[]{:S(2)}) collective-permute-start(bf16[2,2,2,1,128,1056]{4,5,3,2,1,0:T(8,128)(2,1)} %pad_maximum_fusion.20), channel_id=1, source_target_pairs={{0,1},{1,0},{2,3},{3,2},{4,5},{5,4},{6,7},{7,6},{8,9},{9,8},{10,11... | collective-permute-start | bytes 6488072 | tf_op jit(solution)/shard_map/ppermute | solution.py:12
  128.0 23.8 %copy-start.38 = (bf16[1,1,1,1,128,1024]{5,4,3,2,1,0:T(8,128)(2,1)S(1)}, bf16[1,1,1,1,128,1024]{5,4,3,2,1,0:T(8,128)(2,1)}, u32[]{:S(2)}) copy-start(bf16[1,1,1,1,128,1024]{5,4,3,2,1,0:T(8,128)(2,1)} %copy-done.37) | copy-start | bytes 786436
  128.0 23.8 %copy-start.40 = (bf16[1,1,1,1,128,1024]{5,4,3,2,1,0:T(8,128)(2,1)S(1)}, bf16[1,1,1,1,128,1024]{5,4,3,2,1,0:T(8,128)(2,1)}, u32[]{:S(2)}) copy-start(bf16[1,1,1,1,128,1024]{5,4,3,2,1,0:T(8,128)(2,1)} %copy-done.39) | copy-start | bytes 786436
  128.0 23.8 %copy-start.47 = (bf16[2,1,1,1,128,1024]{5,4,3,2,1,0:T(8,128)(2,1)S(1)}, bf16[2,1,1,1,128,1024]{5,4,3,2,1,0:T(8,128)(2,1)}, u32[]{:S(2)}) copy-start(bf16[2,1,1,1,128,1024]{5,4,3,2,1,0:T(8,128)(2,1)} %copy-done.46) | copy-start | bytes 1572868
  128.0 23.8 %copy-start.55 = (bf16[2,1,2,1,128,1024]{5,4,3,2,1,0:T(8,128)(2,1)S(1)}, bf16[2,1,2,1,128,1024]{5,4,3,2,1,0:T(8,128)(2,1)}, u32[]{:S(2)}) copy-start(bf16[2,1,2,1,128,1024]{5,4,3,2,1,0:T(8,128)(2,1)} %copy-done.54) | copy-start | bytes 3145732
  151.7 41.6 %collective-permute-start.21 = (bf16[2,2,2,1,128,1024]{5,4,3,2,1,0:T(8,128)(2,1)}, bf16[2,2,2,1,128,1024]{5,4,3,2,1,0:T(8,128)(2,1)}, u32[]{:S(2)}, u32[]{:S(2)}) collective-permute-start(bf16[2,2,2,1,128,1024]{5,4,3,2,1,0:T(8,128)(2,1)} %pad_maximum_fusion.22), channel_id=1, source_target_pairs={{0,1},{1,0},{2,3},{3,2},{4,5},{5,4},{6,7},{7,6},{8,9},{9,8},{10,11... | collective-permute-start | bytes 6291464 | tf_op jit(solution)/shard_map/ppermute | solution.py:12
  192.1 46.0 %collective-permute-start.8 = (bf16[640,1536]{0,1:T(8,128)(2,1)}, bf16[640,1536]{0,1:T(8,128)(2,1)}, u32[]{:S(2)}, u32[]{:S(2)}) collective-permute-start(bf16[640,1536]{0,1:T(8,128)(2,1)} %pad_maximum_fusion.24), channel_id=1, source_target_pairs={{0,16},{16,0},{1,17},{17,1},{2,18},{18,2},{3,19},{19,3},{4,20},{20... | collective-permute-start | bytes 5898248 | tf_op jit(solution)/shard_map/ppermute | solution.py:12
  207.7 50.8 %collective-permute-start.26 = (bf16[640,768]{0,1:T(8,128)(2,1)}, bf16[640,768]{0,1:T(8,128)(2,1)}, u32[]{:S(2)}, u32[]{:S(2)}) collective-permute-start(bf16[640,768]{0,1:T(8,128)(2,1)} %slice.254), channel_id=1, source_target_pairs={{0,16},{16,0},{1,17},{17,1},{2,18},{18,2},{3,19},{19,3},{4,20},{20... | collective-permute-start | bytes 2949128 | tf_op jit(solution)/shard_map/ppermute | solution.py:12
  210.2 48.4 %copy-start.57 = (bf16[1280,768]{0,1:T(8,128)(2,1)S(1)}, bf16[1280,768]{0,1:T(8,128)(2,1)}, u32[]{:S(2)}) copy-start(bf16[1280,768]{0,1:T(8,128)(2,1)} %copy-done.56) | copy-start | bytes 5898244
  262.0 24.9 %collective-permute-start.9 = (bf16[640,768]{0,1:T(8,128)(2,1)}, bf16[640,768]{0,1:T(8,128)(2,1)S(1)}, u32[]{:S(2)}, u32[]{:S(2)}) collective-permute-start(bf16[640,768]{0,1:T(8,128)(2,1)} %get-tuple-element.13), channel_id=1, source_target_pairs={{0,16},{16,0},{1,17},{17,1},{2,18},{18,2},{3,19},{19,3},{4,20},{20... | collective-permute-start | bytes 2949128 | tf_op jit(solution)/shard_map/ppermute | solution.py:12
  264.1 90.3 %collective-permute-start.38 = (bf16[640,768]{0,1:T(8,128)(2,1)}, bf16[640,768]{0,1:T(8,128)(2,1)}, u32[]{:S(2)}, u32[]{:S(2)}) collective-permute-start(bf16[640,768]{0,1:T(8,128)(2,1)} %get-tuple-element.13), channel_id=1, source_target_pairs={{0,8},{1,9},{2,10},{3,11},{4,12},{5,13},{6,14},{7,15},{8,0},{9,1},... | collective-permute-start | bytes 2949128 | tf_op jit(solution)/shard_map/ppermute | solution.py:12
  270.9 155.7 %collective-permute-start.36 = (bf16[640,1536]{0,1:T(8,128)(2,1)}, bf16[640,1536]{0,1:T(8,128)(2,1)}, u32[]{:S(2)}, u32[]{:S(2)}) collective-permute-start(bf16[640,1536]{0,1:T(8,128)(2,1)} %pad_maximum_fusion.26), channel_id=1, source_target_pairs={{0,8},{1,9},{2,10},{3,11},{4,12},{5,13},{6,14},{7,15},{8,0},{9,1},... | collective-permute-start | bytes 5898248 | tf_op jit(solution)/shard_map/ppermute | solution.py:12
  271.0 124.7 %collective-permute-start.27 = (bf16[640,1536]{0,1:T(8,128)(2,1)}, bf16[640,1536]{0,1:T(8,128)(2,1)}, u32[]{:S(2)}, u32[]{:S(2)}) collective-permute-start(bf16[640,1536]{0,1:T(8,128)(2,1)} %pad_maximum_fusion.26), channel_id=1, source_target_pairs={{0,16},{16,0},{1,17},{17,1},{2,18},{18,2},{3,19},{19,3},{4,20},{20... | collective-permute-start | bytes 5898248 | tf_op jit(solution)/shard_map/ppermute | solution.py:12
  354.4 22.0 %collective-permute-start.39 = (bf16[640,768]{0,1:T(8,128)(2,1)}, bf16[640,768]{0,1:T(8,128)(2,1)S(1)}, u32[]{:S(2)}, u32[]{:S(2)}) collective-permute-start(bf16[640,768]{0,1:T(8,128)(2,1)} %collective-permute-done.38), channel_id=1, source_target_pairs={{0,16},{16,0},{1,17},{17,1},{2,18},{18,2},{3,19},{19,3},{4,20},{20... | collective-permute-start | bytes 2949128 | tf_op jit(solution)/shard_map/ppermute | solution.py:12
  368.0 12.4 %copy-start.59 = (bf16[16,80,128]{2,1,0:T(8,128)(2,1)S(1)}, bf16[16,80,128]{2,1,0:T(8,128)(2,1)}, u32[]{:S(2)}) copy-start(bf16[16,80,128]{2,1,0:T(8,128)(2,1)} %select_convert_fusion) | copy-start | bytes 983044
  368.0 82.4 %collective-permute-start.10 = (bf16[2,2,2,1,128,1024]{5,4,3,2,1,0:T(8,128)(2,1)}, bf16[2,2,2,1,128,1024]{5,4,3,2,1,0:T(8,128)(2,1)}, u32[]{:S(2)}, u32[]{:S(2)}) collective-permute-start(bf16[2,2,2,1,128,1024]{5,4,3,2,1,0:T(8,128)(2,1)} %slice.237), channel_id=1, source_target_pairs={{0,1},{1,0},{2,3},{3,2},{4,5},{5,4},{6,7},{7,6},{8,9},{9,8},{10,11... | collective-permute-start | bytes 6291464 | tf_op jit(solution)/shard_map/ppermute | solution.py:12
  368.0 87.9 %collective-permute-start.14 = (bf16[2,2,2,1,128,1024]{5,4,3,2,1,0:T(8,128)(2,1)}, bf16[2,2,2,1,128,1024]{5,4,3,2,1,0:T(8,128)(2,1)}, u32[]{:S(2)}, u32[]{:S(2)}) collective-permute-start(bf16[2,2,2,1,128,1024]{5,4,3,2,1,0:T(8,128)(2,1)} %slice.246), channel_id=1, source_target_pairs={{0,1},{1,0},{2,3},{3,2},{4,5},{5,4},{6,7},{7,6},{8,9},{9,8},{10,11... | collective-permute-start | bytes 6291464 | tf_op jit(solution)/shard_map/ppermute | solution.py:12
  380.4 15.2 %copy-start.18 = (bf16[640,768]{0,1:T(8,128)(2,1)S(1)}, bf16[640,768]{0,1:T(8,128)(2,1)}, u32[]{:S(2)}) copy-start(bf16[640,768]{0,1:T(8,128)(2,1)} %copy-done.17) | copy-start | bytes 2949124
  380.5 15.2 %copy-start.20 = (bf16[640,768]{0,1:T(8,128)(2,1)S(1)}, bf16[640,768]{0,1:T(8,128)(2,1)}, u32[]{:S(2)}) copy-start(bf16[640,768]{0,1:T(8,128)(2,1)} %copy-done.19) | copy-start | bytes 2949124
  426.6 42.3 %collective-permute-start.37 = (bf16[640,1536]{0,1:T(8,128)(2,1)}, bf16[640,1536]{0,1:T(8,128)(2,1)}, u32[]{:S(2)}, u32[]{:S(2)}) collective-permute-start(bf16[640,1536]{0,1:T(8,128)(2,1)} %collective-permute-done.36), channel_id=1, source_target_pairs={{0,16},{16,0},{1,17},{17,1},{2,18},{18,2},{3,19},{19,3},{4,20},{20... | collective-permute-start | bytes 5898248 | tf_op jit(solution)/shard_map/ppermute | solution.py:12
  449.9 62.6 %collective-permute-start.28 = (bf16[2,2,2,1,128,1024]{5,4,3,2,1,0:T(8,128)(2,1)}, bf16[2,2,2,1,128,1024]{5,4,3,2,1,0:T(8,128)(2,1)}, u32[]{:S(2)}, u32[]{:S(2)}) collective-permute-start(bf16[2,2,2,1,128,1024]{5,4,3,2,1,0:T(8,128)(2,1)} %slice.259), channel_id=1, source_target_pairs={{0,1},{1,0},{2,3},{3,2},{4,5},{5,4},{6,7},{7,6},{8,9},{9,8},{10,11... | collective-permute-start | bytes 6291464 | tf_op jit(solution)/shard_map/ppermute | solution.py:12
  449.9 72.9 %collective-permute-start.32 = (bf16[2,2,2,1,128,1024]{5,4,3,2,1,0:T(8,128)(2,1)}, bf16[2,2,2,1,128,1024]{5,4,3,2,1,0:T(8,128)(2,1)}, u32[]{:S(2)}, u32[]{:S(2)}) collective-permute-start(bf16[2,2,2,1,128,1024]{5,4,3,2,1,0:T(8,128)(2,1)} %slice.268), channel_id=1, source_target_pairs={{0,1},{1,0},{2,3},{3,2},{4,5},{5,4},{6,7},{7,6},{8,9},{9,8},{10,11... | collective-permute-start | bytes 6291464 | tf_op jit(solution)/shard_map/ppermute | solution.py:12
  454.4 62.4 %collective-permute-start.11 = (bf16[2,2,1,1,128,1024]{5,4,3,2,1,0:T(8,128)(2,1)}, bf16[2,2,1,1,128,1024]{5,4,3,2,1,0:T(8,128)(2,1)S(1)}, u32[]{:S(2)}, u32[]{:S(2)}) collective-permute-start(bf16[2,2,1,1,128,1024]{5,4,3,2,1,0:T(8,128)(2,1)} %slice.239), channel_id=1, source_target_pairs={{0,2},{1,3},{2,0},{3,1},{4,6},{5,7},{6,4},{7,5},{8,10},{9,11},{10,... | collective-permute-start | bytes 3145736 | tf_op jit(solution)/shard_map/ppermute | solution.py:12
  460.1 60.5 %collective-permute-start.15 = (bf16[2,1,2,1,128,1024]{5,4,3,2,1,0:T(8,128)(2,1)}, bf16[2,1,2,1,128,1024]{5,4,3,2,1,0:T(8,128)(2,1)}, u32[]{:S(2)}, u32[]{:S(2)}) collective-permute-start(bf16[2,1,2,1,128,1024]{5,4,3,2,1,0:T(8,128)(2,1)} %slice.248), channel_id=1, source_target_pairs={{0,4},{1,5},{2,6},{3,7},{4,0},{5,1},{6,2},{7,3},{8,12},{9,13},{10,... | collective-permute-start | bytes 3145736 | tf_op jit(solution)/shard_map/ppermute | solution.py:12
  500.1 12.4 %copy-start.16 = (bf16[16,128,1024]{2,1,0:T(8,128)(2,1)S(1)}, bf16[16,128,1024]{2,1,0:T(8,128)(2,1)}, u32[]{:S(2)}) copy-start(bf16[16,128,1024]{2,1,0:T(8,128)(2,1)} %copy-done.15) | copy-start | bytes 12582916
  515.3 46.0 %collective-permute-start.29 = (bf16[2,2,1,1,128,1024]{5,4,3,2,1,0:T(8,128)(2,1)S(1)}, bf16[2,2,1,1,128,1024]{5,4,3,2,1,0:T(8,128)(2,1)S(1)}, u32[]{:S(2)}, u32[]{:S(2)}) collective-permute-start(bf16[2,2,1,1,128,1024]{5,4,3,2,1,0:T(8,128)(2,1)S(1)} %slice.261), channel_id=1, source_target_pairs={{0,2},{1,3},{2,0},{3,1},{4,6},{5,7},{6,4},{7,5},{8,10},{9,11},{10,... | collective-permute-start | bytes 3145736 | tf_op jit(solution)/shard_map/ppermute | solution.py:12
  517.3 19.0 %collective-permute-start.12 = (bf16[2,1,1,1,128,1024]{5,4,3,2,1,0:T(8,128)(2,1)S(1)}, bf16[2,1,1,1,128,1024]{5,4,3,2,1,0:T(8,128)(2,1)S(1)}, u32[]{:S(2)}, u32[]{:S(2)}) collective-permute-start(bf16[2,1,1,1,128,1024]{5,4,3,2,1,0:T(8,128)(2,1)S(1)} %slice.241), channel_id=1, source_target_pairs={{0,4},{1,5},{2,6},{3,7},{4,0},{5,1},{6,2},{7,3},{8,12},{9,13},{10,... | collective-permute-start | bytes 1572872 | tf_op jit(solution)/shard_map/ppermute | solution.py:12
  522.3 25.8 %collective-permute-start.16 = (bf16[2,1,1,1,128,1024]{5,4,3,2,1,0:T(8,128)(2,1)S(1)}, bf16[2,1,1,1,128,1024]{5,4,3,2,1,0:T(8,128)(2,1)S(1)}, u32[]{:S(2)}, u32[]{:S(2)}) collective-permute-start(bf16[2,1,1,1,128,1024]{5,4,3,2,1,0:T(8,128)(2,1)S(1)} %slice.250), channel_id=1, source_target_pairs={{0,2},{1,3},{2,0},{3,1},{4,6},{5,7},{6,4},{7,5},{8,10},{9,11},{10,... | collective-permute-start | bytes 1572872 | tf_op jit(solution)/shard_map/ppermute | solution.py:12
  525.5 41.7 %collective-permute-start.33 = (bf16[2,1,2,1,128,1024]{5,4,3,2,1,0:T(8,128)(2,1)S(1)}, bf16[2,1,2,1,128,1024]{5,4,3,2,1,0:T(8,128)(2,1)S(1)}, u32[]{:S(2)}, u32[]{:S(2)}) collective-permute-start(bf16[2,1,2,1,128,1024]{5,4,3,2,1,0:T(8,128)(2,1)S(1)} %slice.270), channel_id=1, source_target_pairs={{0,4},{1,5},{2,6},{3,7},{4,0},{5,1},{6,2},{7,3},{8,12},{9,13},{10,... | collective-permute-start | bytes 3145736 | tf_op jit(solution)/shard_map/ppermute | solution.py:12
  536.5 24.6 %collective-permute-start.13 = (bf16[1,1,1,1,128,1024]{5,4,3,2,1,0:T(8,128)(2,1)S(1)}, bf16[1,1,1,1,128,1024]{5,4,3,2,1,0:T(8,128)(2,1)S(1)}, u32[]{:S(2)}, u32[]{:S(2)}) collective-permute-start(bf16[1,1,1,1,128,1024]{5,4,3,2,1,0:T(8,128)(2,1)S(1)} %broadcast_select_fusion.9), channel_id=1, source_target_pairs={{0,8},{1,9},{2,10},{3,11},{4,12},{5,13},{6,14},{7,15},{8,0},{9,1},... | collective-permute-start | bytes 786440 | tf_op jit(solution)/shard_map/ppermute | solution.py:12
  548.3 19.8 %collective-permute-start.17 = (bf16[1,1,1,1,128,1024]{5,4,3,2,1,0:T(8,128)(2,1)S(1)}, bf16[1,1,1,1,128,1024]{5,4,3,2,1,0:T(8,128)(2,1)S(1)}, u32[]{:S(2)}, u32[]{:S(2)}) collective-permute-start(bf16[1,1,1,1,128,1024]{5,4,3,2,1,0:T(8,128)(2,1)S(1)} %broadcast_select_fusion.8), channel_id=1, source_target_pairs={{0,8},{1,9},{2,10},{3,11},{4,12},{5,13},{6,14},{7,15},{8,0},{9,1},... | collective-permute-start | bytes 786440 | tf_op jit(solution)/shard_map/ppermute | solution.py:12
  561.7 13.7 %collective-permute-start.30 = (bf16[2,1,1,1,128,1024]{5,4,3,2,1,0:T(8,128)(2,1)S(1)}, bf16[2,1,1,1,128,1024]{5,4,3,2,1,0:T(8,128)(2,1)S(1)}, u32[]{:S(2)}, u32[]{:S(2)}) collective-permute-start(bf16[2,1,1,1,128,1024]{5,4,3,2,1,0:T(8,128)(2,1)S(1)} %slice.263), channel_id=1, source_target_pairs={{0,4},{1,5},{2,6},{3,7},{4,0},{5,1},{6,2},{7,3},{8,12},{9,13},{10,... | collective-permute-start | bytes 1572872 | tf_op jit(solution)/shard_map/ppermute | solution.py:12
  567.6 11.8 %collective-permute-start.34 = (bf16[2,1,1,1,128,1024]{5,4,3,2,1,0:T(8,128)(2,1)S(1)}, bf16[2,1,1,1,128,1024]{5,4,3,2,1,0:T(8,128)(2,1)S(1)}, u32[]{:S(2)}, u32[]{:S(2)}) collective-permute-start(bf16[2,1,1,1,128,1024]{5,4,3,2,1,0:T(8,128)(2,1)S(1)} %slice.272), channel_id=1, source_target_pairs={{0,2},{1,3},{2,0},{3,1},{4,6},{5,7},{6,4},{7,5},{8,10},{9,11},{10,... | collective-permute-start | bytes 1572872 | tf_op jit(solution)/shard_map/ppermute | solution.py:12
  575.4 25.4 %copy-start.1 = (bf16[1,768,2048]{2,1,0:T(8,128)(2,1)S(1)}, bf16[1,768,2048]{2,1,0:T(8,128)(2,1)}, u32[]{:S(2)}) copy-start(bf16[1,768,2048]{2,1,0:T(8,128)(2,1)} %param.14) | copy-start | bytes 9437188
  575.6 19.8 %collective-permute-start.31 = (bf16[1,1,1,1,128,1024]{5,4,3,2,1,0:T(8,128)(2,1)S(1)}, bf16[1,1,1,1,128,1024]{5,4,3,2,1,0:T(8,128)(2,1)S(1)}, u32[]{:S(2)}, u32[]{:S(2)}) collective-permute-start(bf16[1,1,1,1,128,1024]{5,4,3,2,1,0:T(8,128)(2,1)S(1)} %broadcast_select_fusion.3), channel_id=1, source_target_pairs={{0,8},{1,9},{2,10},{3,11},{4,12},{5,13},{6,14},{7,15},{8,0},{9,1},... | collective-permute-start | bytes 786440 | tf_op jit(solution)/shard_map/ppermute | solution.py:12
  579.6 20.2 %collective-permute-start.35 = (bf16[1,1,1,1,128,1024]{5,4,3,2,1,0:T(8,128)(2,1)S(1)}, bf16[1,1,1,1,128,1024]{5,4,3,2,1,0:T(8,128)(2,1)S(1)}, u32[]{:S(2)}, u32[]{:S(2)}) collective-permute-start(bf16[1,1,1,1,128,1024]{5,4,3,2,1,0:T(8,128)(2,1)S(1)} %broadcast_select_fusion.2), channel_id=1, source_target_pairs={{0,8},{1,9},{2,10},{3,11},{4,12},{5,13},{6,14},{7,15},{8,0},{9,1},... | collective-permute-start | bytes 786440 | tf_op jit(solution)/shard_map/ppermute | solution.py:12
  (39 other events, 187.6 us)

commit v2 on v1

--- a/solution.py
+++ b/solution.py
@@ -1,6 +1,10 @@
+import functools
+
 import jax
 import jax.numpy as jnp
 from jax import lax
+from jax.experimental import pallas as pl
+from jax.experimental.pallas import tpu as pltpu
 from jax.sharding import PartitionSpec as P
 
 BF = jnp.bfloat16
@@ -61,7 +65,7 @@
     return current.reshape(blocks.shape[1:])
 
 
-def per_device(tokens, routing, gate_probs, paired, w_gate, w_up, w_down, cotangent):
+def general(tokens, routing, gate_probs, paired, w_gate, w_up, w_down, cotangent):
     n_expert = lax.axis_size("expert")
     n_data = lax.axis_size("dp")
     token_count, top_count = routing.shape
@@ -210,6 +214,646 @@
     other_order = [up[0], up[2], up[1]] + up[3:]
     second = scatter_sources(blocks[:, :, half:], other_order, bits, flip)
     return jnp.concatenate([first, second], axis=1)
+
+
+VMEM_BYTES = 56 * 2**20
+LIGHT = 1000
+OUT_PARTS = (3, 3, 2)
+BACK_PARTS = (4, 4)
+CUTS = 1
+MIXED = True
+NN = ((1,), (0,))
+NT = ((1,), (1,))
+TN = ((0,), (0,))
+
+
+def call(kernel, grid, in_specs, out_specs, out_shape, scratch, flops, moved, deps=(), prefetch=1):
+    held = prefetch + len(in_specs)
+
+    def body(*refs):
+        kernel(*refs[:held], *refs[held + len(deps) :])
+
+    run = pl.pallas_call(
+        body,
+        grid_spec=pltpu.PrefetchScalarGridSpec(
+            num_scalar_prefetch=prefetch,
+            grid=grid,
+            in_specs=in_specs + [pl.BlockSpec(memory_space=pl.ANY)] * len(deps),
+            out_specs=out_specs,
+            scratch_shapes=scratch,
+        ),
+        out_shape=out_shape,
+        compiler_params=pltpu.CompilerParams(
+            dimension_semantics=("arbitrary",) * len(grid), vmem_limit_bytes=VMEM_BYTES
+        ),
+        cost_estimate=pl.CostEstimate(
+            flops=flops // LIGHT, bytes_accessed=moved // LIGHT, transcendentals=0
+        ),
+    )
+    return lambda *operands: run(*operands, *deps)
+
+
+def whole(value):
+    if isinstance(value, tuple):
+        stack, part = value
+        return pl.BlockSpec((None,) + stack.shape[1:], lambda j, s: (part, 0, 0)), stack
+    return fixed(value.shape), value
+
+
+def fixed(shape):
+    return pl.BlockSpec(shape, lambda j, s: (0,) * len(shape))
+
+
+def rows_kernel(count, cuts, dims, capacity, half_ref, slot_ref, *refs):
+    pieces = refs[:4]
+    weights = refs[4 : 4 + count]
+    outs, rows = refs[4 + count : -1], refs[-1]
+    width = pieces[0].shape[2]
+    tokens = pieces[0].shape[1]
+
+    @pl.when(pl.program_id(0) == 0)
+    def _():
+        place = lax.broadcasted_iota(jnp.int32, (capacity, tokens), 0)
+        for local in range(slot_ref.shape[0]):
+            pick = (place == slot_ref[local : local + 1, :]).astype(F32).astype(BF)
+            for side in range(2):
+                block = pieces[2 * side + local % 2][local // 2]
+                rows[local * capacity : (local + 1) * capacity, side * width : (side + 1) * width] = (
+                    contract(pick, block, NN).astype(BF)
+                )
+
+    for w in range(count):
+        value = contract(rows[...], weights[w][...], dims).astype(BF)
+        width = value.shape[1] // cuts
+        for cut in range(cuts):
+            outs[w * cuts + cut][...] = value[:, cut * width : (cut + 1) * width]
+
+
+def rows_product(half, slots, pieces, weights, dims, capacity, width, cuts=1, deps=()):
+    sources, tokens = slots.shape
+    mine = sources // 2
+    depth = mine // 2
+    slab = 2 * width
+    hidden = weights[0].shape[1] if dims == NN else weights[0].shape[0]
+    tile = min(256, hidden) if cuts == 1 else hidden
+    rows = mine * capacity
+    weight_spec = (
+        pl.BlockSpec((slab, tile), lambda j, s: (0, j))
+        if dims == NN
+        else pl.BlockSpec((tile, slab), lambda j, s: (j, 0))
+    )
+    count = len(weights)
+    return call(
+        functools.partial(rows_kernel, count, cuts, dims, capacity),
+        (hidden // tile,),
+        [pl.BlockSpec((mine, tokens), lambda j, s: (s[0], 0))]
+        + [pl.BlockSpec((depth, tokens, width), lambda j, s: (s[0], 0, 0))] * 4
+        + [weight_spec] * count,
+        [pl.BlockSpec((rows, tile // cuts), lambda j, s: (0, j))] * (count * cuts),
+        [jax.ShapeDtypeStruct((rows, hidden // cuts), BF)] * (count * cuts),
+        [pltpu.VMEM((rows, slab), BF)],
+        2 * count * rows * slab * hidden,
+        2 * slab * (count * hidden + mine * tokens),
+        deps,
+    )(half, slots, *pieces, *weights)
+
+
+def spread(dp, column_ref, sources, capacity, act):
+    tokens = column_ref.shape[1]
+    place = lax.broadcasted_iota(jnp.int32, (tokens, capacity), 1)
+    mine = sources // 2
+    for block in range(sources):
+        upper = jnp.bitwise_xor(dp, block // mine)
+        position = block % mine + mine * upper
+        pick = (place == column_ref[position]).astype(F32).astype(BF)
+        start = pl.multiple_of(((block % mine) // 2 + (mine // 2) * upper) * tokens, tokens)
+        act(block % 2, start, pick, block, position)
+
+
+def back_kernel(count, dims, capacity, dp_ref, column_ref, *refs):
+    values = refs[: 2 * count]
+    weights = refs[2 * count : 3 * count]
+    spreads = refs[-2 * count :]
+    keep_ref, sends = refs[3 * count], refs[3 * count + 1 : -2 * count]
+    sources, tokens, _ = column_ref.shape
+    mine = sources // 2
+
+    @pl.when(pl.program_id(0) == 0)
+    def _():
+        def act(parity, start, pick, block, position):
+            for v in range(count):
+                rows = values[2 * v + block // mine]
+                at = (block % mine) * capacity
+                spreads[2 * v + parity][pl.ds(start, tokens), :] = contract(
+                    pick, rows[at : at + capacity, :], NN
+                ).astype(BF)
+
+        spread(dp_ref[0], column_ref, sources, capacity, act)
+
+    def total(parity):
+        value = contract(spreads[parity][...], weights[0][...], dims)
+        for v in range(1, count):
+            value = value + contract(spreads[2 * v + parity][...], weights[v][...], dims)
+        return value.astype(BF)
+
+    keep_ref[...] = total(0)
+    sent = total(1)
+    tile = sent.shape[1]
+    spots = [(send, at) for send in sends for at in range(0, send.shape[1], tile)]
+    for step, (send, at) in enumerate(spots):
+
+        @pl.when(pl.program_id(0) == step)
+        def _():
+            send[:, at : at + tile] = sent
+
+
+def back_product(dp, columns, values, weights, dims, capacity, parts, deps=()):
+    sources, tokens, _ = columns.shape
+    specs, values = zip(*[whole(value) for value in values])
+    hidden = values[0].shape[-1]
+    slab = weights[0].shape[1] if dims == NN else weights[0].shape[0]
+    tile = 256
+    count = len(weights)
+    out_rows = sources * tokens // 2
+    weight_spec = (
+        pl.BlockSpec((hidden, tile), lambda j, s: (0, j))
+        if dims == NN
+        else pl.BlockSpec((tile, hidden), lambda j, s: (j, 0))
+    )
+    return call(
+        functools.partial(back_kernel, count, dims, capacity),
+        (slab // tile,),
+        [fixed(columns.shape)] + list(specs) + [weight_spec] * count,
+        [pl.BlockSpec((out_rows, tile), lambda j, s: (0, j))]
+        + [pl.BlockSpec((out_rows, tile * part), lambda j, s: (0, 0)) for part in parts],
+        [jax.ShapeDtypeStruct((out_rows, slab), BF)]
+        + [jax.ShapeDtypeStruct((out_rows, tile * part), BF) for part in parts],
+        [pltpu.VMEM((out_rows, hidden), BF)] * (2 * count),
+        4 * count * out_rows * slab * hidden,
+        2 * slab * (count * hidden + 2 * out_rows),
+        deps,
+    )(dp, columns, *values, *weights)
+
+
+def grad_kernel(flat, capacity, dp_ref, *refs):
+    columns, pair_columns = refs[:2]
+    own, other, crossed, beyond = refs[2:6]
+    pieces = refs[6:10]
+    out_ref = refs[10]
+    spreads = refs[11:]
+    sources, tokens, _ = columns.shape
+    mine = sources // 2
+    step = pl.program_id(0)
+
+    @pl.when(step == 0)
+    def _():
+        def act(parity, start, pick, block, position):
+            place = lax.broadcasted_iota(jnp.int32, (tokens, capacity), 1)
+            pair_pick = (place == pair_columns[position]).astype(F32).astype(BF)
+            at = (block % mine) * capacity
+            rows = (own if block < mine else other)[at : at + capacity, :]
+            pair_rows = (beyond if block < mine else crossed)[at : at + capacity, :]
+            value = contract(pick, rows, NN) + contract(pair_pick, pair_rows, NN)
+            if flat:
+                spreads[parity][pl.ds(start, tokens), :] = value.astype(BF)
+            else:
+                spreads[parity][:, pl.ds(start, tokens)] = value.T.astype(BF)
+
+        spread(dp_ref[0], columns, sources, capacity, act)
+
+    def product_of(blocks):
+        total = None
+        for parity in range(2):
+            block = blocks[parity][...].reshape(mine * tokens, blocks[parity].shape[2])
+            if flat:
+                term = contract(block, spreads[parity][...], TN)
+            else:
+                term = contract(spreads[parity][...], block, NN)
+            total = term if total is None else total + term
+        out_ref[...] = total
+
+    half_steps = pl.num_programs(0) // 2
+
+    @pl.when(step < half_steps)
+    def _():
+        product_of(pieces[:2])
+
+    @pl.when(step >= half_steps)
+    def _():
+        product_of(pieces[2:])
+
+
+def weight_gradient(dp, columns, pair_columns, values, pieces, flat, capacity, width, deps=()):
+    sources, tokens, _ = columns.shape
+    specs, values = zip(*[whole(value) for value in values])
+    hidden = values[0].shape[-1]
+    slab = 2 * width
+    tile = min(256, width)
+    steps = slab // tile
+    depth = sources // 2
+    first = pl.BlockSpec(
+        (depth, tokens, tile), lambda j, s: (0, 0, jnp.minimum(j, steps // 2 - 1))
+    )
+    second = pl.BlockSpec(
+        (depth, tokens, tile), lambda j, s: (0, 0, jnp.maximum(j - steps // 2, 0))
+    )
+    shape = (slab, hidden) if flat else (hidden, slab)
+    return call(
+        functools.partial(grad_kernel, flat, capacity),
+        (steps,),
+        [fixed(columns.shape)] * 2 + list(specs) + [first] * 2 + [second] * 2,
+        pl.BlockSpec((tile, hidden), lambda j, s: (j, 0))
+        if flat
+        else pl.BlockSpec((hidden, tile), lambda j, s: (0, j)),
+        jax.ShapeDtypeStruct(shape, F32),
+        [pltpu.VMEM((depth * tokens, hidden) if flat else (hidden, depth * tokens), BF)] * 2,
+        2 * sources * tokens * slab * hidden,
+        4 * slab * hidden + 2 * sources * tokens * slab,
+        deps,
+    )(dp, columns, pair_columns, *values, *pieces)
+
+
+def split_kernel(axes, *refs):
+    count = len(axes)
+    for i, axis in enumerate(axes):
+        total = (refs[2 * i][...].astype(F32) + refs[2 * i + 1][...].astype(F32)).astype(BF)
+        outs = refs[2 * count + 2 * i : 2 * count + 2 * i + 2]
+        for side, out in enumerate(outs):
+            out[...] = total[(slice(None),) * axis + (side,)]
+
+
+def sum_split(kept, coming, axes, sides, deps=()):
+    tokens = kept[0].shape[-2]
+    chunk = min(32, tokens)
+    in_specs, out_specs, out_shape, operands = [], [], [], []
+    for k, c, axis, side in zip(kept, coming, axes, sides):
+        lead = k.shape[:-2]
+        width = k.shape[-1] // (1 if side is None else 2)
+        at = 0 if side is None else side
+        spec = pl.BlockSpec(
+            lead + (chunk, width), functools.partial(lambda n, at, j: (0,) * n + (j, at), len(lead), at)
+        )
+        in_specs += [spec, spec]
+        operands += [k, c]
+        left = lead[:axis] + lead[axis + 1 :]
+        out_specs += [
+            pl.BlockSpec(
+                left + (chunk, width), functools.partial(lambda n, j: (0,) * n + (j, 0), len(left))
+            )
+        ] * 2
+        out_shape += [jax.ShapeDtypeStruct(left + (tokens, width), BF)] * 2
+    moved = sum(3 * 2 * value.size for value in kept)
+    return call(
+        functools.partial(split_kernel, tuple(axes)),
+        (tokens // chunk,),
+        in_specs,
+        out_specs,
+        out_shape,
+        [],
+        moved // 4,
+        moved,
+        deps,
+        prefetch=0,
+    )(*operands)
+
+
+def first_kernel(mixed, keep, *refs):
+    outs = refs[-4:] if mixed else refs[-2:]
+    pieces = refs[: -len(outs)]
+    each = outs[0].shape[-1]
+    at = 0
+    for piece in pieces:
+        width = min(piece.shape[-1], each)
+        for first in range(0, piece.shape[-1], width):
+            total = keep[..., at : at + width].astype(F32)
+            total = (total + piece[..., first : first + width].astype(F32)).astype(BF)
+            right, place = divmod(at, each)
+            for side in range(2):
+                outs[side + 2 * right][..., place : place + width] = (
+                    total[:, side] if right else total[:, :, side]
+                )
+            at += width
+
+
+def sum_first(keep, coming, mixed, deps=()):
+    lead, (tokens, width) = keep.shape[:-2], keep.shape[-2:]
+    chunk = min(16, tokens)
+    four = lambda j: (0, 0, j, 0)
+    five = lambda j: (0, 0, 0, j, 0)
+    outs = 4 if mixed else 2
+    each = 2 * width // outs
+    return call(
+        functools.partial(first_kernel, mixed),
+        (tokens // chunk,),
+        [pl.BlockSpec(lead + (chunk, value.shape[-1]), five) for value in [keep] + coming],
+        [pl.BlockSpec(lead[:2] + (chunk, each), four)] * outs,
+        [jax.ShapeDtypeStruct(lead[:2] + (tokens, each), BF)] * outs,
+        [],
+        0,
+        0,
+        deps,
+        prefetch=0,
+    )(keep, *coming)
+
+
+def last_kernel(*refs):
+    width = refs[0].shape[1]
+    for i in range(len(refs) // 2):
+        refs[-1][:, i * width : (i + 1) * width] = (
+            refs[2 * i][...].astype(F32) + refs[2 * i + 1][...].astype(F32)
+        ).astype(BF)
+
+
+def last_sum(kept, coming, deps=()):
+    tokens, width = kept[0].shape
+    spec = pl.BlockSpec((tokens, width), lambda j: (0, 0))
+    count = len(kept)
+    return call(
+        last_kernel,
+        (1,),
+        [spec] * (2 * count),
+        pl.BlockSpec((tokens, count * width), lambda j: (0, 0)),
+        jax.ShapeDtypeStruct((tokens, count * width), BF),
+        [],
+        0,
+        0,
+        deps,
+        prefetch=0,
+    )(*[value for pair in zip(kept, coming) for value in pair])
+
+
+def join_kernel(axes, cut, *refs):
+    count = len(axes)
+    held = 2 if cut else 2 * count
+    outs, stages = refs[held : held + count], refs[held + count : held + 2 * count]
+    in_sems, out_sems = refs[held + 2 * count :]
+    reads, writes = [], []
+    for i, axis in enumerate(axes):
+        width = outs[i].shape[-1]
+        for side in range(2):
+            n = 2 * i + side
+            at = (slice(None),) * axis + (slice(side, side + 1),)
+            source = refs[side].at[..., i * width : (i + 1) * width] if cut else refs[n]
+            reads.append(pltpu.make_async_copy(source, stages[i].at[at], in_sems.at[n]))
+            writes.append(
+                pltpu.make_async_copy(stages[i].at[at], outs[i].at[at], out_sems.at[n])
+            )
+    for copy in reads:
+        copy.start()
+    for read, write in zip(reads, writes):
+        read.wait()
+        write.start()
+    for copy in writes:
+        copy.wait()
+
+
+def join(now, coming, axes, deps=(), cut=False):
+    out_shape, operands = [], []
+    for value, other in zip(now, coming):
+        operands += [value, other]
+    for i, axis in enumerate(axes):
+        value = now[0 if cut else i]
+        shape = value.shape[:axis] + (2,) + value.shape[axis + 1 : -1]
+        width = value.shape[-1] // (2 if cut else 1)
+        out_shape.append(jax.ShapeDtypeStruct(shape + (width,), BF))
+    place = pl.BlockSpec(memory_space=pl.ANY)
+    return call(
+        functools.partial(join_kernel, tuple(axes), cut),
+        (),
+        [place] * len(operands),
+        [place] * len(out_shape),
+        out_shape,
+        [pltpu.VMEM(whole.shape, BF) for whole in out_shape]
+        + [pltpu.SemaphoreType.DMA((2 * len(axes),))] * 2,
+        0,
+        0,
+        deps,
+        prefetch=0,
+    )(*operands)
+
+
+def hidden_kernel(gate_kept, gate_coming, up_kept, up_coming, prob, out):
+    gate = gate_kept[...].astype(F32) + gate_coming[...].astype(F32)
+    up = up_kept[...].astype(F32) + up_coming[...].astype(F32)
+    out[...] = (gate * jax.nn.sigmoid(gate) * up * prob[...]).astype(BF)
+
+
+def slopes_kernel(
+    gate_kept, gate_coming, up_kept, up_coming, prob, grad_kept, *refs
+):
+    gate = gate_kept[...].astype(F32) + gate_coming[...].astype(F32)
+    up = up_kept[...].astype(F32) + up_coming[...].astype(F32)
+    out, gate_out, up_out = refs[-3:]
+    grad_coming = jnp.concatenate([ref[...] for ref in refs[:-3]], axis=1)
+    grad = (grad_kept[...].astype(F32) + grad_coming.astype(F32)) * prob[...]
+    sigma = jax.nn.sigmoid(gate)
+    out[0] = (grad * up * sigma * (1.0 + gate * (1.0 - sigma))).astype(BF)
+    out[1] = (grad * gate * sigma).astype(BF)
+    gate_out[...] = out[0]
+    up_out[...] = out[1]
+
+
+def by_rows(kernel, operands, stacks, outs, deps=()):
+    rows, hidden = operands[0].shape
+    chunk = rows // 5 if rows % 80 == 0 else rows
+    return call(
+        kernel,
+        (rows // chunk,),
+        [pl.BlockSpec((chunk, value.shape[1]), lambda j: (j, 0)) for value in operands],
+        [pl.BlockSpec((2, chunk, hidden), lambda j: (0, j, 0))] * stacks
+        + [pl.BlockSpec((chunk, hidden), lambda j: (j, 0))] * outs,
+        [jax.ShapeDtypeStruct((2, rows, hidden), BF)] * stacks
+        + [jax.ShapeDtypeStruct((rows, hidden), BF)] * outs,
+        [],
+        0,
+        0,
+        deps,
+        prefetch=0,
+    )(*operands)
+
+
+def nothing_kernel(*refs):
+    pass
+
+
+def after(value, *others):
+    return pl.pallas_call(
+        nothing_kernel,
+        in_specs=[pl.BlockSpec(memory_space=pl.ANY)] * (1 + len(others)),
+        out_specs=pl.BlockSpec(memory_space=pl.ANY),
+        out_shape=jax.ShapeDtypeStruct(value.shape, value.dtype),
+        input_output_aliases={0: 0},
+    )(value, *others)
+
+
+def fast(tokens, routing, gate_probs, paired, w_gate, w_up, w_down, cotangent):
+    n_expert = lax.axis_size("expert")
+    token_count, top_count = routing.shape
+    slab = tokens.shape[1]
+    hidden = w_gate.shape[2]
+    capacity = max(2, 5 * token_count * top_count // (4 * n_expert))
+    half = slab // 2
+    mine = n_expert // 2
+    copy = lax.axis_index("expert")
+    dp = lax.axis_index("dp").astype(jnp.int32)
+    dp_one = dp.reshape(1)
+    other_one = (1 - dp).reshape(1)
+    gate_slab, up_slab, down_slab = w_gate[0], w_up[0], w_down[0]
+
+    def cross(value, bit):
+        return exchange(value, "expert", bit)
+
+    meta = jnp.concatenate([routing.astype(BF)] + split_exact(gate_probs), axis=1)
+    meta = jnp.pad(meta, ((0, 0), (0, 128 - meta.shape[1])))
+
+    def blocks(value):
+        return [value[:, :half].reshape(1, 1, 1, token_count, half), value[:, half:].reshape(1, 1, 1, token_count, half)]
+
+    def widen(now, bits, coming=None, deps=()):
+        if coming is None:
+            coming = [cross(value, bit) for value, bit in zip(now, bits)]
+        axis = {8: 0, 4: 1, 2: 2}
+        return join(now, coming, [axis[bit] for bit in bits], deps)
+
+    token_now = blocks(tokens)
+    token_now[0] = jnp.concatenate([token_now[0], meta.reshape(1, 1, 1, token_count, -1)], axis=-1)
+    token_now = widen(token_now, (8, 8))
+    token_now = widen(token_now, (4, 2))
+    token_now = widen(token_now, (2, 4))
+    cot_whole = after(cotangent, *token_now).reshape(1, 1, 1, token_count, slab)
+
+    def finish(now):
+        pieces = []
+        for value in now:
+            value = value.reshape(mine, token_count, -1)
+            pieces += [value, cross(value, 1)]
+        return pieces
+
+    token_pieces = finish(token_now)
+
+    meta = jnp.stack([piece[:, :, half:] for piece in token_pieces[:2]], axis=1)
+    meta = meta.reshape(n_expert, token_count, -1).astype(F32)
+    named, high, middle, low = [
+        meta[:, :, i * top_count : (i + 1) * top_count] for i in range(4)
+    ]
+    probs = high + middle + low
+    before = (
+        jnp.arange(token_count)[:, None] < jnp.arange(token_count)[None, :]
+    ).astype(BF)
+
+    def selection(index):
+        hit = named == index.astype(F32)
+        member = jnp.any(hit, axis=2)
+        slot = product(member.astype(BF), before).astype(jnp.int32)
+        return hit, jnp.where(member, slot, -1)
+
+    hit, slots = selection(copy)
+    _, pair_slots = selection(jnp.bitwise_xor(copy, mine))
+    pair_slots = jnp.where(paired[0] == 1, pair_slots, -1)
+    columns, pair_columns = slots[:, :, None], pair_slots[:, :, None]
+    prob = jnp.sum(jnp.where(hit, probs, 0.0), axis=2)
+    select = jnp.arange(capacity, dtype=jnp.int32)[None, :, None] == slots[:, None, :]
+    row_prob = jnp.sum(jnp.where(select, prob[:, None, :], 0.0), axis=2)
+    prob_own = lax.dynamic_slice_in_dim(row_prob, dp * mine, mine).reshape(mine * capacity, 1)
+
+    def rows_of(which, pieces, weights, dims, cuts=1, deps=()):
+        return rows_product(which, slots, pieces, weights, dims, capacity, half, cuts, deps)
+
+    def over(value):
+        return exchange(value, "dp", 1)
+
+    leaving = rows_of(other_one, token_pieces, [gate_slab, up_slab], NN)
+    gate_coming, up_coming = over(leaving[0]), over(leaving[1])
+    cot_now = join([cot_whole], [cross(cot_whole, 8)], (0, 0), (leaving[1],), True)
+    gate_kept, up_kept = rows_of(
+        dp_one, token_pieces, [gate_slab, up_slab], NN, 1, (cot_now[0],)
+    )
+    cot_now = widen(cot_now, (4, 2), None, (up_kept, gate_coming))
+    cot_pieces = finish(widen(cot_now, (2, 4), None, (up_coming,)))
+    both = [gate_kept, gate_coming, up_kept, up_coming, prob_own]
+    (hid,) = by_rows(hidden_kernel, both, 0, 1, (cot_pieces[0],))
+    hid_crossed = cross(hid, mine)
+    hid_other = over(hid)
+
+    (leaving,) = rows_of(other_one, cot_pieces, [down_slab], NT, 1, (hid,))
+    dhid_coming = over(leaving)
+    (dhid_kept,) = rows_of(dp_one, cot_pieces, [down_slab], NT)
+    out_keep, *out_send = back_product(
+        dp_one, columns, [hid, hid_other], [down_slab], NN, capacity, OUT_PARTS, (dhid_kept,)
+    )
+    slopes, dgate_sent, dup_sent = by_rows(
+        slopes_kernel, both + [dhid_kept, dhid_coming], 1, 2, (out_send[0],)
+    )
+    out_send[0] = after(out_send[0], hid_crossed)
+    slopes_other = over(slopes)
+    dgate_crossed = cross(dgate_sent, mine)
+
+    shape = (2, 2, 2, token_count, slab)
+
+    def first_sum(keep, send, mixed, *deps):
+        coming = [cross(value, 1).reshape(shape[:-1] + value.shape[-1:]) for value in send]
+        return sum_first(keep.reshape(shape), coming, mixed, deps)
+
+    def next_sum(parts, bits, axis, *deps):
+        kept, sent = parts[::2], parts[1::2]
+        coming = [cross(value, bit) for value, bit in zip(sent, bits)]
+        return sum_split(kept, coming, [axis] * len(kept), [None] * len(kept), deps)
+
+    def end_sum(parts, *deps):
+        return last_sum(parts[::2], [cross(value, 8) for value in parts[1::2]], deps)
+
+    def gradient(values, pieces, flat, *deps):
+        return weight_gradient(
+            dp_one, columns, pair_columns, values, pieces, flat, capacity, half, deps
+        )
+
+    out_parts = first_sum(out_keep, out_send, False)
+    back_keep, *back_send = back_product(
+        dp_one,
+        columns,
+        [(slopes, 0), (slopes_other, 0), (slopes, 1), (slopes_other, 1)],
+        [gate_slab, up_slab],
+        NT,
+        capacity,
+        BACK_PARTS,
+        (out_parts[1],),
+    )
+    dup_crossed = cross(after(dup_sent, dgate_crossed), mine)
+    hid_crossed = after(hid_crossed, slopes_other, out_parts[1])
+    hid_beyond = over(hid_crossed)
+    out_parts = next_sum(out_parts, (2,), 1)
+    back_send[0] = after(back_send[0], hid_beyond, out_parts[1], dgate_crossed)
+    dgate_beyond = over(dgate_crossed)
+    back_parts = first_sum(back_keep, back_send, MIXED)
+    bits = ((2, 4), (4, 2)) if MIXED else ((2,), (4,))
+    out_parts = next_sum(out_parts, (4,), 0, back_parts[1])
+    grad_down = gradient(
+        [hid, hid_other, hid_crossed, hid_beyond], cot_pieces, False, out_parts[1]
+    )
+    dup_crossed = after(dup_crossed, grad_down)
+    dup_beyond = over(dup_crossed)
+    grad_gate = gradient(
+        [(slopes, 0), (slopes_other, 0), dgate_crossed, dgate_beyond],
+        token_pieces,
+        True,
+        dup_crossed,
+    )
+    output = end_sum(out_parts, grad_gate)
+    back_parts = next_sum(back_parts, bits[0], 1, grad_gate)
+    back_parts = next_sum(back_parts, bits[1], 0, output)
+    grad_up = gradient(
+        [(slopes, 1), (slopes_other, 1), dup_crossed, dup_beyond],
+        token_pieces,
+        True,
+        back_parts[1],
+    )
+    grad_tokens = end_sum(back_parts)
+    return (output, grad_tokens, grad_gate[None], grad_up[None], grad_down[None])
+
+
+def per_device(*arrays):
+    quick = lax.axis_size("dp") == 2 and lax.axis_size("expert") == 16
+    return (fast if quick else general)(*arrays)
 
 
 def solution(mesh):

time: 607 us -> 445 us (0.73)
  Pallas kernels: 0 us -> 182 us
  waiting for transfers between devices: 309 us -> 182 us
  matrix products: 112 us -> 0.89 us
  other arithmetic: 75.2 us -> 3.72 us
  local copies, waits for them, and re-layouts: 56.1 us -> 27.8 us
    pallas_call x0 -> x31, Pallas kernels: none -> 182 us  [the longest x25 182 us: call(): return lambda *operands: run(*operands, *deps)]
    ppermute x40, waiting for transfers between devices: 309 us -> 182 us  [exchange(): return lax.ppermute(value, axis, pairs)]
    dot_general x11 -> x0, matrix products: 91.8 us -> none  [the longest x6 69.6 us: contract(): lax.dot_general(left, right, (dims, ((), ())), preferred_element_type=F32)]
    concatenate x25 -> x2, other arithmetic: 47.1 us -> 0.03 us  [the longest x1 0.02 us: fast(): jnp.concatenate([token_now[0], meta.reshape(1, 1, 1, token_count, -1)], a...]
    concatenate x5 -> x1, local copies, waits for them, and re-layouts: 25.9 us -> 0.12 us  [fast(): jnp.concatenate([routing.astype(BF)] + split_exact(gate_probs), axis=1)]
    slice x18 -> x0, local copies, waits for them, and re-layouts: 20.5 us -> none  [the longest x12 9.33 us: scatter_sources(): second = lax.slice_in_dim(current, 1, 2, axis=place)]
    dot_general x5 -> x2, matrix products: 20 us -> 0.89 us  [product(): return jnp.dot(left, right, preferred_element_type=F32)]
    convert_element_type x15 -> x3, other arithmetic: 18.6 us -> 1.45 us  [the longest x1 0.69 us: split_exact(): return [high.astype(BF), middle.astype(BF), (rest - middle).astype(BF)]]
  transfers between devices with their start and end apart: 40 -> 40, of which waited for: 23 -> 22; matrix products, arithmetic and copies ran while one was open for 38% -> 2% of each run, Pallas kernels for 0% -> 38%
where the time goes in v2:
time: 445 us; the launch traced here: 443 us
  waiting for transfers between devices  182 us (41%)
  Pallas kernels  182 us (41%)
  starting transfers between devices  44.7 us (10%)
  local copies, waits for them, and re-layouts  27.8 us (6%)
    ppermute x40, waiting for transfers between devices, exchange(): return lax.ppermute(value, axis, pairs)  182 us
    pallas_call x25, Pallas kernels, call(): return lambda *operands: run(*operands, *deps)  182 us
    ppermute x40, starting transfers between devices, exchange(): return lax.ppermute(value, axis, pairs)  44.7 us
    unnamed x69, local copies, waits for them, and re-layouts  21.9 us
  transfers between devices with their start and end apart: 40, of which 22 were waited for; matrix products, arithmetic and copies ran while one was open for 2% of the time, Pallas kernels for 38%

profile of v2, /device:TPU:0, one launch (start us, length us, event | category | flops | bytes accessed | tf_op | source)
XLA Modules:
  0.0 442.8 jit_solution(5178073220710861241)
XLA Ops:
  0.6 1.9 copy.82.refs_0_
  5.2 4.1 collective-permute-start
  9.4 24.5 %collective-permute-done.1.refs_3_ = bf16[1,1,1,128,1024]{4,3,2,1,0:T(8,128)(2,1)S(1)} collective-permute-done((bf16[1,1,1,128,1024]{4,3,2,1,0:T(8,128)(2,1)S(1)}, bf16[1,1,1,128,1024]{4,3,2,1,0:T(8,128)(2,1)S(1)}, u32[]{:S(2)}, u32[]{:S(2)}) %collective-permute-start.1) | collective-permute-done | bytes 262176 | tf_op jit(solution)/shard_map/ppermute | solution.py:16
  35.3 2.0 shard_map.119
  38.1 1.5 collective-permute-start.3
  39.6 12.3 %collective-permute-done.3.refs_3_ = bf16[2,1,1,128,1024]{4,3,2,1,0:T(8,128)(2,1)S(1)} collective-permute-done((bf16[2,1,1,128,1024]{4,3,2,1,0:T(8,128)(2,1)}, bf16[2,1,1,128,1024]{4,3,2,1,0:T(8,128)(2,1)S(1)}, u32[]{:S(2)}, u32[]{:S(2)}) %collective-permute-start.3) | collective-permute-done | bytes 524320 | tf_op jit(solution)/shard_map/ppermute | solution.py:16
  53.5 2.5 shard_map.120
  56.0 1.6 collective-permute-start.4
  58.5 22.9 %collective-permute-done.5.refs_3_ = bf16[2,1,2,128,1024]{4,3,2,1,0:T(8,128)(2,1)S(1)} collective-permute-done((bf16[2,1,2,128,1024]{4,3,2,1,0:T(8,128)(2,1)}, bf16[2,1,2,128,1024]{4,3,2,1,0:T(8,128)(2,1)S(1)}, u32[]{:S(2)}, u32[]{:S(2)}) %collective-permute-start.5) | collective-permute-done | bytes 1048608 | tf_op jit(solution)/shard_map/ppermute | solution.py:16
  81.4 1.6 collective-permute-done.4.refs_1_
  84.0 3.4 shard_map.121
  88.0 3.4 collective-permute-start.8
  92.4 2.5 collective-permute-done.6.refs_3_.refs_8_
  95.1 1.2 copy-done.1
  96.3 1.2 fusion.5
  98.6 9.6 %shard_map.123 = (bf16[640,768]{1,0:T(8,128)(2,1)}, bf16[640,768]{1,0:T(8,128)(2,1)}) custom-call(s32[1]{0:T(128)} %bitcast.13.refs_0_, s32[16,128]{1,0:T(8,128)} %fusion.3.refs_1_, bf16[8,128,1152]{2,1,0:T(8,128)(2,1)} %bitcast.39, bf16[8,128,1152]{2,1,0:T(8,128)(2,1)} %copy-done.1, bf16[8,128,1024]{2,1,0:T(8,128)(2,1)} %bitcast.45, ...), custom_call_target="tpu_custom_call" | custom-call | flops 4026531 | bytes 10485 | tf_op jit(solution)/shard_map/pallas_call | solution.py:253
  108.2 1.5 collective-permute-start.9
  109.6 5.5 %collective-permute-done.8.refs_1_ = bf16[1,1,1,128,2048]{4,3,2,1,0:T(8,128)(2,1)} collective-permute-done((bf16[1,1,1,128,2048]{4,3,2,1,0:T(8,128)(2,1)}, bf16[1,1,1,128,2048]{4,3,2,1,0:T(8,128)(2,1)}, u32[]{:S(2)}, u32[]{:S(2)}) %collective-permute-start.8) | collective-permute-done | bytes 524320 | tf_op jit(solution)/shard_map/ppermute | solution.py:16
  115.1 2.0 shard_map.124
  117.7 1.5 collective-permute-start.12
  119.2 9.4 %shard_map.125 = (bf16[640,768]{1,0:T(8,128)(2,1)}, bf16[640,768]{1,0:T(8,128)(2,1)}) custom-call(s32[1]{0:T(128)} %bitcast.refs_0_, s32[16,128]{1,0:T(8,128)} %fusion.3.refs_1_, bf16[8,128,1152]{2,1,0:T(8,128)(2,1)} %bitcast.40, bf16[8,128,1152]{2,1,0:T(8,128)(2,1)} %copy-done.1, bf16[8,128,1024]{2,1,0:T(8,128)(2,1)} %bitcast.46, ...), custom_call_target="tpu_custom_call" | custom-call | flops 4026531 | bytes 10485 | tf_op jit(solution)/shard_map/pallas_call | solution.py:253
  128.6 2.2 collective-permute-done.11.refs_1_
  133.2 2.4 shard_map.126
  135.6 1.6 collective-permute-start.13
  137.2 1.2 collective-permute-start.14
  138.4 1.5 collective-permute-start.10
  139.9 20.9 %collective-permute-done.10.refs_4_.refs_3_ = bf16[640,768]{1,0:T(8,128)(2,1)S(1)} collective-permute-done((bf16[640,768]{1,0:T(8,128)(2,1)S(1)}, bf16[640,768]{1,0:T(8,128)(2,1)S(1)}, u32[]{:S(2)}, u32[]{:S(2)}) %collective-permute-start.10) | collective-permute-done | bytes 983072 | tf_op jit(solution)/shard_map/ppermute | solution.py:16
  163.1 3.3 shard_map.127
  168.3 4.9 %shard_map.128.refs_2_.refs_7_.refs_3_ = bf16[640,768]{1,0:T(8,128)(2,1)} custom-call(bf16[640,768]{1,0:T(8,128)(2,1)} %get-tuple-element.57.refs_0_, bf16[640,768]{1,0:T(8,128)(2,1)} %copy-done.4, bf16[640,768]{1,0:T(8,128)(2,1)} %get-tuple-element.59.refs_4_.refs_2_, bf16[640,768]{1,0:T(8,128)(2,1)} %copy-done.3, f32[640,1]{1,0:T(8,128)} %reshape.90.refs_4_, ...), custom_call_target="tpu_custom_call" | custom-call | tf_op jit(solution)/shard_map/pallas_call | solution.py:253
  173.2 1.5 collective-permute-start.15
  174.7 1.4 copy-done.2
  176.1 7.3 %shard_map.134 = bf16[640,768]{1,0:T(8,128)(2,1)} custom-call(s32[1]{0:T(128)} %bitcast.13.refs_0_, s32[16,128]{1,0:T(8,128)} %fusion.3.refs_1_, bf16[8,128,1024]{2,1,0:T(8,128)(2,1)} %bitcast.53, bf16[8,128,1024]{2,1,0:T(8,128)(2,1)} %copy-done.2, bf16[8,128,1024]{2,1,0:T(8,128)(2,1)} %bitcast.67, ...), custom_call_target="tpu_custom_call" | custom-call | flops 2013265 | bytes 7340 | tf_op jit(solution)/shard_map/pallas_call | solution.py:253
  184.0 3.4 collective-permute-start.18
  187.4 1.4 copy.65.refs_1_
  188.7 7.3 %shard_map.129.refs_5_ = bf16[640,768]{1,0:T(8,128)(2,1)} custom-call(s32[1]{0:T(128)} %bitcast.refs_0_, s32[16,128]{1,0:T(8,128)} %fusion.3.refs_1_, bf16[8,128,1024]{2,1,0:T(8,128)(2,1)} %bitcast.54, bf16[8,128,1024]{2,1,0:T(8,128)(2,1)} %copy-done.2, bf16[8,128,1024]{2,1,0:T(8,128)(2,1)} %bitcast.68, ...), custom_call_target="tpu_custom_call" | custom-call | flops 2013265 | bytes 7340 | tf_op jit(solution)/shard_map/pallas_call | solution.py:253
  196.1 2.1 collective-permute-done.15.refs_3_.refs_4_
  198.2 14.2 %shard_map.130 = (bf16[1024,2048]{1,0:T(8,128)(2,1)}, bf16[1024,768]{1,0:T(8,128)(2,1)}, bf16[1024,768]{1,0:T(8,128)(2,1)}, bf16[1024,512]{1,0:T(8,128)(2,1)}) custom-call(s32[1]{0:T(128)} %bitcast.refs_0_, s32[16,128,1]{2,1,0:T(8,128)} %copy.65.refs_1_, bf16[640,768]{1,0:T(8,128)(2,1)} %shard_map.128.refs_2_.refs_7_.refs_3_, ...), custom_call_target="tpu_custom_call" | custom-call | flops 6442450 | bytes 11534 | tf_op jit(solution)/shard_map/pallas_call | solution.py:253
  212.3 5.9 %collective-permute-done.24.refs_6_ = bf16[640,768]{1,0:T(8,128)(2,1)S(1)} collective-permute-done((bf16[640,768]{1,0:T(8,128)(2,1)}, bf16[640,768]{1,0:T(8,128)(2,1)S(1)}, u32[]{:S(2)}, u32[]{:S(2)}) %collective-permute-start.24) | collective-permute-done | bytes 983072 | tf_op jit(solution)/shard_map/ppermute | solution.py:16
  219.2 7.6 %shard_map.135 = (bf16[2,640,768]{2,1,0:T(8,128)(2,1)}, bf16[640,768]{1,0:T(8,128)(2,1)}, bf16[640,768]{1,0:T(8,128)(2,1)}) custom-call(bf16[640,768]{1,0:T(8,128)(2,1)} %get-tuple-element.57.refs_0_, bf16[640,768]{1,0:T(8,128)(2,1)} %copy-done.4, bf16[640,768]{1,0:T(8,128)(2,1)} %get-tuple-element.59.refs_4_.refs_2_, bf16[640,768]{1,0:T(8,128)(2,1)} %copy-done.3, ...), custom_call_target="tpu_custom_call" | custom-call | tf_op jit(solution)/shard_map/pallas_call | solution.py:253
  226.8 3.3 collective-permute-done.18.refs_1_.refs_0_
  231.6 1.4 collective-permute-start.25
  233.0 3.2 collective-permute-done.21
  237.7 7.7 %shard_map.132 = (bf16[2,2,128,2048]{3,2,1,0:T(8,128)(2,1)}, bf16[2,2,128,2048]{3,2,1,0:T(8,128)(2,1)}) custom-call(bf16[2,2,2,128,2048]{4,3,2,1,0:T(8,128)(2,1)} %bitcast.73, bf16[2,2,2,128,768]{4,3,2,1,0:T(8,128)(2,1)} %bitcast.75, bf16[2,2,2,128,768]{4,3,2,1,0:T(8,128)(2,1)} %bitcast.19.refs_2_, bf16[2,2,2,128,512]{4,3,2,1,0:T(8,128)(2,1)} %bitcast.76), custom_call_target="tpu_custom_call" | custom-call | tf_op jit(solution)/shard_map/pallas_call | solution.py:253
  246.2 30.4 %collective-permute-done.25.refs_3_.refs_5_.refs_1_.refs_4_ = bf16[2,640,768]{2,1,0:T(8,128)(2,1)S(1)} collective-permute-done((bf16[2,640,768]{2,1,0:T(8,128)(2,1)}, bf16[2,640,768]{2,1,0:T(8,128)(2,1)S(1)}, u32[]{:S(2)}, u32[]{:S(2)}) %collective-permute-start.25) | collective-permute-done | bytes 1966112 | tf_op jit(solution)/shard_map/ppermute | solution.py:16
  276.5 1.3 copy-done
  277.9 1.4 collective-permute-start.26
  279.3 22.3 %shard_map.136 = (bf16[1024,2048]{1,0:T(8,128)(2,1)}, bf16[1024,1024]{1,0:T(8,128)(2,1)}, bf16[1024,1024]{1,0:T(8,128)(2,1)}) custom-call(s32[1]{0:T(128)} %bitcast.refs_0_, s32[16,128,1]{2,1,0:T(8,128)} %copy.65.refs_1_, bf16[2,640,768]{2,1,0:T(8,128)(2,1)} %get-tuple-element.73.refs_2_.refs_4_.refs_3_, bf16[2,640,768]{2,1,0:T(8,128)(2,1)} %copy-done, ...), custom_call_target="tpu_custom_call" | custom-call | flops 12884901 | bytes 14680 | tf_op jit(solution)/shard_map/pallas_call | solution.py:253
  301.7 4.3 shard_map.133
  307.6 3.3 collective-permute-start.32
  311.6 7.7 %shard_map.139 = (bf16[2,2,128,1024]{3,2,1,0:T(8,128)(2,1)}, bf16[2,2,128,1024]{3,2,1,0:T(8,128)(2,1)}, bf16[2,2,128,1024]{3,2,1,0:T(8,128)(2,1)}, bf16[2,2,128,1024]{3,2,1,0:T(8,128)(2,1)}) custom-call(bf16[2,2,2,128,2048]{4,3,2,1,0:T(8,128)(2,1)} %bitcast.74, bf16[2,2,2,128,1024]{4,3,2,1,0:T(8,128)(2,1)} %bitcast.22.refs_1_, ...), custom_call_target="tpu_custom_call" | custom-call | tf_op jit(solution)/shard_map/pallas_call | solution.py:253
  322.2 1.4 copy.71.refs_2_
  323.6 31.2 %collective-permute-done.23.refs_1_ = bf16[2,128,2048]{2,1,0:T(8,128)(2,1)} collective-permute-done((bf16[2,128,2048]{2,1,0:T(8,128)(2,1)}, bf16[2,128,2048]{2,1,0:T(8,128)(2,1)}, u32[]{:S(2)}, u32[]{:S(2)}) %collective-permute-start.23) | collective-permute-done | bytes 1048608 | tf_op jit(solution)/shard_map/ppermute | solution.py:16
  354.8 3.6 shard_map.140
  358.4 16.4 %shard_map.142.refs_1_ = f32[768,2048]{1,0:T(8,128)} custom-call(s32[1]{0:T(128)} %bitcast.refs_0_, s32[16,128,1]{2,1,0:T(8,128)} %copy.65.refs_1_, s32[16,128,1]{2,1,0:T(8,128)} %copy.71.refs_2_, bf16[640,768]{1,0:T(8,128)(2,1)} %shard_map.128.refs_2_.refs_7_.refs_3_, bf16[640,768]{1,0:T(8,128)(2,1)} %collective-permute-done.15.refs_3_.refs_4_, ...), custom_call_target="tpu_custom_call" | custom-call | flops 6442450 | bytes 14680 | tf_op jit(solution)/shard_map/pallas_call | solution.py:253
  377.3 15.9 %shard_map.144.refs_2_.refs_4_ = f32[2048,768]{1,0:T(8,128)} custom-call(s32[1]{0:T(128)} %bitcast.refs_0_, s32[16,128,1]{2,1,0:T(8,128)} %copy.65.refs_1_, s32[16,128,1]{2,1,0:T(8,128)} %copy.71.refs_2_, bf16[2,640,768]{2,1,0:T(8,128)(2,1)} %get-tuple-element.73.refs_2_.refs_4_.refs_3_, bf16[2,640,768]{2,1,0:T(8,128)(2,1)} %copy-done, ...), custom_call_target="tpu_custom_call" | custom-call | flops 6442450 | bytes 14680 | tf_op jit(solution)/shard_map/pallas_call | solution.py:253
  394.2 4.3 shard_map.146
  398.6 2.5 collective-permute-start.35
  402.9 2.1 shard_map.145.refs_4_
  405.0 6.6 %collective-permute-done.35.refs_1_ = bf16[2,128,1024]{2,1,0:T(8,128)(2,1)S(1)} collective-permute-done((bf16[2,128,1024]{2,1,0:T(8,128)(2,1)}, bf16[2,128,1024]{2,1,0:T(8,128)(2,1)S(1)}, u32[]{:S(2)}, u32[]{:S(2)}) %collective-permute-start.35) | collective-permute-done | bytes 524320 | tf_op jit(solution)/shard_map/ppermute | solution.py:16
  413.3 3.7 shard_map.147
  417.3 2.6 collective-permute-start.38
  420.9 15.9 %shard_map.149 = f32[2048,768]{1,0:T(8,128)} custom-call(s32[1]{0:T(128)} %bitcast.refs_0_, s32[16,128,1]{2,1,0:T(8,128)} %copy.65.refs_1_, s32[16,128,1]{2,1,0:T(8,128)} %copy.71.refs_2_, bf16[2,640,768]{2,1,0:T(8,128)(2,1)} %get-tuple-element.73.refs_2_.refs_4_.refs_3_, bf16[2,640,768]{2,1,0:T(8,128)(2,1)} %copy-done, ...), custom_call_target="tpu_custom_call" | custom-call | flops 6442450 | bytes 14680 | tf_op jit(solution)/shard_map/pallas_call | solution.py:253
  436.8 3.2 collective-permute-done.38.refs_3_
  440.7 2.1 shard_map.148
  (137 shorter events, 37.3 us)
Async XLA Ops:
  5.1 28.7 %copy-start.15 = (bf16[1,1,1,128,1024]{4,3,2,1,0:T(8,128)(2,1)}, bf16[1,1,1,128,1024]{4,3,2,1,0:T(8,128)(2,1)S(1)}, u32[]{:S(2)}) copy-start(bf16[1,1,1,128,1024]{4,3,2,1,0:T(8,128)(2,1)S(1)} %get-tuple-element.95.refs_2_) | copy-start | bytes 786436
  5.2 28.7 %copy-start.9 = (bf16[1,1,1,128,1152]{4,3,2,1,0:T(8,128)(2,1)}, bf16[1,1,1,128,1152]{4,3,2,1,0:T(8,128)(2,1)S(1)}, u32[]{:S(2)}) copy-start(bf16[1,1,1,128,1152]{4,3,2,1,0:T(8,128)(2,1)S(1)} %pad_maximum_fusion.refs_0_) | copy-start | bytes 884740
  5.2 28.7 %collective-permute-start = (bf16[1,1,1,128,1152]{4,3,2,1,0:T(8,128)(2,1)S(1)}, bf16[1,1,1,128,1152]{4,3,2,1,0:T(8,128)(2,1)S(1)}, u32[]{:S(2)}, u32[]{:S(2)}) collective-permute-start(bf16[1,1,1,128,1152]{4,3,2,1,0:T(8,128)(2,1)S(1)} %pad_maximum_fusion.refs_0_), channel_id=1, source_target_pairs={{0,8},{1,9},{2,10},{3,11},{4,12},{5,13},{6,14},{7,15},{8,0},{9,1},... | collective-permute-start | bytes 884744 | tf_op jit(solution)/shard_map/ppermute | solution.py:16
  9.3 24.6 %collective-permute-start.1 = (bf16[1,1,1,128,1024]{4,3,2,1,0:T(8,128)(2,1)S(1)}, bf16[1,1,1,128,1024]{4,3,2,1,0:T(8,128)(2,1)S(1)}, u32[]{:S(2)}, u32[]{:S(2)}) collective-permute-start(bf16[1,1,1,128,1024]{4,3,2,1,0:T(8,128)(2,1)S(1)} %get-tuple-element.95.refs_2_), channel_id=1, source_target_pairs={{0,8},{1,9},{2,10},{3,11},{4,12},{5,13},{6,14},{7,15},{8,0},{9,1},... | collective-permute-start | bytes 786440 | tf_op jit(solution)/shard_map/ppermute | solution.py:16
  37.3 14.8 %collective-permute-start.2 = (bf16[2,1,1,128,1152]{4,3,2,1,0:T(8,128)(2,1)}, bf16[2,1,1,128,1152]{4,3,2,1,0:T(8,128)(2,1)S(1)}, u32[]{:S(2)}, u32[]{:S(2)}) collective-permute-start(bf16[2,1,1,128,1152]{4,3,2,1,0:T(8,128)(2,1)} %get-tuple-element.49.refs_0_), channel_id=1, source_target_pairs={{0,4},{1,5},{2,6},{3,7},{4,0},{5,1},{6,2},{7,3},{8,12},{9,13},{10,... | collective-permute-start | bytes 1769480 | tf_op jit(solution)/shard_map/ppermute | solution.py:16
  38.1 13.8 %collective-permute-start.3 = (bf16[2,1,1,128,1024]{4,3,2,1,0:T(8,128)(2,1)}, bf16[2,1,1,128,1024]{4,3,2,1,0:T(8,128)(2,1)S(1)}, u32[]{:S(2)}, u32[]{:S(2)}) collective-permute-start(bf16[2,1,1,128,1024]{4,3,2,1,0:T(8,128)(2,1)} %get-tuple-element.50.refs_2_), channel_id=1, source_target_pairs={{0,2},{1,3},{2,0},{3,1},{4,6},{5,7},{6,4},{7,5},{8,10},{9,11},{10,... | collective-permute-start | bytes 1572872 | tf_op jit(solution)/shard_map/ppermute | solution.py:16
  56.0 27.0 %collective-permute-start.4 = (bf16[2,2,1,128,1152]{4,3,2,1,0:T(8,128)(2,1)}, bf16[2,2,1,128,1152]{4,3,2,1,0:T(8,128)(2,1)S(1)}, u32[]{:S(2)}, u32[]{:S(2)}) collective-permute-start(bf16[2,2,1,128,1152]{4,3,2,1,0:T(8,128)(2,1)} %get-tuple-element.51.refs_0_), channel_id=1, source_target_pairs={{0,2},{1,3},{2,0},{3,1},{4,6},{5,7},{6,4},{7,5},{8,10},{9,11},{10,... | collective-permute-start | bytes 3538952 | tf_op jit(solution)/shard_map/ppermute | solution.py:16
  57.6 23.8 %collective-permute-start.5 = (bf16[2,1,2,128,1024]{4,3,2,1,0:T(8,128)(2,1)}, bf16[2,1,2,128,1024]{4,3,2,1,0:T(8,128)(2,1)S(1)}, u32[]{:S(2)}, u32[]{:S(2)}) collective-permute-start(bf16[2,1,2,128,1024]{4,3,2,1,0:T(8,128)(2,1)} %get-tuple-element.52.refs_2_), channel_id=1, source_target_pairs={{0,4},{1,5},{2,6},{3,7},{4,0},{5,1},{6,2},{7,3},{8,12},{9,13},{10,... | collective-permute-start | bytes 3145736 | tf_op jit(solution)/shard_map/ppermute | solution.py:16
  81.4 1.6 copy-start.14
  83.0 1.0 copy-start.10
  87.5 7.4 %collective-permute-start.6 = (bf16[8,128,1152]{2,1,0:T(8,128)(2,1)}, bf16[8,128,1152]{2,1,0:T(8,128)(2,1)S(1)}, u32[]{:S(2)}, u32[]{:S(2)}) collective-permute-start(bf16[8,128,1152]{2,1,0:T(8,128)(2,1)} %bitcast.37), channel_id=1, source_target_pairs={{0,1},{1,0},{2,3},{3,2},{4,5},{5,4},{6,7},{7,6},{8,9},{9,8},{10,11... | collective-permute-start | bytes 7077896 | tf_op jit(solution)/shard_map/ppermute | solution.py:16
  87.5 11.0 %collective-permute-start.7 = (bf16[8,128,1024]{2,1,0:T(8,128)(2,1)}, bf16[8,128,1024]{2,1,0:T(8,128)(2,1)}, u32[]{:S(2)}, u32[]{:S(2)}) collective-permute-start(bf16[8,128,1024]{2,1,0:T(8,128)(2,1)} %bitcast.44), channel_id=1, source_target_pairs={{0,1},{1,0},{2,3},{3,2},{4,5},{5,4},{6,7},{7,6},{8,9},{9,8},{10,11... | collective-permute-start | bytes 6291464 | tf_op jit(solution)/shard_map/ppermute | solution.py:16
  88.0 27.1 %collective-permute-start.8 = (bf16[1,1,1,128,2048]{4,3,2,1,0:T(8,128)(2,1)}, bf16[1,1,1,128,2048]{4,3,2,1,0:T(8,128)(2,1)}, u32[]{:S(2)}, u32[]{:S(2)}) collective-permute-start(bf16[1,1,1,128,2048]{4,3,2,1,0:T(8,128)(2,1)} %bitcast.71), channel_id=1, source_target_pairs={{0,8},{1,9},{2,10},{3,11},{4,12},{5,13},{6,14},{7,15},{8,0},{9,1},... | collective-permute-start | bytes 1572872 | tf_op jit(solution)/shard_map/ppermute | solution.py:16
  94.9 1.4 copy-start.1
  108.2 24.0 %collective-permute-start.9 = (bf16[640,768]{1,0:T(8,128)(2,1)}, bf16[640,768]{1,0:T(8,128)(2,1)S(1)}, u32[]{:S(2)}, u32[]{:S(2)}) collective-permute-start(bf16[640,768]{1,0:T(8,128)(2,1)} %get-tuple-element.58), channel_id=1, source_target_pairs={{0,16},{16,0},{1,17},{17,1},{2,18},{18,2},{3,19},{19,3},{4,20},{20... | collective-permute-start | bytes 2949128 | tf_op jit(solution)/shard_map/ppermute | solution.py:16
  117.1 13.7 %collective-permute-start.11 = (bf16[2,1,1,128,1024]{4,3,2,1,0:T(8,128)(2,1)}, bf16[2,1,1,128,1024]{4,3,2,1,0:T(8,128)(2,1)S(1)}, u32[]{:S(2)}, u32[]{:S(2)}) collective-permute-start(bf16[2,1,1,128,1024]{4,3,2,1,0:T(8,128)(2,1)} %get-tuple-element.56.refs_8_.refs_0_), channel_id=1, source_target_pairs={{0,4},{1,5},{2,6},{3,7},{4,0},{5,1},{6,2},{7,3},{8,12},{9,13},{10,... | collective-permute-start | bytes 1572872 | tf_op jit(solution)/shard_map/ppermute | solution.py:16
  117.7 13.5 %collective-permute-start.12 = (bf16[2,1,1,128,1024]{4,3,2,1,0:T(8,128)(2,1)}, bf16[2,1,1,128,1024]{4,3,2,1,0:T(8,128)(2,1)S(1)}, u32[]{:S(2)}, u32[]{:S(2)}) collective-permute-start(bf16[2,1,1,128,1024]{4,3,2,1,0:T(8,128)(2,1)} %get-tuple-element.60.refs_2_), channel_id=1, source_target_pairs={{0,2},{1,3},{2,0},{3,1},{4,6},{5,7},{6,4},{7,5},{8,10},{9,11},{10,... | collective-permute-start | bytes 1572872 | tf_op jit(solution)/shard_map/ppermute | solution.py:16
  128.6 9.8 %copy-start.18 = (bf16[640,768]{1,0:T(8,128)(2,1)S(1)}, bf16[640,768]{1,0:T(8,128)(2,1)}, u32[]{:S(2)}) copy-start(bf16[640,768]{1,0:T(8,128)(2,1)} %get-tuple-element.55.refs_2_) | copy-start | bytes 2949124
  130.8 1.4 copy-start.25
  131.2 1.0 copy-start.26
  132.2 1.0 copy-start.4
  135.6 25.2 %collective-permute-start.13 = (bf16[2,2,1,128,1024]{4,3,2,1,0:T(8,128)(2,1)}, bf16[2,2,1,128,1024]{4,3,2,1,0:T(8,128)(2,1)S(1)}, u32[]{:S(2)}, u32[]{:S(2)}) collective-permute-start(bf16[2,2,1,128,1024]{4,3,2,1,0:T(8,128)(2,1)} %get-tuple-element.61.refs_0_), channel_id=1, source_target_pairs={{0,2},{1,3},{2,0},{3,1},{4,6},{5,7},{6,4},{7,5},{8,10},{9,11},{10,... | collective-permute-start | bytes 3145736 | tf_op jit(solution)/shard_map/ppermute | solution.py:16
  137.2 29.8 %copy-start.29 = (s32[16,128]{1,0:T(8,128)S(1)}, s32[16,128]{1,0:T(8,128)}, u32[]{:S(2)}) copy-start(s32[16,128]{1,0:T(8,128)} %fusion.3.refs_1_) | copy-start | bytes 24580
  137.2 24.3 %collective-permute-start.14 = (bf16[2,1,2,128,1024]{4,3,2,1,0:T(8,128)(2,1)}, bf16[2,1,2,128,1024]{4,3,2,1,0:T(8,128)(2,1)S(1)}, u32[]{:S(2)}, u32[]{:S(2)}) collective-permute-start(bf16[2,1,2,128,1024]{4,3,2,1,0:T(8,128)(2,1)} %get-tuple-element.62.refs_2_), channel_id=1, source_target_pairs={{0,4},{1,5},{2,6},{3,7},{4,0},{5,1},{6,2},{7,3},{8,12},{9,13},{10,... | collective-permute-start | bytes 3145736 | tf_op jit(solution)/shard_map/ppermute | solution.py:16
  138.4 22.4 %collective-permute-start.10 = (bf16[640,768]{1,0:T(8,128)(2,1)S(1)}, bf16[640,768]{1,0:T(8,128)(2,1)S(1)}, u32[]{:S(2)}, u32[]{:S(2)}) collective-permute-start(bf16[640,768]{1,0:T(8,128)(2,1)S(1)} %copy-done.18), channel_id=1, source_target_pairs={{0,16},{16,0},{1,17},{17,1},{2,18},{18,2},{3,19},{19,3},{4,20},{20... | collective-permute-start | bytes 2949128 | tf_op jit(solution)/shard_map/ppermute | solution.py:16
  160.8 1.0 copy-start.3
  160.8 1.3 copy-start.12
  162.2 1.0 copy-start.13
  166.4 8.3 %collective-permute-start.16 = (bf16[8,128,1024]{2,1,0:T(8,128)(2,1)}, bf16[8,128,1024]{2,1,0:T(8,128)(2,1)S(1)}, u32[]{:S(2)}, u32[]{:S(2)}) collective-permute-start(bf16[8,128,1024]{2,1,0:T(8,128)(2,1)} %bitcast.51), channel_id=1, source_target_pairs={{0,1},{1,0},{2,3},{3,2},{4,5},{5,4},{6,7},{7,6},{8,9},{9,8},{10,11... | collective-permute-start | bytes 6291464 | tf_op jit(solution)/shard_map/ppermute | solution.py:16
  166.5 8.2 %collective-permute-start.17 = (bf16[8,128,1024]{2,1,0:T(8,128)(2,1)}, bf16[8,128,1024]{2,1,0:T(8,128)(2,1)}, u32[]{:S(2)}, u32[]{:S(2)}) collective-permute-start(bf16[8,128,1024]{2,1,0:T(8,128)(2,1)} %bitcast.66), channel_id=1, source_target_pairs={{0,1},{1,0},{2,3},{3,2},{4,5},{5,4},{6,7},{7,6},{8,9},{9,8},{10,11... | collective-permute-start | bytes 6291464 | tf_op jit(solution)/shard_map/ppermute | solution.py:16
  173.2 24.9 %collective-permute-start.15 = (bf16[640,768]{1,0:T(8,128)(2,1)}, bf16[640,768]{1,0:T(8,128)(2,1)}, u32[]{:S(2)}, u32[]{:S(2)}) collective-permute-start(bf16[640,768]{1,0:T(8,128)(2,1)} %shard_map.128.refs_2_.refs_7_.refs_3_), channel_id=1, source_target_pairs={{0,16},{16,0},{1,17},{17,1},{2,18},{18,2},{3,19},{19,3},{4,20},{20... | collective-permute-start | bytes 2949128 | tf_op jit(solution)/shard_map/ppermute | solution.py:16
  174.7 1.4 copy-start.2
  176.1 11.3 %copy-start.30 = (s32[16,128]{1,0:T(8,128)S(1)}, s32[16,128]{1,0:T(8,128)}, u32[]{:S(2)}) copy-start(s32[16,128]{1,0:T(8,128)} %fusion.3.refs_1_) | copy-start | bytes 24580
  183.4 34.8 %collective-permute-start.24 = (bf16[640,768]{1,0:T(8,128)(2,1)}, bf16[640,768]{1,0:T(8,128)(2,1)S(1)}, u32[]{:S(2)}, u32[]{:S(2)}) collective-permute-start(bf16[640,768]{1,0:T(8,128)(2,1)} %shard_map.134), channel_id=1, source_target_pairs={{0,16},{16,0},{1,17},{17,1},{2,18},{18,2},{3,19},{19,3},{4,20},{20... | collective-permute-start | bytes 2949128 | tf_op jit(solution)/shard_map/ppermute | solution.py:16
  184.0 46.1 %collective-permute-start.18 = (bf16[640,768]{1,0:T(8,128)(2,1)}, bf16[640,768]{1,0:T(8,128)(2,1)S(1)}, u32[]{:S(2)}, u32[]{:S(2)}) collective-permute-start(bf16[640,768]{1,0:T(8,128)(2,1)} %shard_map.128.refs_2_.refs_7_.refs_3_), channel_id=1, source_target_pairs={{0,8},{1,9},{2,10},{3,11},{4,12},{5,13},{6,14},{7,15},{8,0},{9,1},... | collective-permute-start | bytes 2949128 | tf_op jit(solution)/shard_map/ppermute | solution.py:16
  212.3 23.9 %collective-permute-start.20 = (bf16[1024,768]{1,0:T(8,128)(2,1)}, bf16[1024,768]{1,0:T(8,128)(2,1)}, u32[]{:S(2)}, u32[]{:S(2)}) collective-permute-start(bf16[1024,768]{1,0:T(8,128)(2,1)} %get-tuple-element.67), channel_id=1, source_target_pairs={{0,1},{1,0},{2,3},{3,2},{4,5},{5,4},{6,7},{7,6},{8,9},{9,8},{10,11... | collective-permute-start | bytes 4718600 | tf_op jit(solution)/shard_map/ppermute | solution.py:16
  218.2 1.0 copy-start.19
  230.1 1.0 copy-start.5
  231.1 5.1 %collective-permute-start.19 = (bf16[1024,768]{1,0:T(8,128)(2,1)}, bf16[1024,768]{1,0:T(8,128)(2,1)S(1)}, u32[]{:S(2)}, u32[]{:S(2)}) collective-permute-start(bf16[1024,768]{1,0:T(8,128)(2,1)} %shard_map.131), channel_id=1, source_target_pairs={{0,1},{1,0},{2,3},{3,2},{4,5},{5,4},{6,7},{7,6},{8,9},{9,8},{10,11... | collective-permute-start | bytes 4718600 | tf_op jit(solution)/shard_map/ppermute | solution.py:16
  231.1 5.1 %collective-permute-start.21 = (bf16[1024,512]{1,0:T(8,128)(2,1)}, bf16[1024,512]{1,0:T(8,128)(2,1)S(1)}, u32[]{:S(2)}, u32[]{:S(2)}) collective-permute-start(bf16[1024,512]{1,0:T(8,128)(2,1)} %get-tuple-element.68), channel_id=1, source_target_pairs={{0,1},{1,0},{2,3},{3,2},{4,5},{5,4},{6,7},{7,6},{8,9},{9,8},{10,11... | collective-permute-start | bytes 3145736 | tf_op jit(solution)/shard_map/ppermute | solution.py:16
  231.6 44.9 %collective-permute-start.25 = (bf16[2,640,768]{2,1,0:T(8,128)(2,1)}, bf16[2,640,768]{2,1,0:T(8,128)(2,1)S(1)}, u32[]{:S(2)}, u32[]{:S(2)}) collective-permute-start(bf16[2,640,768]{2,1,0:T(8,128)(2,1)} %get-tuple-element.73.refs_2_.refs_4_.refs_3_), channel_id=1, source_target_pairs={{0,16},{16,0},{1,17},{17,1},{2,18},{18,2},{3,19},{19,3},{4,20},{20... | collective-permute-start | bytes 5898248 | tf_op jit(solution)/shard_map/ppermute | solution.py:16
  236.2 1.0 copy-start.16
  236.2 1.5 copy-start.8
  245.4 56.2 %collective-permute-start.22 = (bf16[2,2,128,2048]{3,2,1,0:T(8,128)(2,1)}, bf16[2,2,128,2048]{3,2,1,0:T(8,128)(2,1)}, u32[]{:S(2)}, u32[]{:S(2)}) collective-permute-start(bf16[2,2,128,2048]{3,2,1,0:T(8,128)(2,1)} %get-tuple-element.70.refs_8_.refs_2_), channel_id=1, source_target_pairs={{0,2},{1,3},{2,0},{3,1},{4,6},{5,7},{6,4},{7,5},{8,10},{9,11},{10,... | collective-permute-start | bytes 6291464 | tf_op jit(solution)/shard_map/ppermute | solution.py:16
  246.1 59.9 %collective-permute-start.27 = (bf16[640,768]{1,0:T(8,128)(2,1)}, bf16[640,768]{1,0:T(8,128)(2,1)}, u32[]{:S(2)}, u32[]{:S(2)}) collective-permute-start(bf16[640,768]{1,0:T(8,128)(2,1)} %get-tuple-element.76), channel_id=1, source_target_pairs={{0,8},{1,9},{2,10},{3,11},{4,12},{5,13},{6,14},{7,15},{8,0},{9,1},... | collective-permute-start | bytes 2949128 | tf_op jit(solution)/shard_map/ppermute | solution.py:16
  276.5 1.3 copy-start
  277.9 28.2 %collective-permute-start.26 = (bf16[640,768]{1,0:T(8,128)(2,1)}, bf16[640,768]{1,0:T(8,128)(2,1)S(1)}, u32[]{:S(2)}, u32[]{:S(2)}) collective-permute-start(bf16[640,768]{1,0:T(8,128)(2,1)} %shard_map.137.refs_5_), channel_id=1, source_target_pairs={{0,16},{16,0},{1,17},{17,1},{2,18},{18,2},{3,19},{19,3},{4,20},{20... | collective-permute-start | bytes 2949128 | tf_op jit(solution)/shard_map/ppermute | solution.py:16
  301.7 9.2 %collective-permute-start.29 = (bf16[1024,1024]{1,0:T(8,128)(2,1)}, bf16[1024,1024]{1,0:T(8,128)(2,1)}, u32[]{:S(2)}, u32[]{:S(2)}) collective-permute-start(bf16[1024,1024]{1,0:T(8,128)(2,1)} %get-tuple-element.77), channel_id=1, source_target_pairs={{0,1},{1,0},{2,3},{3,2},{4,5},{5,4},{6,7},{7,6},{8,9},{9,8},{10,11... | collective-permute-start | bytes 6291464 | tf_op jit(solution)/shard_map/ppermute | solution.py:16
  307.0 4.6 %collective-permute-start.28 = (bf16[1024,1024]{1,0:T(8,128)(2,1)}, bf16[1024,1024]{1,0:T(8,128)(2,1)}, u32[]{:S(2)}, u32[]{:S(2)}) collective-permute-start(bf16[1024,1024]{1,0:T(8,128)(2,1)} %shard_map.138), channel_id=1, source_target_pairs={{0,1},{1,0},{2,3},{3,2},{4,5},{5,4},{6,7},{7,6},{8,9},{9,8},{10,11... | collective-permute-start | bytes 6291464 | tf_op jit(solution)/shard_map/ppermute | solution.py:16
  307.4 47.4 %collective-permute-start.23 = (bf16[2,128,2048]{2,1,0:T(8,128)(2,1)}, bf16[2,128,2048]{2,1,0:T(8,128)(2,1)}, u32[]{:S(2)}, u32[]{:S(2)}) collective-permute-start(bf16[2,128,2048]{2,1,0:T(8,128)(2,1)} %get-tuple-element.72.refs_2_), channel_id=1, source_target_pairs={{0,4},{1,5},{2,6},{3,7},{4,0},{5,1},{6,2},{7,3},{8,12},{9,13},{10,... | collective-permute-start | bytes 3145736 | tf_op jit(solution)/shard_map/ppermute | solution.py:16
  307.6 67.2 %collective-permute-start.32 = (bf16[640,768]{1,0:T(8,128)(2,1)}, bf16[640,768]{1,0:T(8,128)(2,1)S(1)}, u32[]{:S(2)}, u32[]{:S(2)}) collective-permute-start(bf16[640,768]{1,0:T(8,128)(2,1)} %shard_map.141), channel_id=1, source_target_pairs={{0,8},{1,9},{2,10},{3,11},{4,12},{5,13},{6,14},{7,15},{8,0},{9,1},... | collective-permute-start | bytes 2949128 | tf_op jit(solution)/shard_map/ppermute | solution.py:16
  319.3 74.0 %collective-permute-start.33 = (bf16[2,2,128,1024]{3,2,1,0:T(8,128)(2,1)}, bf16[2,2,128,1024]{3,2,1,0:T(8,128)(2,1)S(1)}, u32[]{:S(2)}, u32[]{:S(2)}) collective-permute-start(bf16[2,2,128,1024]{3,2,1,0:T(8,128)(2,1)} %get-tuple-element.78.refs_2_), channel_id=1, source_target_pairs={{0,2},{1,3},{2,0},{3,1},{4,6},{5,7},{6,4},{7,5},{8,10},{9,11},{10,... | collective-permute-start | bytes 3145736 | tf_op jit(solution)/shard_map/ppermute | solution.py:16
  319.9 73.3 %collective-permute-start.34 = (bf16[2,2,128,1024]{3,2,1,0:T(8,128)(2,1)}, bf16[2,2,128,1024]{3,2,1,0:T(8,128)(2,1)}, u32[]{:S(2)}, u32[]{:S(2)}) collective-permute-start(bf16[2,2,128,1024]{3,2,1,0:T(8,128)(2,1)} %get-tuple-element.84), channel_id=1, source_target_pairs={{0,4},{1,5},{2,6},{3,7},{4,0},{5,1},{6,2},{7,3},{8,12},{9,13},{10,... | collective-permute-start | bytes 3145736 | tf_op jit(solution)/shard_map/ppermute | solution.py:16
  320.5 56.8 %collective-permute-start.31 = (bf16[640,768]{1,0:T(8,128)(2,1)}, bf16[640,768]{1,0:T(8,128)(2,1)}, u32[]{:S(2)}, u32[]{:S(2)}) collective-permute-start(bf16[640,768]{1,0:T(8,128)(2,1)} %collective-permute-done.27.refs_3_.refs_1_.refs_5_), channel_id=1, source_target_pairs={{0,16},{16,0},{1,17},{17,1},{2,18},{18,2},{3,19},{19,3},{4,20},{20... | collective-permute-start | bytes 2949128 | tf_op jit(solution)/shard_map/ppermute | solution.py:16
  374.8 1.6 copy-start.21
  374.8 1.0 copy-start.6
  375.8 44.2 %collective-permute-start.39 = (bf16[640,768]{1,0:T(8,128)(2,1)}, bf16[640,768]{1,0:T(8,128)(2,1)S(1)}, u32[]{:S(2)}, u32[]{:S(2)}) collective-permute-start(bf16[640,768]{1,0:T(8,128)(2,1)} %shard_map.143.refs_11_.refs_5_), channel_id=1, source_target_pairs={{0,16},{16,0},{1,17},{17,1},{2,18},{18,2},{3,19},{19,3},{4,20},{20... | collective-permute-start | bytes 2949128 | tf_op jit(solution)/shard_map/ppermute | solution.py:16
  376.3 25.8 %collective-permute-start.30 = (bf16[128,2048]{1,0:T(8,128)(2,1)S(1)}, bf16[128,2048]{1,0:T(8,128)(2,1)S(1)}, u32[]{:S(2)}, u32[]{:S(2)}) collective-permute-start(bf16[128,2048]{1,0:T(8,128)(2,1)S(1)} %copy-done.21), channel_id=1, source_target_pairs={{0,8},{1,9},{2,10},{3,11},{4,12},{5,13},{6,14},{7,15},{8,0},{9,1},... | collective-permute-start | bytes 1572872 | tf_op jit(solution)/shard_map/ppermute | solution.py:16
  393.3 1.0 copy-start.11
  398.6 13.1 %collective-permute-start.35 = (bf16[2,128,1024]{2,1,0:T(8,128)(2,1)}, bf16[2,128,1024]{2,1,0:T(8,128)(2,1)S(1)}, u32[]{:S(2)}, u32[]{:S(2)}) collective-permute-start(bf16[2,128,1024]{2,1,0:T(8,128)(2,1)} %get-tuple-element.86), channel_id=1, source_target_pairs={{0,4},{1,5},{2,6},{3,7},{4,0},{5,1},{6,2},{7,3},{8,12},{9,13},{10,... | collective-permute-start | bytes 1572872 | tf_op jit(solution)/shard_map/ppermute | solution.py:16
  401.1 11.5 %collective-permute-start.36 = (bf16[2,128,1024]{2,1,0:T(8,128)(2,1)}, bf16[2,128,1024]{2,1,0:T(8,128)(2,1)S(1)}, u32[]{:S(2)}, u32[]{:S(2)}) collective-permute-start(bf16[2,128,1024]{2,1,0:T(8,128)(2,1)} %get-tuple-element.88), channel_id=1, source_target_pairs={{0,2},{1,3},{2,0},{3,1},{4,6},{5,7},{6,4},{7,5},{8,10},{9,11},{10,... | collective-permute-start | bytes 1572872 | tf_op jit(solution)/shard_map/ppermute | solution.py:16
  417.0 19.8 %collective-permute-start.37 = (bf16[128,1024]{1,0:T(8,128)(2,1)}, bf16[128,1024]{1,0:T(8,128)(2,1)S(1)}, u32[]{:S(2)}, u32[]{:S(2)}) collective-permute-start(bf16[128,1024]{1,0:T(8,128)(2,1)} %get-tuple-element.90.refs_11_), channel_id=1, source_target_pairs={{0,8},{1,9},{2,10},{3,11},{4,12},{5,13},{6,14},{7,15},{8,0},{9,1},... | collective-permute-start | bytes 786440 | tf_op jit(solution)/shard_map/ppermute | solution.py:16
  417.3 22.7 %collective-permute-start.38 = (bf16[128,1024]{1,0:T(8,128)(2,1)}, bf16[128,1024]{1,0:T(8,128)(2,1)S(1)}, u32[]{:S(2)}, u32[]{:S(2)}) collective-permute-start(bf16[128,1024]{1,0:T(8,128)(2,1)} %get-tuple-element.92), channel_id=1, source_target_pairs={{0,8},{1,9},{2,10},{3,11},{4,12},{5,13},{6,14},{7,15},{8,0},{9,1},... | collective-permute-start | bytes 786440 | tf_op jit(solution)/shard_map/ppermute | solution.py:16
  436.8 3.2 copy-start.32
  (10 other events, 8.2 us)

commit v3 on v2

--- a/solution.py
+++ b/solution.py
@@ -216,12 +216,16 @@
     return jnp.concatenate([first, second], axis=1)
 
 
-VMEM_BYTES = 56 * 2**20
+VMEM_BYTES = 62 * 2**20
 LIGHT = 1000
-OUT_PARTS = (3, 3, 2)
-BACK_PARTS = (4, 4)
+BACK_TILE = 512
+GRAD_TILE = 512
+ROWS_TILE = 256
+OUT_PARTS = (2, 2, 2, 2)
+BACK_PARTS = (3, 3, 2)
 CUTS = 1
 MIXED = True
+MIXED_OUT = True
 NN = ((1,), (0,))
 NT = ((1,), (1,))
 TN = ((0,), (0,))
@@ -264,7 +268,7 @@
     return pl.BlockSpec(shape, lambda j, s: (0,) * len(shape))
 
 
-def rows_kernel(count, cuts, dims, capacity, half_ref, slot_ref, *refs):
+def rows_kernel(count, dims, capacity, half_ref, slot_ref, *refs):
     pieces = refs[:4]
     weights = refs[4 : 4 + count]
     outs, rows = refs[4 + count : -1], refs[-1]
@@ -273,29 +277,30 @@
 
     @pl.when(pl.program_id(0) == 0)
     def _():
-        place = lax.broadcasted_iota(jnp.int32, (capacity, tokens), 0)
-        for local in range(slot_ref.shape[0]):
-            pick = (place == slot_ref[local : local + 1, :]).astype(F32).astype(BF)
+        place = lax.broadcasted_iota(jnp.int32, (2 * capacity, 2 * tokens), 0)
+        for pair in range(slot_ref.shape[0] // 2):
+            slots = [slot_ref[2 * pair + i : 2 * pair + i + 1, :] for i in range(2)]
+            pick = (place == jnp.concatenate(slots, axis=1)).astype(F32).astype(BF)
+            at = 2 * pair * capacity
             for side in range(2):
-                block = pieces[2 * side + local % 2][local // 2]
-                rows[local * capacity : (local + 1) * capacity, side * width : (side + 1) * width] = (
-                    contract(pick, block, NN).astype(BF)
+                block = jnp.concatenate(
+                    [pieces[2 * side + i][pair] for i in range(2)], axis=0
                 )
+                rows[at : at + 2 * capacity, side * width : (side + 1) * width] = contract(
+                    pick, block, NN
+                ).astype(BF)
 
     for w in range(count):
-        value = contract(rows[...], weights[w][...], dims).astype(BF)
-        width = value.shape[1] // cuts
-        for cut in range(cuts):
-            outs[w * cuts + cut][...] = value[:, cut * width : (cut + 1) * width]
-
-
-def rows_product(half, slots, pieces, weights, dims, capacity, width, cuts=1, deps=()):
+        outs[0][w] = contract(rows[...], weights[w][...], dims).astype(BF)
+
+
+def rows_product(half, slots, pieces, weights, dims, capacity, width, deps=()):
     sources, tokens = slots.shape
     mine = sources // 2
     depth = mine // 2
     slab = 2 * width
     hidden = weights[0].shape[1] if dims == NN else weights[0].shape[0]
-    tile = min(256, hidden) if cuts == 1 else hidden
+    tile = min(ROWS_TILE, hidden)
     rows = mine * capacity
     weight_spec = (
         pl.BlockSpec((slab, tile), lambda j, s: (0, j))
@@ -304,13 +309,13 @@
     )
     count = len(weights)
     return call(
-        functools.partial(rows_kernel, count, cuts, dims, capacity),
+        functools.partial(rows_kernel, count, dims, capacity),
         (hidden // tile,),
         [pl.BlockSpec((mine, tokens), lambda j, s: (s[0], 0))]
         + [pl.BlockSpec((depth, tokens, width), lambda j, s: (s[0], 0, 0))] * 4
         + [weight_spec] * count,
-        [pl.BlockSpec((rows, tile // cuts), lambda j, s: (0, j))] * (count * cuts),
-        [jax.ShapeDtypeStruct((rows, hidden // cuts), BF)] * (count * cuts),
+        [pl.BlockSpec((count, rows, tile), lambda j, s: (0, 0, j))],
+        [jax.ShapeDtypeStruct((count, rows, hidden), BF)],
         [pltpu.VMEM((rows, slab), BF)],
         2 * count * rows * slab * hidden,
         2 * slab * (count * hidden + mine * tokens),
@@ -320,14 +325,16 @@
 
 def spread(dp, column_ref, sources, capacity, act):
     tokens = column_ref.shape[1]
-    place = lax.broadcasted_iota(jnp.int32, (tokens, capacity), 1)
+    place = lax.broadcasted_iota(jnp.int32, (2 * tokens, 2 * capacity), 1)
     mine = sources // 2
-    for block in range(sources):
-        upper = jnp.bitwise_xor(dp, block // mine)
-        position = block % mine + mine * upper
-        pick = (place == column_ref[position]).astype(F32).astype(BF)
-        start = pl.multiple_of(((block % mine) // 2 + (mine // 2) * upper) * tokens, tokens)
-        act(block % 2, start, pick, block, position)
+    for pair in range(mine):
+        half, local = divmod(2 * pair, mine)
+        upper = jnp.bitwise_xor(dp, half)
+        position = local + mine * upper
+        column = column_ref[pl.ds(position, 2)].reshape(2 * tokens, 1)
+        pick = (place == column).astype(F32).astype(BF)
+        start = pl.multiple_of((local // 2 + (mine // 2) * upper) * tokens, tokens)
+        act(start, pick, half, local * capacity, position)
 
 
 def back_kernel(count, dims, capacity, dp_ref, column_ref, *refs):
@@ -336,17 +343,17 @@
     spreads = refs[-2 * count :]
     keep_ref, sends = refs[3 * count], refs[3 * count + 1 : -2 * count]
     sources, tokens, _ = column_ref.shape
-    mine = sources // 2
 
     @pl.when(pl.program_id(0) == 0)
     def _():
-        def act(parity, start, pick, block, position):
+        def act(start, pick, half, at, position):
             for v in range(count):
-                rows = values[2 * v + block // mine]
-                at = (block % mine) * capacity
-                spreads[2 * v + parity][pl.ds(start, tokens), :] = contract(
-                    pick, rows[at : at + capacity, :], NN
-                ).astype(BF)
+                rows = values[2 * v + half][at : at + 2 * capacity, :]
+                value = contract(pick, rows, NN).astype(BF)
+                for parity in range(2):
+                    spreads[2 * v + parity][pl.ds(start, tokens), :] = value[
+                        parity * tokens : (parity + 1) * tokens
+                    ]
 
         spread(dp_ref[0], column_ref, sources, capacity, act)
 
@@ -359,12 +366,15 @@
     keep_ref[...] = total(0)
     sent = total(1)
     tile = sent.shape[1]
-    spots = [(send, at) for send in sends for at in range(0, send.shape[1], tile)]
-    for step, (send, at) in enumerate(spots):
+    unit = min(256, tile)
+    spots = [(send, at) for send in sends for at in range(0, send.shape[1], unit)]
+    per = tile // unit
+    for step in range(len(spots) // per):
 
         @pl.when(pl.program_id(0) == step)
         def _():
-            send[:, at : at + tile] = sent
+            for n, (send, at) in enumerate(spots[step * per : (step + 1) * per]):
+                send[:, at : at + unit] = sent[:, n * unit : (n + 1) * unit]
 
 
 def back_product(dp, columns, values, weights, dims, capacity, parts, deps=()):
@@ -372,7 +382,7 @@
     specs, values = zip(*[whole(value) for value in values])
     hidden = values[0].shape[-1]
     slab = weights[0].shape[1] if dims == NN else weights[0].shape[0]
-    tile = 256
+    tile, unit = BACK_TILE, 256
     count = len(weights)
     out_rows = sources * tokens // 2
     weight_spec = (
@@ -385,9 +395,9 @@
         (slab // tile,),
         [fixed(columns.shape)] + list(specs) + [weight_spec] * count,
         [pl.BlockSpec((out_rows, tile), lambda j, s: (0, j))]
-        + [pl.BlockSpec((out_rows, tile * part), lambda j, s: (0, 0)) for part in parts],
+        + [pl.BlockSpec((out_rows, unit * part), lambda j, s: (0, 0)) for part in parts],
         [jax.ShapeDtypeStruct((out_rows, slab), BF)]
-        + [jax.ShapeDtypeStruct((out_rows, tile * part), BF) for part in parts],
+        + [jax.ShapeDtypeStruct((out_rows, unit * part), BF) for part in parts],
         [pltpu.VMEM((out_rows, hidden), BF)] * (2 * count),
         4 * count * out_rows * slab * hidden,
         2 * slab * (count * hidden + 2 * out_rows),
@@ -407,17 +417,19 @@
 
     @pl.when(step == 0)
     def _():
-        def act(parity, start, pick, block, position):
-            place = lax.broadcasted_iota(jnp.int32, (tokens, capacity), 1)
-            pair_pick = (place == pair_columns[position]).astype(F32).astype(BF)
-            at = (block % mine) * capacity
-            rows = (own if block < mine else other)[at : at + capacity, :]
-            pair_rows = (beyond if block < mine else crossed)[at : at + capacity, :]
+        def act(start, pick, half, at, position):
+            place = lax.broadcasted_iota(jnp.int32, (2 * tokens, 2 * capacity), 1)
+            column = pair_columns[pl.ds(position, 2)].reshape(2 * tokens, 1)
+            pair_pick = (place == column).astype(F32).astype(BF)
+            rows = (own, other)[half][at : at + 2 * capacity, :]
+            pair_rows = (beyond, crossed)[half][at : at + 2 * capacity, :]
             value = contract(pick, rows, NN) + contract(pair_pick, pair_rows, NN)
-            if flat:
-                spreads[parity][pl.ds(start, tokens), :] = value.astype(BF)
-            else:
-                spreads[parity][:, pl.ds(start, tokens)] = value.T.astype(BF)
+            for parity in range(2):
+                part = value[parity * tokens : (parity + 1) * tokens]
+                if flat:
+                    spreads[parity][pl.ds(start, tokens), :] = part.astype(BF)
+                else:
+                    spreads[parity][:, pl.ds(start, tokens)] = part.T.astype(BF)
 
         spread(dp_ref[0], columns, sources, capacity, act)
 
@@ -448,7 +460,7 @@
     specs, values = zip(*[whole(value) for value in values])
     hidden = values[0].shape[-1]
     slab = 2 * width
-    tile = min(256, width)
+    tile = min(GRAD_TILE, width)
     steps = slab // tile
     depth = sources // 2
     first = pl.BlockSpec(
@@ -473,64 +485,64 @@
     )(dp, columns, pair_columns, *values, *pieces)
 
 
-def split_kernel(axes, *refs):
+def split_kernel(axes, merge, *refs):
     count = len(axes)
     for i, axis in enumerate(axes):
         total = (refs[2 * i][...].astype(F32) + refs[2 * i + 1][...].astype(F32)).astype(BF)
-        outs = refs[2 * count + 2 * i : 2 * count + 2 * i + 2]
-        for side, out in enumerate(outs):
-            out[...] = total[(slice(None),) * axis + (side,)]
-
-
-def sum_split(kept, coming, axes, sides, deps=()):
+        width = total.shape[-1]
+        for side in range(2):
+            part = total[(slice(None),) * axis + (side,)]
+            if merge:
+                refs[2 * count + side][..., i * width : (i + 1) * width] = part
+            else:
+                refs[2 * count + 2 * i + side][...] = part
+
+
+def sum_split(kept, coming, axes, merge, deps=()):
     tokens = kept[0].shape[-2]
     chunk = min(32, tokens)
     in_specs, out_specs, out_shape, operands = [], [], [], []
-    for k, c, axis, side in zip(kept, coming, axes, sides):
-        lead = k.shape[:-2]
-        width = k.shape[-1] // (1 if side is None else 2)
-        at = 0 if side is None else side
+    for k, c, axis in zip(kept, coming, axes):
+        lead, width = k.shape[:-2], k.shape[-1]
         spec = pl.BlockSpec(
-            lead + (chunk, width), functools.partial(lambda n, at, j: (0,) * n + (j, at), len(lead), at)
+            lead + (chunk, width), functools.partial(lambda n, j: (0,) * n + (j, 0), len(lead))
         )
         in_specs += [spec, spec]
         operands += [k, c]
         left = lead[:axis] + lead[axis + 1 :]
+        width = width * len(kept) if merge else width
         out_specs += [
             pl.BlockSpec(
                 left + (chunk, width), functools.partial(lambda n, j: (0,) * n + (j, 0), len(left))
             )
         ] * 2
         out_shape += [jax.ShapeDtypeStruct(left + (tokens, width), BF)] * 2
-    moved = sum(3 * 2 * value.size for value in kept)
     return call(
-        functools.partial(split_kernel, tuple(axes)),
+        functools.partial(split_kernel, tuple(axes), merge),
         (tokens // chunk,),
         in_specs,
-        out_specs,
-        out_shape,
+        out_specs[:2] if merge else out_specs,
+        out_shape[:2] if merge else out_shape,
         [],
-        moved // 4,
-        moved,
+        0,
+        0,
         deps,
         prefetch=0,
     )(*operands)
 
 
 def first_kernel(mixed, keep, *refs):
-    outs = refs[-4:] if mixed else refs[-2:]
-    pieces = refs[: -len(outs)]
+    outs, pieces = refs[-4:], refs[:-4]
     each = outs[0].shape[-1]
-    at = 0
+    at, width = 0, min(256, each)
     for piece in pieces:
-        width = min(piece.shape[-1], each)
         for first in range(0, piece.shape[-1], width):
             total = keep[..., at : at + width].astype(F32)
             total = (total + piece[..., first : first + width].astype(F32)).astype(BF)
             right, place = divmod(at, each)
             for side in range(2):
                 outs[side + 2 * right][..., place : place + width] = (
-                    total[:, side] if right else total[:, :, side]
+                    total[:, side] if mixed and right else total[:, :, side]
                 )
             at += width
 
@@ -540,7 +552,7 @@
     chunk = min(16, tokens)
     four = lambda j: (0, 0, j, 0)
     five = lambda j: (0, 0, 0, j, 0)
-    outs = 4 if mixed else 2
+    outs = 4
     each = 2 * width // outs
     return call(
         functools.partial(first_kernel, mixed),
@@ -632,34 +644,33 @@
     )(*operands)
 
 
-def hidden_kernel(gate_kept, gate_coming, up_kept, up_coming, prob, out):
-    gate = gate_kept[...].astype(F32) + gate_coming[...].astype(F32)
-    up = up_kept[...].astype(F32) + up_coming[...].astype(F32)
+def hidden_kernel(kept, coming, prob, out):
+    gate = kept[0].astype(F32) + coming[0].astype(F32)
+    up = kept[1].astype(F32) + coming[1].astype(F32)
     out[...] = (gate * jax.nn.sigmoid(gate) * up * prob[...]).astype(BF)
 
 
-def slopes_kernel(
-    gate_kept, gate_coming, up_kept, up_coming, prob, grad_kept, *refs
-):
-    gate = gate_kept[...].astype(F32) + gate_coming[...].astype(F32)
-    up = up_kept[...].astype(F32) + up_coming[...].astype(F32)
-    out, gate_out, up_out = refs[-3:]
-    grad_coming = jnp.concatenate([ref[...] for ref in refs[:-3]], axis=1)
-    grad = (grad_kept[...].astype(F32) + grad_coming.astype(F32)) * prob[...]
+def slopes_kernel(kept, coming, prob, grad_kept, grad_coming, out):
+    gate = kept[0].astype(F32) + coming[0].astype(F32)
+    up = kept[1].astype(F32) + coming[1].astype(F32)
+    grad = (grad_kept[0].astype(F32) + grad_coming[0].astype(F32)) * prob[...]
     sigma = jax.nn.sigmoid(gate)
     out[0] = (grad * up * sigma * (1.0 + gate * (1.0 - sigma))).astype(BF)
     out[1] = (grad * gate * sigma).astype(BF)
-    gate_out[...] = out[0]
-    up_out[...] = out[1]
 
 
 def by_rows(kernel, operands, stacks, outs, deps=()):
-    rows, hidden = operands[0].shape
+    rows, hidden = operands[0].shape[1:]
     chunk = rows // 5 if rows % 80 == 0 else rows
     return call(
         kernel,
         (rows // chunk,),
-        [pl.BlockSpec((chunk, value.shape[1]), lambda j: (j, 0)) for value in operands],
+        [
+            pl.BlockSpec((chunk, 1), lambda j: (j, 0))
+            if value.ndim == 2
+            else pl.BlockSpec((value.shape[0], chunk, hidden), lambda j: (0, j, 0))
+            for value in operands
+        ],
         [pl.BlockSpec((2, chunk, hidden), lambda j: (0, j, 0))] * stacks
         + [pl.BlockSpec((chunk, hidden), lambda j: (j, 0))] * outs,
         [jax.ShapeDtypeStruct((2, rows, hidden), BF)] * stacks
@@ -720,7 +731,7 @@
     token_now = widen(token_now, (8, 8))
     token_now = widen(token_now, (4, 2))
     token_now = widen(token_now, (2, 4))
-    cot_whole = after(cotangent, *token_now).reshape(1, 1, 1, token_count, slab)
+    cot_whole = cotangent.reshape(1, 1, 1, token_count, slab)
 
     def finish(now):
         pieces = []
@@ -750,43 +761,47 @@
     hit, slots = selection(copy)
     _, pair_slots = selection(jnp.bitwise_xor(copy, mine))
     pair_slots = jnp.where(paired[0] == 1, pair_slots, -1)
+    select = jnp.arange(capacity, dtype=jnp.int32)[None, :, None] == slots[:, None, :]
+    shift = capacity * (jnp.arange(n_expert, dtype=jnp.int32) % 2)[:, None]
+    slots, pair_slots = [
+        jnp.where(value < 0, value, value + shift) for value in (slots, pair_slots)
+    ]
     columns, pair_columns = slots[:, :, None], pair_slots[:, :, None]
     prob = jnp.sum(jnp.where(hit, probs, 0.0), axis=2)
-    select = jnp.arange(capacity, dtype=jnp.int32)[None, :, None] == slots[:, None, :]
     row_prob = jnp.sum(jnp.where(select, prob[:, None, :], 0.0), axis=2)
     prob_own = lax.dynamic_slice_in_dim(row_prob, dp * mine, mine).reshape(mine * capacity, 1)
 
-    def rows_of(which, pieces, weights, dims, cuts=1, deps=()):
-        return rows_product(which, slots, pieces, weights, dims, capacity, half, cuts, deps)
+    def rows_of(which, pieces, weights, dims, *deps):
+        return rows_product(which, slots, pieces, weights, dims, capacity, half, deps)[0]
 
     def over(value):
         return exchange(value, "dp", 1)
 
     leaving = rows_of(other_one, token_pieces, [gate_slab, up_slab], NN)
-    gate_coming, up_coming = over(leaving[0]), over(leaving[1])
-    cot_now = join([cot_whole], [cross(cot_whole, 8)], (0, 0), (leaving[1],), True)
-    gate_kept, up_kept = rows_of(
-        dp_one, token_pieces, [gate_slab, up_slab], NN, 1, (cot_now[0],)
-    )
-    cot_now = widen(cot_now, (4, 2), None, (up_kept, gate_coming))
-    cot_pieces = finish(widen(cot_now, (2, 4), None, (up_coming,)))
-    both = [gate_kept, gate_coming, up_kept, up_coming, prob_own]
-    (hid,) = by_rows(hidden_kernel, both, 0, 1, (cot_pieces[0],))
+    coming = over(leaving)
+    cot_now = join([cot_whole], [cross(cot_whole, 8)], (0, 0), (leaving,), True)
+    kept = rows_of(dp_one, token_pieces, [gate_slab, up_slab], NN, cot_now[0])
+    cot_now = widen(cot_now, (4, 2), None, (kept,))
+    cot_third = [cross(value, bit) for value, bit in zip(cot_now, (2, 4))]
+    (hid,) = by_rows(hidden_kernel, [kept, coming, prob_own], 0, 1)
     hid_crossed = cross(hid, mine)
     hid_other = over(hid)
-
-    (leaving,) = rows_of(other_one, cot_pieces, [down_slab], NT, 1, (hid,))
+    cot_pieces = finish(widen(cot_now, (2, 4), cot_third, (hid,)))
+    leaving = rows_of(other_one, cot_pieces, [down_slab], NT)
     dhid_coming = over(leaving)
-    (dhid_kept,) = rows_of(dp_one, cot_pieces, [down_slab], NT)
+    dhid_kept = rows_of(dp_one, cot_pieces, [down_slab], NT)
     out_keep, *out_send = back_product(
-        dp_one, columns, [hid, hid_other], [down_slab], NN, capacity, OUT_PARTS, (dhid_kept,)
-    )
-    slopes, dgate_sent, dup_sent = by_rows(
-        slopes_kernel, both + [dhid_kept, dhid_coming], 1, 2, (out_send[0],)
-    )
-    out_send[0] = after(out_send[0], hid_crossed)
+        dp_one, columns, [hid, hid_other], [down_slab], NN, capacity, OUT_PARTS, (dhid_kept, leaving)
+    )
+    (slopes,) = by_rows(
+        slopes_kernel,
+        [kept, coming, prob_own, dhid_kept, dhid_coming],
+        1,
+        0,
+        (out_send[0], hid_crossed),
+    )
     slopes_other = over(slopes)
-    dgate_crossed = cross(dgate_sent, mine)
+    slopes_crossed = cross(slopes, mine)
 
     shape = (2, 2, 2, token_count, slab)
 
@@ -797,7 +812,7 @@
     def next_sum(parts, bits, axis, *deps):
         kept, sent = parts[::2], parts[1::2]
         coming = [cross(value, bit) for value, bit in zip(sent, bits)]
-        return sum_split(kept, coming, [axis] * len(kept), [None] * len(kept), deps)
+        return sum_split(kept, coming, [axis] * len(kept), axis == 0, deps)
 
     def end_sum(parts, *deps):
         return last_sum(parts[::2], [cross(value, 8) for value in parts[1::2]], deps)
@@ -807,7 +822,9 @@
             dp_one, columns, pair_columns, values, pieces, flat, capacity, half, deps
         )
 
-    out_parts = first_sum(out_keep, out_send, False)
+    out_parts = first_sum(out_keep, out_send, MIXED_OUT)
+    out_bits = ((2, 4), (4, 2)) if MIXED_OUT else ((2, 2), (4, 4))
+    back_bits = ((2, 4), (4, 2)) if MIXED else ((2, 2), (4, 4))
     back_keep, *back_send = back_product(
         dp_one,
         columns,
@@ -818,35 +835,26 @@
         BACK_PARTS,
         (out_parts[1],),
     )
-    dup_crossed = cross(after(dup_sent, dgate_crossed), mine)
-    hid_crossed = after(hid_crossed, slopes_other, out_parts[1])
     hid_beyond = over(hid_crossed)
-    out_parts = next_sum(out_parts, (2,), 1)
-    back_send[0] = after(back_send[0], hid_beyond, out_parts[1], dgate_crossed)
-    dgate_beyond = over(dgate_crossed)
-    back_parts = first_sum(back_keep, back_send, MIXED)
-    bits = ((2, 4), (4, 2)) if MIXED else ((2,), (4,))
-    out_parts = next_sum(out_parts, (4,), 0, back_parts[1])
+    out_parts = next_sum(out_parts, out_bits[0], 1, back_keep)
+    back_send[1] = after(back_send[1], out_parts[1])
+    back_parts = list(first_sum(back_keep, back_send, MIXED))
+    back_parts[3] = after(back_parts[3], slopes_crossed)
+    slopes_beyond = [over(slopes_crossed[part]) for part in range(2)]
+
+    def slope_values(part):
+        stacks = [(value, part) for value in (slopes, slopes_other, slopes_crossed)]
+        return stacks + [slopes_beyond[part]]
+
+    out_parts = next_sum(out_parts, out_bits[1], 0, back_parts[3])
     grad_down = gradient(
-        [hid, hid_other, hid_crossed, hid_beyond], cot_pieces, False, out_parts[1]
-    )
-    dup_crossed = after(dup_crossed, grad_down)
-    dup_beyond = over(dup_crossed)
-    grad_gate = gradient(
-        [(slopes, 0), (slopes_other, 0), dgate_crossed, dgate_beyond],
-        token_pieces,
-        True,
-        dup_crossed,
-    )
-    output = end_sum(out_parts, grad_gate)
-    back_parts = next_sum(back_parts, bits[0], 1, grad_gate)
-    back_parts = next_sum(back_parts, bits[1], 0, output)
-    grad_up = gradient(
-        [(slopes, 1), (slopes_other, 1), dup_crossed, dup_beyond],
-        token_pieces,
-        True,
-        back_parts[1],
-    )
+        [hid, hid_other, hid_crossed, hid_beyond], cot_pieces, False, back_parts[3]
+    )
+    output = end_sum(out_parts, grad_down)
+    back_parts = next_sum(back_parts, back_bits[0], 1, output)
+    grad_gate = gradient(slope_values(0), token_pieces, True, back_parts[1])
+    back_parts = next_sum(back_parts, back_bits[1], 0, grad_gate)
+    grad_up = gradient(slope_values(1), token_pieces, True, back_parts[1])
     grad_tokens = end_sum(back_parts)
     return (output, grad_tokens, grad_gate[None], grad_up[None], grad_down[None])
 

time: 445 us -> 413 us (0.928)
  waiting for transfers between devices: 182 us -> 163 us
  local copies, waits for them, and re-layouts: 27.8 us -> 20.7 us
  Pallas kernels: 182 us -> 176 us
    ppermute x40 -> x41, waiting for transfers between devices: 182 us -> 163 us  [exchange(): return lax.ppermute(value, axis, pairs)]
    unnamed x69 -> x46, local copies, waits for them, and re-layouts: 21.9 us -> 11.8 us
    pallas_call x25, Pallas kernels: 182 us -> 176 us  [call(): return lambda *operands: run(*operands, *deps)]
    ppermute x40 -> x41, starting transfers between devices: 44.7 us -> 46.6 us  [exchange(): return lax.ppermute(value, axis, pairs)]
  transfers between devices with their start and end apart: 40 -> 41, of which waited for: 22 -> 19; matrix products, arithmetic and copies ran while one was open for 2% -> 3% of each run, Pallas kernels for 38% -> 39%
where the time goes in v3:
time: 413 us; the launch traced here: 412 us
  Pallas kernels  176 us (43%)
  waiting for transfers between devices  163 us (39%)
  starting transfers between devices  46.6 us (11%)
  local copies, waits for them, and re-layouts  20.7 us (5%)
    pallas_call x25, Pallas kernels, call(): return lambda *operands: run(*operands, *deps)  176 us
    ppermute x41, waiting for transfers between devices, exchange(): return lax.ppermute(value, axis, pairs)  163 us
    ppermute x41, starting transfers between devices, exchange(): return lax.ppermute(value, axis, pairs)  46.6 us
    unnamed x46, local copies, waits for them, and re-layouts  11.8 us
  transfers between devices with their start and end apart: 41, of which 19 were waited for; matrix products, arithmetic and copies ran while one was open for 3% of the time, Pallas kernels for 39%

profile of v3, /device:TPU:0, one launch (start us, length us, event | category | flops | bytes accessed | tf_op | source)
XLA Modules:
  0.0 411.9 jit_solution(4029386328047996773)
XLA Ops:
  3.3 4.1 collective-permute-start
  7.5 24.5 %collective-permute-done.1.refs_3_ = bf16[1,1,1,128,1024]{4,3,2,1,0:T(8,128)(2,1)S(1)} collective-permute-done((bf16[1,1,1,128,1024]{4,3,2,1,0:T(8,128)(2,1)S(1)}, bf16[1,1,1,128,1024]{4,3,2,1,0:T(8,128)(2,1)S(1)}, u32[]{:S(2)}, u32[]{:S(2)}) %collective-permute-start.1) | collective-permute-done | bytes 262176 | tf_op jit(solution)/shard_map/ppermute | solution.py:16
  33.4 2.0 shard_map.119
  36.2 1.5 collective-permute-start.3
  37.7 12.3 %collective-permute-done.3.refs_3_ = bf16[2,1,1,128,1024]{4,3,2,1,0:T(8,128)(2,1)S(1)} collective-permute-done((bf16[2,1,1,128,1024]{4,3,2,1,0:T(8,128)(2,1)}, bf16[2,1,1,128,1024]{4,3,2,1,0:T(8,128)(2,1)S(1)}, u32[]{:S(2)}, u32[]{:S(2)}) %collective-permute-start.3) | collective-permute-done | bytes 524320 | tf_op jit(solution)/shard_map/ppermute | solution.py:16
  51.6 2.5 shard_map.120
  54.1 1.6 collective-permute-start.4
  56.6 23.1 %collective-permute-done.5.refs_3_ = bf16[2,1,2,128,1024]{4,3,2,1,0:T(8,128)(2,1)} collective-permute-done((bf16[2,1,2,128,1024]{4,3,2,1,0:T(8,128)(2,1)}, bf16[2,1,2,128,1024]{4,3,2,1,0:T(8,128)(2,1)}, u32[]{:S(2)}, u32[]{:S(2)}) %collective-permute-start.5) | collective-permute-done | bytes 1048608 | tf_op jit(solution)/shard_map/ppermute | solution.py:16
  79.6 1.5 collective-permute-done.4.refs_1_
  82.1 3.5 shard_map.121
  86.1 3.4 collective-permute-start.8
  90.5 2.5 collective-permute-done.6.refs_3_.refs_8_
  93.2 1.3 copy-done.1
  96.7 9.6 %shard_map.122.refs_2_ = bf16[2,640,768]{2,1,0:T(8,128)(2,1)} custom-call(s32[1]{0:T(128)} %bitcast.13.refs_0_, s32[16,128]{1,0:T(8,128)} %get-tuple-element.96.refs_1_, bf16[8,128,1152]{2,1,0:T(8,128)(2,1)} %bitcast.45, bf16[8,128,1152]{2,1,0:T(8,128)(2,1)} %copy-done.1, bf16[8,128,1024]{2,1,0:T(8,128)(2,1)} %bitcast.52, ...), custom_call_target="tpu_custom_call" | custom-call | flops 4026531 | bytes 10485 | tf_op jit(solution)/shard_map/pallas_call | solution.py:257
  106.3 1.5 collective-permute-start.9
  107.8 5.4 %collective-permute-done.8.refs_1_ = bf16[1,1,1,128,2048]{4,3,2,1,0:T(8,128)(2,1)} collective-permute-done((bf16[1,1,1,128,2048]{4,3,2,1,0:T(8,128)(2,1)}, bf16[1,1,1,128,2048]{4,3,2,1,0:T(8,128)(2,1)}, u32[]{:S(2)}, u32[]{:S(2)}) %collective-permute-start.8) | collective-permute-done | bytes 524320 | tf_op jit(solution)/shard_map/ppermute | solution.py:16
  113.2 2.0 shard_map.123
  115.8 1.5 collective-permute-start.12
  117.3 9.4 %shard_map.124.refs_0_.refs_4_ = bf16[2,640,768]{2,1,0:T(8,128)(2,1)} custom-call(s32[1]{0:T(128)} %bitcast.refs_0_, s32[16,128]{1,0:T(8,128)} %get-tuple-element.96.refs_1_, bf16[8,128,1152]{2,1,0:T(8,128)(2,1)} %bitcast.46, bf16[8,128,1152]{2,1,0:T(8,128)(2,1)} %copy-done.1, bf16[8,128,1024]{2,1,0:T(8,128)(2,1)} %bitcast.53, ...), custom_call_target="tpu_custom_call" | custom-call | flops 4026531 | bytes 10485 | tf_op jit(solution)/shard_map/pallas_call | solution.py:257
  126.7 2.3 collective-permute-done.11.refs_1_
  129.4 2.4 shard_map.126
  131.8 1.6 collective-permute-start.13
  133.4 1.3 collective-permute-start.14
  136.0 15.4 %collective-permute-done.9.refs_1_ = bf16[2,640,768]{2,1,0:T(8,128)(2,1)S(1)} collective-permute-done((bf16[2,640,768]{2,1,0:T(8,128)(2,1)}, bf16[2,640,768]{2,1,0:T(8,128)(2,1)S(1)}, u32[]{:S(2)}, u32[]{:S(2)}) %collective-permute-start.9) | collective-permute-done | bytes 1966112 | tf_op jit(solution)/shard_map/ppermute | solution.py:16
  151.4 1.3 copy-done.5
  152.7 4.8 %shard_map.125.refs_4_.refs_2_.refs_3_ = bf16[640,768]{1,0:T(8,128)(2,1)} custom-call(bf16[2,640,768]{2,1,0:T(8,128)(2,1)} %shard_map.124.refs_0_.refs_4_, bf16[2,640,768]{2,1,0:T(8,128)(2,1)} %copy-done.5, f32[640,1]{1,0:T(8,128)} %reshape.109.refs_2_), custom_call_target="tpu_custom_call" | custom-call | tf_op jit(solution)/shard_map/pallas_call | solution.py:257
  157.5 3.4 shard_map.127
  161.5 1.5 collective-permute-start.10
  162.9 3.4 collective-permute-start.24
  166.3 2.1 collective-permute-done.16.refs_5_.refs_10_
  168.4 7.2 %shard_map.129.refs_6_ = bf16[1,640,768]{2,1,0:T(8,128)(2,1)} custom-call(s32[1]{0:T(128)} %bitcast.13.refs_0_, s32[16,128]{1,0:T(8,128)} %get-tuple-element.96.refs_1_, bf16[8,128,1024]{2,1,0:T(8,128)(2,1)} %bitcast.68, bf16[8,128,1024]{2,1,0:T(8,128)(2,1)} %collective-permute-done.15.refs_3_.refs_8_, bf16[8,128,1024]{2,1,0:T(8,128)(2,1)} %bitcast.72, ...), custom_call_target="tpu_custom_call" | custom-call | flops 2013265 | bytes 7340 | tf_op jit(solution)/shard_map/pallas_call | solution.py:257
  175.7 1.6 collective-permute-start.23
  177.2 1.4 copy.61.refs_1_
  178.6 7.3 %shard_map.128.refs_5_.refs_3_ = bf16[1,640,768]{2,1,0:T(8,128)(2,1)} custom-call(s32[1]{0:T(128)} %bitcast.refs_0_, s32[16,128]{1,0:T(8,128)} %get-tuple-element.96.refs_1_, bf16[8,128,1024]{2,1,0:T(8,128)(2,1)} %bitcast.69, bf16[8,128,1024]{2,1,0:T(8,128)(2,1)} %collective-permute-done.15.refs_3_.refs_8_, bf16[8,128,1024]{2,1,0:T(8,128)(2,1)} %bitcast.73, ...), custom_call_target="tpu_custom_call" | custom-call | flops 2013265 | bytes 7340 | tf_op jit(solution)/shard_map/pallas_call | solution.py:257
  187.0 13.3 %shard_map.130 = (bf16[1024,2048]{1,0:T(8,128)(2,1)}, bf16[1024,512]{1,0:T(8,128)(2,1)}, bf16[1024,512]{1,0:T(8,128)(2,1)}, bf16[1024,512]{1,0:T(8,128)(2,1)}, bf16[1024,512]{1,0:T(8,128)(2,1)}) custom-call(s32[1]{0:T(128)} %bitcast.refs_0_, s32[16,128,1]{2,1,0:T(8,128)} %copy.61.refs_1_, bf16[640,768]{1,0:T(8,128)(2,1)} %shard_map.125.refs_4_.refs_2_.refs_3_, ...), custom_call_target="tpu_custom_call" | custom-call | flops 6442450 | bytes 11534 | tf_op jit(solution)/shard_map/pallas_call | solution.py:257
  200.9 8.3 %collective-permute-done.24.refs_6_.refs_5_ = bf16[640,768]{1,0:T(8,128)(2,1)} collective-permute-done((bf16[640,768]{1,0:T(8,128)(2,1)S(1)}, bf16[640,768]{1,0:T(8,128)(2,1)}, u32[]{:S(2)}, u32[]{:S(2)}) %collective-permute-start.24) | collective-permute-done | bytes 983072 | tf_op jit(solution)/shard_map/ppermute | solution.py:16
  209.2 6.3 %shard_map.132.refs_2_.refs_4_.refs_3_ = bf16[2,640,768]{2,1,0:T(8,128)(2,1)} custom-call(bf16[2,640,768]{2,1,0:T(8,128)(2,1)} %shard_map.124.refs_0_.refs_4_, bf16[2,640,768]{2,1,0:T(8,128)(2,1)} %copy-done.5, f32[640,1]{1,0:T(8,128)} %reshape.109.refs_2_, bf16[1,640,768]{2,1,0:T(8,128)(2,1)} %shard_map.128.refs_5_.refs_3_, ...), custom_call_target="tpu_custom_call" | custom-call | tf_op jit(solution)/shard_map/pallas_call | solution.py:257
  217.0 8.1 %shard_map.131 = (bf16[2,2,128,1024]{3,2,1,0:T(8,128)(2,1)}, bf16[2,2,128,1024]{3,2,1,0:T(8,128)(2,1)}, bf16[2,2,128,1024]{3,2,1,0:T(8,128)(2,1)}, bf16[2,2,128,1024]{3,2,1,0:T(8,128)(2,1)}) custom-call(bf16[2,2,2,128,2048]{4,3,2,1,0:T(8,128)(2,1)} %bitcast.77, bf16[2,2,2,128,512]{4,3,2,1,0:T(8,128)(2,1)} %bitcast.78, ...), custom_call_target="tpu_custom_call" | custom-call | tf_op jit(solution)/shard_map/pallas_call | solution.py:257
  225.1 1.5 collective-permute-start.21
  227.1 3.5 collective-permute-start.31
  230.5 30.5 %collective-permute-done.25.refs_3_.refs_5_.refs_4_ = bf16[2,640,768]{2,1,0:T(8,128)(2,1)} collective-permute-done((bf16[2,640,768]{2,1,0:T(8,128)(2,1)}, bf16[2,640,768]{2,1,0:T(8,128)(2,1)}, u32[]{:S(2)}, u32[]{:S(2)}) %collective-permute-start.25) | collective-permute-done | bytes 1966112 | tf_op jit(solution)/shard_map/ppermute | solution.py:16
  261.1 21.5 %shard_map.133 = (bf16[1024,2048]{1,0:T(8,128)(2,1)}, bf16[1024,768]{1,0:T(8,128)(2,1)}, bf16[1024,768]{1,0:T(8,128)(2,1)}, bf16[1024,512]{1,0:T(8,128)(2,1)}) custom-call(s32[1]{0:T(128)} %bitcast.refs_0_, s32[16,128,1]{2,1,0:T(8,128)} %copy.61.refs_1_, bf16[2,640,768]{2,1,0:T(8,128)(2,1)} %shard_map.132.refs_2_.refs_4_.refs_3_, ...), custom_call_target="tpu_custom_call" | custom-call | flops 12884901 | bytes 14680 | tf_op jit(solution)/shard_map/pallas_call | solution.py:257
  282.6 4.3 %shard_map.134 = (bf16[2,128,1024]{2,1,0:T(8,128)(2,1)}, bf16[2,128,1024]{2,1,0:T(8,128)(2,1)}, bf16[2,128,1024]{2,1,0:T(8,128)(2,1)}, bf16[2,128,1024]{2,1,0:T(8,128)(2,1)}) custom-call(bf16[2,2,128,1024]{3,2,1,0:T(8,128)(2,1)} %get-tuple-element.63.refs_0_, bf16[2,2,128,1024]{3,2,1,0:T(8,128)(2,1)} %collective-permute-done.21.refs_1_, ...), custom_call_target="tpu_custom_call" | custom-call | tf_op jit(solution)/shard_map/pallas_call | solution.py:257
  289.0 3.1 collective-permute-done.30
  292.1 1.5 collective-permute-start.27
  293.6 7.8 %shard_map.136 = (bf16[2,2,128,1024]{3,2,1,0:T(8,128)(2,1)}, bf16[2,2,128,1024]{3,2,1,0:T(8,128)(2,1)}, bf16[2,2,128,1024]{3,2,1,0:T(8,128)(2,1)}, bf16[2,2,128,1024]{3,2,1,0:T(8,128)(2,1)}) custom-call(bf16[2,2,2,128,2048]{4,3,2,1,0:T(8,128)(2,1)} %bitcast.75, bf16[2,2,2,128,768]{4,3,2,1,0:T(8,128)(2,1)} %bitcast.23.refs_1_, ...), custom_call_target="tpu_custom_call" | custom-call | tf_op jit(solution)/shard_map/pallas_call | solution.py:257
  301.9 13.6 %collective-permute-done.31.refs_1_.refs_5_ = bf16[2,640,768]{2,1,0:T(8,128)(2,1)} collective-permute-done((bf16[2,640,768]{2,1,0:T(8,128)(2,1)S(1)}, bf16[2,640,768]{2,1,0:T(8,128)(2,1)}, u32[]{:S(2)}, u32[]{:S(2)}) %collective-permute-start.31) | collective-permute-done | bytes 1966112 | tf_op jit(solution)/shard_map/ppermute | solution.py:16
  315.6 1.5 collective-permute-start.33
  317.1 6.3 %collective-permute-done.26.refs_1_ = bf16[2,128,1024]{2,1,0:T(8,128)(2,1)} collective-permute-done((bf16[2,128,1024]{2,1,0:T(8,128)(2,1)}, bf16[2,128,1024]{2,1,0:T(8,128)(2,1)}, u32[]{:S(2)}, u32[]{:S(2)}) %collective-permute-start.26) | collective-permute-done | bytes 524320 | tf_op jit(solution)/shard_map/ppermute | solution.py:16
  323.4 3.7 shard_map.138
  327.1 3.0 collective-permute-start.32
  330.1 2.9 slice_bitcast_fusion
  334.8 1.4 copy.65.refs_2_
  336.2 4.3 %collective-permute-done.33.refs_6_ = bf16[640,768]{1,0:T(8,128)(2,1)S(1)} collective-permute-done((bf16[640,768]{1,0:T(8,128)(2,1)}, bf16[640,768]{1,0:T(8,128)(2,1)S(1)}, u32[]{:S(2)}, u32[]{:S(2)}) %collective-permute-start.33) | collective-permute-done | bytes 983072 | tf_op jit(solution)/shard_map/ppermute | solution.py:16
  341.4 15.1 %shard_map.139.refs_2_ = f32[768,2048]{1,0:T(8,128)} custom-call(s32[1]{0:T(128)} %bitcast.refs_0_, s32[16,128,1]{2,1,0:T(8,128)} %copy.61.refs_1_, s32[16,128,1]{2,1,0:T(8,128)} %copy.65.refs_2_, bf16[640,768]{1,0:T(8,128)(2,1)} %shard_map.125.refs_4_.refs_2_.refs_3_, bf16[640,768]{1,0:T(8,128)(2,1)} %copy-done.6, ...), custom_call_target="tpu_custom_call" | custom-call | flops 6442450 | bytes 14680 | tf_op jit(solution)/shard_map/pallas_call | solution.py:257
  356.5 2.1 shard_map.140.refs_4_
  359.6 4.3 %shard_map.141 = (bf16[2,128,1024]{2,1,0:T(8,128)(2,1)}, bf16[2,128,1024]{2,1,0:T(8,128)(2,1)}, bf16[2,128,1024]{2,1,0:T(8,128)(2,1)}, bf16[2,128,1024]{2,1,0:T(8,128)(2,1)}) custom-call(bf16[2,2,128,1024]{3,2,1,0:T(8,128)(2,1)} %get-tuple-element.78.refs_0_, bf16[2,2,128,1024]{3,2,1,0:T(8,128)(2,1)} %collective-permute-done.34.refs_1_, ...), custom_call_target="tpu_custom_call" | custom-call | tf_op jit(solution)/shard_map/pallas_call | solution.py:257
  363.9 2.0 collective-permute-start.36
  366.5 1.5 collective-permute-start.40
  368.0 14.9 %shard_map.142.refs_4_ = f32[2048,768]{1,0:T(8,128)} custom-call(s32[1]{0:T(128)} %bitcast.refs_0_, s32[16,128,1]{2,1,0:T(8,128)} %copy.61.refs_1_, s32[16,128,1]{2,1,0:T(8,128)} %copy.65.refs_2_, bf16[2,640,768]{2,1,0:T(8,128)(2,1)} %shard_map.132.refs_2_.refs_4_.refs_3_, bf16[2,640,768]{2,1,0:T(8,128)(2,1)} %collective-permute-done.25.refs_3_.refs_5_.refs_4_, ...), custom_call_target="tpu_custom_call" | custom-call | flops 6442450 | bytes 14680 | tf_op jit(solution)/shard_map/pallas_call | solution.py:257
  382.9 3.7 shard_map.143
  388.7 14.7 %shard_map.145 = f32[2048,768]{1,0:T(8,128)} custom-call(s32[1]{0:T(128)} %bitcast.refs_0_, s32[16,128,1]{2,1,0:T(8,128)} %copy.61.refs_1_, s32[16,128,1]{2,1,0:T(8,128)} %copy.65.refs_2_, bf16[2,640,768]{2,1,0:T(8,128)(2,1)} %shard_map.132.refs_2_.refs_4_.refs_3_, bf16[2,640,768]{2,1,0:T(8,128)(2,1)} %collective-permute-done.25.refs_3_.refs_5_.refs_4_, ...), custom_call_target="tpu_custom_call" | custom-call | flops 6442450 | bytes 14680 | tf_op jit(solution)/shard_map/pallas_call | solution.py:257
  403.3 6.5 %collective-permute-done.39.refs_1_ = bf16[128,2048]{1,0:T(8,128)(2,1)} collective-permute-done((bf16[128,2048]{1,0:T(8,128)(2,1)}, bf16[128,2048]{1,0:T(8,128)(2,1)}, u32[]{:S(2)}, u32[]{:S(2)}) %collective-permute-start.39) | collective-permute-done | bytes 524320 | tf_op jit(solution)/shard_map/ppermute | solution.py:16
  409.8 2.1 shard_map.144
  (114 shorter events, 27.0 us)
Async XLA Ops:
  3.2 28.7 %copy-start.9 = (bf16[1,1,1,128,1024]{4,3,2,1,0:T(8,128)(2,1)}, bf16[1,1,1,128,1024]{4,3,2,1,0:T(8,128)(2,1)S(1)}, u32[]{:S(2)}) copy-start(bf16[1,1,1,128,1024]{4,3,2,1,0:T(8,128)(2,1)S(1)} %get-tuple-element.91.refs_2_) | copy-start | bytes 786436
  3.3 28.7 %copy-start.7 = (bf16[1,1,1,128,1152]{4,3,2,1,0:T(8,128)(2,1)}, bf16[1,1,1,128,1152]{4,3,2,1,0:T(8,128)(2,1)S(1)}, u32[]{:S(2)}) copy-start(bf16[1,1,1,128,1152]{4,3,2,1,0:T(8,128)(2,1)S(1)} %pad_maximum_fusion.refs_0_) | copy-start | bytes 884740
  3.3 28.7 %collective-permute-start = (bf16[1,1,1,128,1152]{4,3,2,1,0:T(8,128)(2,1)S(1)}, bf16[1,1,1,128,1152]{4,3,2,1,0:T(8,128)(2,1)S(1)}, u32[]{:S(2)}, u32[]{:S(2)}) collective-permute-start(bf16[1,1,1,128,1152]{4,3,2,1,0:T(8,128)(2,1)S(1)} %pad_maximum_fusion.refs_0_), channel_id=1, source_target_pairs={{0,8},{1,9},{2,10},{3,11},{4,12},{5,13},{6,14},{7,15},{8,0},{9,1},... | collective-permute-start | bytes 884744 | tf_op jit(solution)/shard_map/ppermute | solution.py:16
  7.4 24.6 %collective-permute-start.1 = (bf16[1,1,1,128,1024]{4,3,2,1,0:T(8,128)(2,1)S(1)}, bf16[1,1,1,128,1024]{4,3,2,1,0:T(8,128)(2,1)S(1)}, u32[]{:S(2)}, u32[]{:S(2)}) collective-permute-start(bf16[1,1,1,128,1024]{4,3,2,1,0:T(8,128)(2,1)S(1)} %get-tuple-element.91.refs_2_), channel_id=1, source_target_pairs={{0,8},{1,9},{2,10},{3,11},{4,12},{5,13},{6,14},{7,15},{8,0},{9,1},... | collective-permute-start | bytes 786440 | tf_op jit(solution)/shard_map/ppermute | solution.py:16
  32.0 0.7 copy-start.18
  32.7 0.7 copy-start.17
  35.4 14.8 %collective-permute-start.2 = (bf16[2,1,1,128,1152]{4,3,2,1,0:T(8,128)(2,1)}, bf16[2,1,1,128,1152]{4,3,2,1,0:T(8,128)(2,1)S(1)}, u32[]{:S(2)}, u32[]{:S(2)}) collective-permute-start(bf16[2,1,1,128,1152]{4,3,2,1,0:T(8,128)(2,1)} %get-tuple-element.46.refs_0_), channel_id=1, source_target_pairs={{0,4},{1,5},{2,6},{3,7},{4,0},{5,1},{6,2},{7,3},{8,12},{9,13},{10,... | collective-permute-start | bytes 1769480 | tf_op jit(solution)/shard_map/ppermute | solution.py:16
  36.2 13.8 %collective-permute-start.3 = (bf16[2,1,1,128,1024]{4,3,2,1,0:T(8,128)(2,1)}, bf16[2,1,1,128,1024]{4,3,2,1,0:T(8,128)(2,1)S(1)}, u32[]{:S(2)}, u32[]{:S(2)}) collective-permute-start(bf16[2,1,1,128,1024]{4,3,2,1,0:T(8,128)(2,1)} %get-tuple-element.47.refs_2_), channel_id=1, source_target_pairs={{0,2},{1,3},{2,0},{3,1},{4,6},{5,7},{6,4},{7,5},{8,10},{9,11},{10,... | collective-permute-start | bytes 1572872 | tf_op jit(solution)/shard_map/ppermute | solution.py:16
  50.0 0.8 copy-start.16
  50.8 0.8 copy-start.15
  54.1 27.0 %collective-permute-start.4 = (bf16[2,2,1,128,1152]{4,3,2,1,0:T(8,128)(2,1)}, bf16[2,2,1,128,1152]{4,3,2,1,0:T(8,128)(2,1)S(1)}, u32[]{:S(2)}, u32[]{:S(2)}) collective-permute-start(bf16[2,2,1,128,1152]{4,3,2,1,0:T(8,128)(2,1)} %get-tuple-element.48.refs_0_), channel_id=1, source_target_pairs={{0,2},{1,3},{2,0},{3,1},{4,6},{5,7},{6,4},{7,5},{8,10},{9,11},{10,... | collective-permute-start | bytes 3538952 | tf_op jit(solution)/shard_map/ppermute | solution.py:16
  55.7 23.9 %collective-permute-start.5 = (bf16[2,1,2,128,1024]{4,3,2,1,0:T(8,128)(2,1)}, bf16[2,1,2,128,1024]{4,3,2,1,0:T(8,128)(2,1)}, u32[]{:S(2)}, u32[]{:S(2)}) collective-permute-start(bf16[2,1,2,128,1024]{4,3,2,1,0:T(8,128)(2,1)} %get-tuple-element.49.refs_2_), channel_id=1, source_target_pairs={{0,4},{1,5},{2,6},{3,7},{4,0},{5,1},{6,2},{7,3},{8,12},{9,13},{10,... | collective-permute-start | bytes 3145736 | tf_op jit(solution)/shard_map/ppermute | solution.py:16
  81.1 1.0 copy-start.8
  85.6 7.4 %collective-permute-start.6 = (bf16[8,128,1152]{2,1,0:T(8,128)(2,1)}, bf16[8,128,1152]{2,1,0:T(8,128)(2,1)S(1)}, u32[]{:S(2)}, u32[]{:S(2)}) collective-permute-start(bf16[8,128,1152]{2,1,0:T(8,128)(2,1)} %bitcast.43), channel_id=1, source_target_pairs={{0,1},{1,0},{2,3},{3,2},{4,5},{5,4},{6,7},{7,6},{8,9},{9,8},{10,11... | collective-permute-start | bytes 7077896 | tf_op jit(solution)/shard_map/ppermute | solution.py:16
  85.6 11.1 %collective-permute-start.7 = (bf16[8,128,1024]{2,1,0:T(8,128)(2,1)}, bf16[8,128,1024]{2,1,0:T(8,128)(2,1)}, u32[]{:S(2)}, u32[]{:S(2)}) collective-permute-start(bf16[8,128,1024]{2,1,0:T(8,128)(2,1)} %bitcast.51), channel_id=1, source_target_pairs={{0,1},{1,0},{2,3},{3,2},{4,5},{5,4},{6,7},{7,6},{8,9},{9,8},{10,11... | collective-permute-start | bytes 6291464 | tf_op jit(solution)/shard_map/ppermute | solution.py:16
  86.1 27.1 %collective-permute-start.8 = (bf16[1,1,1,128,2048]{4,3,2,1,0:T(8,128)(2,1)}, bf16[1,1,1,128,2048]{4,3,2,1,0:T(8,128)(2,1)}, u32[]{:S(2)}, u32[]{:S(2)}) collective-permute-start(bf16[1,1,1,128,2048]{4,3,2,1,0:T(8,128)(2,1)} %bitcast.12.refs_0_), channel_id=1, source_target_pairs={{0,8},{1,9},{2,10},{3,11},{4,12},{5,13},{6,14},{7,15},{8,0},{9,1},... | collective-permute-start | bytes 1572872 | tf_op jit(solution)/shard_map/ppermute | solution.py:16
  89.5 6.5 %copy-start.21 = (s32[16]{0:T(128)}, s32[16]{0:T(128)S(1)}, u32[]{:S(2)}) copy-start(s32[16]{0:T(128)S(1)} %fusion.7) | copy-start | bytes 196
  93.0 1.5 copy-start.1
  94.4 1.2 copy-start.2
  106.3 45.1 %collective-permute-start.9 = (bf16[2,640,768]{2,1,0:T(8,128)(2,1)}, bf16[2,640,768]{2,1,0:T(8,128)(2,1)S(1)}, u32[]{:S(2)}, u32[]{:S(2)}) collective-permute-start(bf16[2,640,768]{2,1,0:T(8,128)(2,1)} %shard_map.122.refs_2_), channel_id=1, source_target_pairs={{0,16},{16,0},{1,17},{17,1},{2,18},{18,2},{3,19},{19,3},{4,20},{20... | collective-permute-start | bytes 5898248 | tf_op jit(solution)/shard_map/ppermute | solution.py:16
  115.2 13.8 %collective-permute-start.11 = (bf16[2,1,1,128,1024]{4,3,2,1,0:T(8,128)(2,1)}, bf16[2,1,1,128,1024]{4,3,2,1,0:T(8,128)(2,1)}, u32[]{:S(2)}, u32[]{:S(2)}) collective-permute-start(bf16[2,1,1,128,1024]{4,3,2,1,0:T(8,128)(2,1)} %get-tuple-element.52.refs_8_.refs_0_), channel_id=1, source_target_pairs={{0,4},{1,5},{2,6},{3,7},{4,0},{5,1},{6,2},{7,3},{8,12},{9,13},{10,... | collective-permute-start | bytes 1572872 | tf_op jit(solution)/shard_map/ppermute | solution.py:16
  115.8 13.6 %collective-permute-start.12 = (bf16[2,1,1,128,1024]{4,3,2,1,0:T(8,128)(2,1)}, bf16[2,1,1,128,1024]{4,3,2,1,0:T(8,128)(2,1)}, u32[]{:S(2)}, u32[]{:S(2)}) collective-permute-start(bf16[2,1,1,128,1024]{4,3,2,1,0:T(8,128)(2,1)} %get-tuple-element.53.refs_2_), channel_id=1, source_target_pairs={{0,2},{1,3},{2,0},{3,1},{4,6},{5,7},{6,4},{7,5},{8,10},{9,11},{10,... | collective-permute-start | bytes 1572872 | tf_op jit(solution)/shard_map/ppermute | solution.py:16
  131.8 25.7 %collective-permute-start.13 = (bf16[2,2,1,128,1024]{4,3,2,1,0:T(8,128)(2,1)}, bf16[2,2,1,128,1024]{4,3,2,1,0:T(8,128)(2,1)}, u32[]{:S(2)}, u32[]{:S(2)}) collective-permute-start(bf16[2,2,1,128,1024]{4,3,2,1,0:T(8,128)(2,1)} %get-tuple-element.54.refs_0_), channel_id=1, source_target_pairs={{0,2},{1,3},{2,0},{3,1},{4,6},{5,7},{6,4},{7,5},{8,10},{9,11},{10,... | collective-permute-start | bytes 3145736 | tf_op jit(solution)/shard_map/ppermute | solution.py:16
  133.4 24.1 %collective-permute-start.14 = (bf16[2,1,2,128,1024]{4,3,2,1,0:T(8,128)(2,1)}, bf16[2,1,2,128,1024]{4,3,2,1,0:T(8,128)(2,1)}, u32[]{:S(2)}, u32[]{:S(2)}) collective-permute-start(bf16[2,1,2,128,1024]{4,3,2,1,0:T(8,128)(2,1)} %get-tuple-element.55.refs_2_), channel_id=1, source_target_pairs={{0,4},{1,5},{2,6},{3,7},{4,0},{5,1},{6,2},{7,3},{8,12},{9,13},{10,... | collective-permute-start | bytes 3145736 | tf_op jit(solution)/shard_map/ppermute | solution.py:16
  151.4 1.3 copy-start.5
  157.5 4.0 copy-start.4
  160.9 5.5 %collective-permute-start.15 = (bf16[8,128,1024]{2,1,0:T(8,128)(2,1)}, bf16[8,128,1024]{2,1,0:T(8,128)(2,1)}, u32[]{:S(2)}, u32[]{:S(2)}) collective-permute-start(bf16[8,128,1024]{2,1,0:T(8,128)(2,1)} %bitcast.67), channel_id=1, source_target_pairs={{0,1},{1,0},{2,3},{3,2},{4,5},{5,4},{6,7},{7,6},{8,9},{9,8},{10,11... | collective-permute-start | bytes 6291464 | tf_op jit(solution)/shard_map/ppermute | solution.py:16
  161.0 7.5 %collective-permute-start.16 = (bf16[8,128,1024]{2,1,0:T(8,128)(2,1)}, bf16[8,128,1024]{2,1,0:T(8,128)(2,1)}, u32[]{:S(2)}, u32[]{:S(2)}) collective-permute-start(bf16[8,128,1024]{2,1,0:T(8,128)(2,1)} %bitcast.71), channel_id=1, source_target_pairs={{0,1},{1,0},{2,3},{3,2},{4,5},{5,4},{6,7},{7,6},{8,9},{9,8},{10,11... | collective-permute-start | bytes 6291464 | tf_op jit(solution)/shard_map/ppermute | solution.py:16
  161.5 24.6 %collective-permute-start.10 = (bf16[640,768]{1,0:T(8,128)(2,1)S(1)}, bf16[640,768]{1,0:T(8,128)(2,1)S(1)}, u32[]{:S(2)}, u32[]{:S(2)}) collective-permute-start(bf16[640,768]{1,0:T(8,128)(2,1)S(1)} %copy-done.4), channel_id=1, source_target_pairs={{0,16},{16,0},{1,17},{17,1},{2,18},{18,2},{3,19},{19,3},{4,20},{20... | collective-permute-start | bytes 2949128 | tf_op jit(solution)/shard_map/ppermute | solution.py:16
  162.9 46.3 %collective-permute-start.24 = (bf16[640,768]{1,0:T(8,128)(2,1)S(1)}, bf16[640,768]{1,0:T(8,128)(2,1)}, u32[]{:S(2)}, u32[]{:S(2)}) collective-permute-start(bf16[640,768]{1,0:T(8,128)(2,1)S(1)} %copy-done.4), channel_id=1, source_target_pairs={{0,8},{1,9},{2,10},{3,11},{4,12},{5,13},{6,14},{7,15},{8,0},{9,1},... | collective-permute-start | bytes 2949128 | tf_op jit(solution)/shard_map/ppermute | solution.py:16
  168.4 8.8 %copy-start.19 = (s32[16,128]{1,0:T(8,128)S(1)}, s32[16,128]{1,0:T(8,128)}, u32[]{:S(2)}) copy-start(s32[16,128]{1,0:T(8,128)} %get-tuple-element.96.refs_1_) | copy-start | bytes 24580
  175.7 33.5 %collective-permute-start.23 = (bf16[1,640,768]{2,1,0:T(8,128)(2,1)}, bf16[1,640,768]{2,1,0:T(8,128)(2,1)}, u32[]{:S(2)}, u32[]{:S(2)}) collective-permute-start(bf16[1,640,768]{2,1,0:T(8,128)(2,1)} %shard_map.129.refs_6_), channel_id=1, source_target_pairs={{0,16},{16,0},{1,17},{17,1},{2,18},{18,2},{3,19},{19,3},{4,20},{20... | collective-permute-start | bytes 2949128 | tf_op jit(solution)/shard_map/ppermute | solution.py:16
  186.1 0.9 copy-start.6
  200.3 15.8 %collective-permute-start.17 = (bf16[1024,512]{1,0:T(8,128)(2,1)}, bf16[1024,512]{1,0:T(8,128)(2,1)S(1)}, u32[]{:S(2)}, u32[]{:S(2)}) collective-permute-start(bf16[1024,512]{1,0:T(8,128)(2,1)} %get-tuple-element.59.refs_5_), channel_id=1, source_target_pairs={{0,1},{1,0},{2,3},{3,2},{4,5},{5,4},{6,7},{7,6},{8,9},{9,8},{10,11... | collective-permute-start | bytes 3145736 | tf_op jit(solution)/shard_map/ppermute | solution.py:16
  200.3 15.8 %collective-permute-start.18 = (bf16[1024,512]{1,0:T(8,128)(2,1)}, bf16[1024,512]{1,0:T(8,128)(2,1)}, u32[]{:S(2)}, u32[]{:S(2)}) collective-permute-start(bf16[1024,512]{1,0:T(8,128)(2,1)} %get-tuple-element.60), channel_id=1, source_target_pairs={{0,1},{1,0},{2,3},{3,2},{4,5},{5,4},{6,7},{7,6},{8,9},{9,8},{10,11... | collective-permute-start | bytes 3145736 | tf_op jit(solution)/shard_map/ppermute | solution.py:16
  200.8 15.3 %collective-permute-start.19 = (bf16[1024,512]{1,0:T(8,128)(2,1)}, bf16[1024,512]{1,0:T(8,128)(2,1)}, u32[]{:S(2)}, u32[]{:S(2)}) collective-permute-start(bf16[1024,512]{1,0:T(8,128)(2,1)} %get-tuple-element.61), channel_id=1, source_target_pairs={{0,1},{1,0},{2,3},{3,2},{4,5},{5,4},{6,7},{7,6},{8,9},{9,8},{10,11... | collective-permute-start | bytes 3145736 | tf_op jit(solution)/shard_map/ppermute | solution.py:16
  209.2 6.9 %collective-permute-start.20 = (bf16[1024,512]{1,0:T(8,128)(2,1)}, bf16[1024,512]{1,0:T(8,128)(2,1)}, u32[]{:S(2)}, u32[]{:S(2)}) collective-permute-start(bf16[1024,512]{1,0:T(8,128)(2,1)} %get-tuple-element.62), channel_id=1, source_target_pairs={{0,1},{1,0},{2,3},{3,2},{4,5},{5,4},{6,7},{7,6},{8,9},{9,8},{10,11... | collective-permute-start | bytes 3145736 | tf_op jit(solution)/shard_map/ppermute | solution.py:16
  215.5 45.5 %collective-permute-start.25 = (bf16[2,640,768]{2,1,0:T(8,128)(2,1)}, bf16[2,640,768]{2,1,0:T(8,128)(2,1)}, u32[]{:S(2)}, u32[]{:S(2)}) collective-permute-start(bf16[2,640,768]{2,1,0:T(8,128)(2,1)} %shard_map.132.refs_2_.refs_4_.refs_3_), channel_id=1, source_target_pairs={{0,16},{16,0},{1,17},{17,1},{2,18},{18,2},{3,19},{19,3},{4,20},{20... | collective-permute-start | bytes 5898248 | tf_op jit(solution)/shard_map/ppermute | solution.py:16
  216.1 1.0 copy-start.11
  217.0 10.0 %copy-start = (bf16[2,640,768]{2,1,0:T(8,128)(2,1)S(1)}, bf16[2,640,768]{2,1,0:T(8,128)(2,1)}, u32[]{:S(2)}) copy-start(bf16[2,640,768]{2,1,0:T(8,128)(2,1)} %shard_map.132.refs_2_.refs_4_.refs_3_) | copy-start | bytes 5898244
  225.1 57.4 %collective-permute-start.21 = (bf16[2,2,128,1024]{3,2,1,0:T(8,128)(2,1)}, bf16[2,2,128,1024]{3,2,1,0:T(8,128)(2,1)}, u32[]{:S(2)}, u32[]{:S(2)}) collective-permute-start(bf16[2,2,128,1024]{3,2,1,0:T(8,128)(2,1)} %get-tuple-element.64.refs_8_), channel_id=1, source_target_pairs={{0,2},{1,3},{2,0},{3,1},{4,6},{5,7},{6,4},{7,5},{8,10},{9,11},{10,... | collective-permute-start | bytes 3145736 | tf_op jit(solution)/shard_map/ppermute | solution.py:16
  226.7 55.9 %collective-permute-start.22 = (bf16[2,2,128,1024]{3,2,1,0:T(8,128)(2,1)}, bf16[2,2,128,1024]{3,2,1,0:T(8,128)(2,1)}, u32[]{:S(2)}, u32[]{:S(2)}) collective-permute-start(bf16[2,2,128,1024]{3,2,1,0:T(8,128)(2,1)} %get-tuple-element.66), channel_id=1, source_target_pairs={{0,4},{1,5},{2,6},{3,7},{4,0},{5,1},{6,2},{7,3},{8,12},{9,13},{10,... | collective-permute-start | bytes 3145736 | tf_op jit(solution)/shard_map/ppermute | solution.py:16
  227.1 88.5 %collective-permute-start.31 = (bf16[2,640,768]{2,1,0:T(8,128)(2,1)S(1)}, bf16[2,640,768]{2,1,0:T(8,128)(2,1)}, u32[]{:S(2)}, u32[]{:S(2)}) collective-permute-start(bf16[2,640,768]{2,1,0:T(8,128)(2,1)S(1)} %copy-done), channel_id=1, source_target_pairs={{0,8},{1,9},{2,10},{3,11},{4,12},{5,13},{6,14},{7,15},{8,0},{9,1},... | collective-permute-start | bytes 5898248 | tf_op jit(solution)/shard_map/ppermute | solution.py:16
  282.6 11.1 %collective-permute-start.28 = (bf16[1024,768]{1,0:T(8,128)(2,1)}, bf16[1024,768]{1,0:T(8,128)(2,1)}, u32[]{:S(2)}, u32[]{:S(2)}) collective-permute-start(bf16[1024,768]{1,0:T(8,128)(2,1)} %get-tuple-element.72), channel_id=1, source_target_pairs={{0,1},{1,0},{2,3},{3,2},{4,5},{5,4},{6,7},{7,6},{8,9},{9,8},{10,11... | collective-permute-start | bytes 4718600 | tf_op jit(solution)/shard_map/ppermute | solution.py:16
  286.9 1.2 copy-start.20
  286.9 6.7 %collective-permute-start.29 = (bf16[1024,768]{1,0:T(8,128)(2,1)}, bf16[1024,768]{1,0:T(8,128)(2,1)}, u32[]{:S(2)}, u32[]{:S(2)}) collective-permute-start(bf16[1024,768]{1,0:T(8,128)(2,1)} %shard_map.135), channel_id=1, source_target_pairs={{0,1},{1,0},{2,3},{3,2},{4,5},{5,4},{6,7},{7,6},{8,9},{9,8},{10,11... | collective-permute-start | bytes 4718600 | tf_op jit(solution)/shard_map/ppermute | solution.py:16
  288.1 4.0 collective-permute-start.30
  288.6 34.8 %collective-permute-start.26 = (bf16[2,128,1024]{2,1,0:T(8,128)(2,1)}, bf16[2,128,1024]{2,1,0:T(8,128)(2,1)}, u32[]{:S(2)}, u32[]{:S(2)}) collective-permute-start(bf16[2,128,1024]{2,1,0:T(8,128)(2,1)} %get-tuple-element.69.refs_1_), channel_id=1, source_target_pairs={{0,4},{1,5},{2,6},{3,7},{4,0},{5,1},{6,2},{7,3},{8,12},{9,13},{10,... | collective-permute-start | bytes 1572872 | tf_op jit(solution)/shard_map/ppermute | solution.py:16
  292.1 31.3 %collective-permute-start.27 = (bf16[2,128,1024]{2,1,0:T(8,128)(2,1)}, bf16[2,128,1024]{2,1,0:T(8,128)(2,1)}, u32[]{:S(2)}, u32[]{:S(2)}) collective-permute-start(bf16[2,128,1024]{2,1,0:T(8,128)(2,1)} %get-tuple-element.71), channel_id=1, source_target_pairs={{0,2},{1,3},{2,0},{3,1},{4,6},{5,7},{6,4},{7,5},{8,10},{9,11},{10,... | collective-permute-start | bytes 1572872 | tf_op jit(solution)/shard_map/ppermute | solution.py:16
  301.4 57.2 %collective-permute-start.34 = (bf16[2,2,128,1024]{3,2,1,0:T(8,128)(2,1)}, bf16[2,2,128,1024]{3,2,1,0:T(8,128)(2,1)}, u32[]{:S(2)}, u32[]{:S(2)}) collective-permute-start(bf16[2,2,128,1024]{3,2,1,0:T(8,128)(2,1)} %get-tuple-element.79), channel_id=1, source_target_pairs={{0,2},{1,3},{2,0},{3,1},{4,6},{5,7},{6,4},{7,5},{8,10},{9,11},{10,... | collective-permute-start | bytes 3145736 | tf_op jit(solution)/shard_map/ppermute | solution.py:16
  315.6 43.1 %collective-permute-start.35 = (bf16[2,2,128,1024]{3,2,1,0:T(8,128)(2,1)}, bf16[2,2,128,1024]{3,2,1,0:T(8,128)(2,1)S(1)}, u32[]{:S(2)}, u32[]{:S(2)}) collective-permute-start(bf16[2,2,128,1024]{3,2,1,0:T(8,128)(2,1)} %shard_map.137.refs_4_.refs_11_), channel_id=1, source_target_pairs={{0,4},{1,5},{2,6},{3,7},{4,0},{5,1},{6,2},{7,3},{8,12},{9,13},{10,... | collective-permute-start | bytes 3145736 | tf_op jit(solution)/shard_map/ppermute | solution.py:16
  315.6 24.9 %collective-permute-start.33 = (bf16[640,768]{1,0:T(8,128)(2,1)}, bf16[640,768]{1,0:T(8,128)(2,1)S(1)}, u32[]{:S(2)}, u32[]{:S(2)}) collective-permute-start(bf16[640,768]{1,0:T(8,128)(2,1)} %collective-permute-done.24.refs_6_.refs_5_), channel_id=1, source_target_pairs={{0,16},{16,0},{1,17},{17,1},{2,18},{18,2},{3,19},{19,3},{4,20},{20... | collective-permute-start | bytes 2949128 | tf_op jit(solution)/shard_map/ppermute | solution.py:16
  327.0 7.3 %copy-start.3 = (f32[8,2,128,128]{3,2,1,0:T(8,128)S(1)}, f32[8,2,128,128]{3,2,1,0:T(8,128)}, u32[]{:S(2)}) copy-start(f32[8,2,128,128]{3,2,1,0:T(8,128)} %copy-done.2) | copy-start | bytes 3145732
  327.0 7.6 %copy-start.22 = (s32[16]{0:T(128)S(1)}, s32[16]{0:T(128)}, u32[]{:S(2)}) copy-start(s32[16]{0:T(128)} %copy-done.21) | copy-start | bytes 196
  327.1 29.5 %collective-permute-start.32 = (bf16[128,2048]{1,0:T(8,128)(2,1)}, bf16[128,2048]{1,0:T(8,128)(2,1)}, u32[]{:S(2)}, u32[]{:S(2)}) collective-permute-start(bf16[128,2048]{1,0:T(8,128)(2,1)} %get-tuple-element.77), channel_id=1, source_target_pairs={{0,8},{1,9},{2,10},{3,11},{4,12},{5,13},{6,14},{7,15},{8,0},{9,1},... | collective-permute-start | bytes 1572872 | tf_op jit(solution)/shard_map/ppermute | solution.py:16
  332.9 35.0 %collective-permute-start.38 = (bf16[640,768]{1,0:T(8,128)(2,1)}, bf16[640,768]{1,0:T(8,128)(2,1)}, u32[]{:S(2)}, u32[]{:S(2)}) collective-permute-start(bf16[640,768]{1,0:T(8,128)(2,1)} %get-tuple-element.90), channel_id=1, source_target_pairs={{0,16},{16,0},{1,17},{17,1},{2,18},{18,2},{3,19},{19,3},{4,20},{20... | collective-permute-start | bytes 2949128 | tf_op jit(solution)/shard_map/ppermute | solution.py:16
  340.5 0.9 copy-start.12
  358.6 1.0 copy-start.10
  359.6 6.9 %copy-start.13 = (bf16[640,768]{1,0:T(8,128)(2,1)S(1)}, bf16[640,768]{1,0:T(8,128)(2,1)}, u32[]{:S(2)}) copy-start(bf16[640,768]{1,0:T(8,128)(2,1)} %get-tuple-element.89) | copy-start | bytes 2949124
  363.9 19.0 %collective-permute-start.36 = (bf16[2,128,1024]{2,1,0:T(8,128)(2,1)}, bf16[2,128,1024]{2,1,0:T(8,128)(2,1)}, u32[]{:S(2)}, u32[]{:S(2)}) collective-permute-start(bf16[2,128,1024]{2,1,0:T(8,128)(2,1)} %get-tuple-element.82.refs_11_), channel_id=1, source_target_pairs={{0,4},{1,5},{2,6},{3,7},{4,0},{5,1},{6,2},{7,3},{8,12},{9,13},{10,... | collective-permute-start | bytes 1572872 | tf_op jit(solution)/shard_map/ppermute | solution.py:16
  366.0 17.0 %collective-permute-start.37 = (bf16[2,128,1024]{2,1,0:T(8,128)(2,1)}, bf16[2,128,1024]{2,1,0:T(8,128)(2,1)}, u32[]{:S(2)}, u32[]{:S(2)}) collective-permute-start(bf16[2,128,1024]{2,1,0:T(8,128)(2,1)} %get-tuple-element.84), channel_id=1, source_target_pairs={{0,2},{1,3},{2,0},{3,1},{4,6},{5,7},{6,4},{7,5},{8,10},{9,11},{10,... | collective-permute-start | bytes 1572872 | tf_op jit(solution)/shard_map/ppermute | solution.py:16
  366.5 21.2 %collective-permute-start.40 = (bf16[640,768]{1,0:T(8,128)(2,1)S(1)}, bf16[640,768]{1,0:T(8,128)(2,1)S(1)}, u32[]{:S(2)}, u32[]{:S(2)}) collective-permute-start(bf16[640,768]{1,0:T(8,128)(2,1)S(1)} %copy-done.13), channel_id=1, source_target_pairs={{0,16},{16,0},{1,17},{17,1},{2,18},{18,2},{3,19},{19,3},{4,20},{20... | collective-permute-start | bytes 2949128 | tf_op jit(solution)/shard_map/ppermute | solution.py:16
  386.6 23.1 %collective-permute-start.39 = (bf16[128,2048]{1,0:T(8,128)(2,1)}, bf16[128,2048]{1,0:T(8,128)(2,1)}, u32[]{:S(2)}, u32[]{:S(2)}) collective-permute-start(bf16[128,2048]{1,0:T(8,128)(2,1)} %get-tuple-element.86.refs_11_), channel_id=1, source_target_pairs={{0,8},{1,9},{2,10},{3,11},{4,12},{5,13},{6,14},{7,15},{8,0},{9,1},... | collective-permute-start | bytes 1572872 | tf_op jit(solution)/shard_map/ppermute | solution.py:16
  387.7 1.0 copy-start.14

commit v4 on v3

--- a/solution.py
+++ b/solution.py
@@ -488,7 +488,7 @@
 def split_kernel(axes, merge, *refs):
     count = len(axes)
     for i, axis in enumerate(axes):
-        total = (refs[2 * i][...].astype(F32) + refs[2 * i + 1][...].astype(F32)).astype(BF)
+        total = refs[2 * i][...] + refs[2 * i + 1][...]
         width = total.shape[-1]
         for side in range(2):
             part = total[(slice(None),) * axis + (side,)]
@@ -500,7 +500,7 @@
 
 def sum_split(kept, coming, axes, merge, deps=()):
     tokens = kept[0].shape[-2]
-    chunk = min(32, tokens)
+    chunk = min(64, tokens)
     in_specs, out_specs, out_shape, operands = [], [], [], []
     for k, c, axis in zip(kept, coming, axes):
         lead, width = k.shape[:-2], k.shape[-1]
@@ -537,8 +537,7 @@
     at, width = 0, min(256, each)
     for piece in pieces:
         for first in range(0, piece.shape[-1], width):
-            total = keep[..., at : at + width].astype(F32)
-            total = (total + piece[..., first : first + width].astype(F32)).astype(BF)
+            total = keep[..., at : at + width] + piece[..., first : first + width]
             right, place = divmod(at, each)
             for side in range(2):
                 outs[side + 2 * right][..., place : place + width] = (
@@ -549,7 +548,7 @@
 
 def sum_first(keep, coming, mixed, deps=()):
     lead, (tokens, width) = keep.shape[:-2], keep.shape[-2:]
-    chunk = min(16, tokens)
+    chunk = min(32, tokens)
     four = lambda j: (0, 0, j, 0)
     five = lambda j: (0, 0, 0, j, 0)
     outs = 4
@@ -571,9 +570,7 @@
 def last_kernel(*refs):
     width = refs[0].shape[1]
     for i in range(len(refs) // 2):
-        refs[-1][:, i * width : (i + 1) * width] = (
-            refs[2 * i][...].astype(F32) + refs[2 * i + 1][...].astype(F32)
-        ).astype(BF)
+        refs[-1][:, i * width : (i + 1) * width] = refs[2 * i][...] + refs[2 * i + 1][...]
 
 
 def last_sum(kept, coming, deps=()):
@@ -661,7 +658,7 @@
 
 def by_rows(kernel, operands, stacks, outs, deps=()):
     rows, hidden = operands[0].shape[1:]
-    chunk = rows // 5 if rows % 80 == 0 else rows
+    chunk = rows // 2 if rows % 32 == 0 else rows
     return call(
         kernel,
         (rows // chunk,),
@@ -839,7 +836,7 @@
     out_parts = next_sum(out_parts, out_bits[0], 1, back_keep)
     back_send[1] = after(back_send[1], out_parts[1])
     back_parts = list(first_sum(back_keep, back_send, MIXED))
-    back_parts[3] = after(back_parts[3], slopes_crossed)
+    back_parts[3] = after(back_parts[3], slopes_crossed, hid_beyond)
     slopes_beyond = [over(slopes_crossed[part]) for part in range(2)]
 
     def slope_values(part):
@@ -848,7 +845,7 @@
 
     out_parts = next_sum(out_parts, out_bits[1], 0, back_parts[3])
     grad_down = gradient(
-        [hid, hid_other, hid_crossed, hid_beyond], cot_pieces, False, back_parts[3]
+        [hid, hid_other, hid_crossed, hid_beyond], cot_pieces, False, out_parts[1]
     )
     output = end_sum(out_parts, grad_down)
     back_parts = next_sum(back_parts, back_bits[0], 1, output)

time: 413 us -> 408 us (0.988)
  Pallas kernels: 176 us -> 164 us
  waiting for transfers between devices: 163 us -> 175 us
  starting transfers between devices: 46.6 us -> 42.2 us
    ppermute x41, waiting for transfers between devices: 163 us -> 175 us  [exchange(): return lax.ppermute(value, axis, pairs)]
    pallas_call x25, Pallas kernels: 176 us -> 164 us  [call(): return lambda *operands: run(*operands, *deps)]
    ppermute x41, starting transfers between devices: 46.6 us -> 42.2 us  [exchange(): return lax.ppermute(value, axis, pairs)]
    unnamed x46 -> x42, local copies, waits for them, and re-layouts: 11.8 us -> 10.8 us
  transfers between devices with their start and end apart: 41 -> 41, of which waited for: 19 -> 23; matrix products, arithmetic and copies ran while one was open for 3% -> 3% of each run, Pallas kernels for 39% -> 37%
where the time goes in v4:
time: 408 us; the launch traced here: 407 us
  waiting for transfers between devices  175 us (43%)
  Pallas kernels  164 us (40%)
  starting transfers between devices  42.2 us (10%)
  local copies, waits for them, and re-layouts  19.4 us (5%)
    ppermute x41, waiting for transfers between devices, exchange(): return lax.ppermute(value, axis, pairs)  175 us
    pallas_call x25, Pallas kernels, call(): return lambda *operands: run(*operands, *deps)  164 us
    ppermute x41, starting transfers between devices, exchange(): return lax.ppermute(value, axis, pairs)  42.2 us
    unnamed x42, local copies, waits for them, and re-layouts  10.8 us
  transfers between devices with their start and end apart: 41, of which 23 were waited for; matrix products, arithmetic and copies ran while one was open for 3% of the time, Pallas kernels for 37%

profile of v4, /device:TPU:0, one launch (start us, length us, event | category | flops | bytes accessed | tf_op | source)
XLA Modules:
  0.0 407.5 jit_solution(12033572310245894008)
XLA Ops:
  3.3 4.1 %collective-permute-start = (bf16[1,1,1,128,1152]{4,3,2,1,0:T(8,128)(2,1)S(1)}, bf16[1,1,1,128,1152]{4,3,2,1,0:T(8,128)(2,1)S(1)}, u32[]{:S(2)}, u32[]{:S(2)}) collective-permute-start(bf16[1,1,1,128,1152]{4,3,2,1,0:T(8,128)(2,1)S(1)} %pad_maximum_fusion.refs_0_), channel_id=1, source_target_pairs={{0,8},{1,9},{2,10},{3,11},{4,12},{5,13},{6,14},{7,15},{8,0},{9,1},... | collective-permute-start | bytes 884744 | tf_op jit(solution)/shard_map/ppermute | solution.py:16
  7.5 24.5 %collective-permute-done.1.refs_3_ = bf16[1,1,1,128,1024]{4,3,2,1,0:T(8,128)(2,1)S(1)} collective-permute-done((bf16[1,1,1,128,1024]{4,3,2,1,0:T(8,128)(2,1)S(1)}, bf16[1,1,1,128,1024]{4,3,2,1,0:T(8,128)(2,1)S(1)}, u32[]{:S(2)}, u32[]{:S(2)}) %collective-permute-start.1) | collective-permute-done | bytes 262176 | tf_op jit(solution)/shard_map/ppermute | solution.py:16
  33.4 2.0 shard_map.119
  36.2 1.5 collective-permute-start.3
  37.7 12.3 %collective-permute-done.3.refs_3_ = bf16[2,1,1,128,1024]{4,3,2,1,0:T(8,128)(2,1)S(1)} collective-permute-done((bf16[2,1,1,128,1024]{4,3,2,1,0:T(8,128)(2,1)}, bf16[2,1,1,128,1024]{4,3,2,1,0:T(8,128)(2,1)S(1)}, u32[]{:S(2)}, u32[]{:S(2)}) %collective-permute-start.3) | collective-permute-done | bytes 524320 | tf_op jit(solution)/shard_map/ppermute | solution.py:16
  51.6 2.5 shard_map.120
  54.1 1.6 collective-permute-start.4
  56.6 23.1 %collective-permute-done.5.refs_3_ = bf16[2,1,2,128,1024]{4,3,2,1,0:T(8,128)(2,1)} collective-permute-done((bf16[2,1,2,128,1024]{4,3,2,1,0:T(8,128)(2,1)}, bf16[2,1,2,128,1024]{4,3,2,1,0:T(8,128)(2,1)}, u32[]{:S(2)}, u32[]{:S(2)}) %collective-permute-start.5) | collective-permute-done | bytes 1048608 | tf_op jit(solution)/shard_map/ppermute | solution.py:16
  79.6 1.5 collective-permute-done.4.refs_1_
  82.1 3.4 shard_map.121
  86.1 3.4 collective-permute-start.8
  90.5 2.5 collective-permute-done.6.refs_3_.refs_8_
  93.1 1.3 copy-done.1
  94.4 1.2 fusion.4
  96.7 9.6 %shard_map.122.refs_2_ = bf16[2,640,768]{2,1,0:T(8,128)(2,1)} custom-call(s32[1]{0:T(128)} %bitcast.13.refs_0_, s32[16,128]{1,0:T(8,128)} %get-tuple-element.96.refs_1_, bf16[8,128,1152]{2,1,0:T(8,128)(2,1)} %bitcast.45, bf16[8,128,1152]{2,1,0:T(8,128)(2,1)} %copy-done.1, bf16[8,128,1024]{2,1,0:T(8,128)(2,1)} %bitcast.52, ...), custom_call_target="tpu_custom_call" | custom-call | flops 4026531 | bytes 10485 | tf_op jit(solution)/shard_map/pallas_call | solution.py:257
  106.3 1.5 collective-permute-start.9
  107.8 5.4 %collective-permute-done.8.refs_1_ = bf16[1,1,1,128,2048]{4,3,2,1,0:T(8,128)(2,1)} collective-permute-done((bf16[1,1,1,128,2048]{4,3,2,1,0:T(8,128)(2,1)}, bf16[1,1,1,128,2048]{4,3,2,1,0:T(8,128)(2,1)}, u32[]{:S(2)}, u32[]{:S(2)}) %collective-permute-start.8) | collective-permute-done | bytes 524320 | tf_op jit(solution)/shard_map/ppermute | solution.py:16
  113.2 2.0 shard_map.123
  115.7 1.5 collective-permute-start.12
  117.3 9.4 %shard_map.124.refs_0_.refs_4_ = bf16[2,640,768]{2,1,0:T(8,128)(2,1)} custom-call(s32[1]{0:T(128)} %bitcast.refs_0_, s32[16,128]{1,0:T(8,128)} %get-tuple-element.96.refs_1_, bf16[8,128,1152]{2,1,0:T(8,128)(2,1)} %bitcast.46, bf16[8,128,1152]{2,1,0:T(8,128)(2,1)} %copy-done.1, bf16[8,128,1024]{2,1,0:T(8,128)(2,1)} %bitcast.53, ...), custom_call_target="tpu_custom_call" | custom-call | flops 4026531 | bytes 10485 | tf_op jit(solution)/shard_map/pallas_call | solution.py:257
  126.6 2.3 collective-permute-done.11.refs_1_
  129.4 2.4 shard_map.126
  131.8 1.6 collective-permute-start.13
  133.4 1.3 collective-permute-start.14
  136.0 15.4 %collective-permute-done.9.refs_1_ = bf16[2,640,768]{2,1,0:T(8,128)(2,1)S(1)} collective-permute-done((bf16[2,640,768]{2,1,0:T(8,128)(2,1)}, bf16[2,640,768]{2,1,0:T(8,128)(2,1)S(1)}, u32[]{:S(2)}, u32[]{:S(2)}) %collective-permute-start.9) | collective-permute-done | bytes 1966112 | tf_op jit(solution)/shard_map/ppermute | solution.py:16
  151.4 1.3 copy-done.5
  152.7 3.3 shard_map.125.refs_4_.refs_2_.refs_3_
  157.1 3.3 shard_map.127
  160.9 1.5 collective-permute-start.10
  162.4 3.4 collective-permute-start.24
  165.8 2.1 collective-permute-done.16.refs_5_.refs_10_
  167.9 7.2 %shard_map.129.refs_6_ = bf16[1,640,768]{2,1,0:T(8,128)(2,1)} custom-call(s32[1]{0:T(128)} %bitcast.13.refs_0_, s32[16,128]{1,0:T(8,128)} %get-tuple-element.96.refs_1_, bf16[8,128,1024]{2,1,0:T(8,128)(2,1)} %bitcast.68, bf16[8,128,1024]{2,1,0:T(8,128)(2,1)} %collective-permute-done.15.refs_3_.refs_8_, bf16[8,128,1024]{2,1,0:T(8,128)(2,1)} %bitcast.72, ...), custom_call_target="tpu_custom_call" | custom-call | flops 2013265 | bytes 7340 | tf_op jit(solution)/shard_map/pallas_call | solution.py:257
  175.2 1.5 collective-permute-start.23
  176.7 1.4 copy.61.refs_1_
  178.1 7.3 %shard_map.128.refs_5_.refs_3_ = bf16[1,640,768]{2,1,0:T(8,128)(2,1)} custom-call(s32[1]{0:T(128)} %bitcast.refs_0_, s32[16,128]{1,0:T(8,128)} %get-tuple-element.96.refs_1_, bf16[8,128,1024]{2,1,0:T(8,128)(2,1)} %bitcast.69, bf16[8,128,1024]{2,1,0:T(8,128)(2,1)} %collective-permute-done.15.refs_3_.refs_8_, bf16[8,128,1024]{2,1,0:T(8,128)(2,1)} %bitcast.73, ...), custom_call_target="tpu_custom_call" | custom-call | flops 2013265 | bytes 7340 | tf_op jit(solution)/shard_map/pallas_call | solution.py:257
  186.5 13.3 %shard_map.130 = (bf16[1024,2048]{1,0:T(8,128)(2,1)}, bf16[1024,512]{1,0:T(8,128)(2,1)}, bf16[1024,512]{1,0:T(8,128)(2,1)}, bf16[1024,512]{1,0:T(8,128)(2,1)}, bf16[1024,512]{1,0:T(8,128)(2,1)}) custom-call(s32[1]{0:T(128)} %bitcast.refs_0_, s32[16,128,1]{2,1,0:T(8,128)} %copy.61.refs_1_, bf16[640,768]{1,0:T(8,128)(2,1)} %shard_map.125.refs_4_.refs_2_.refs_3_, ...), custom_call_target="tpu_custom_call" | custom-call | flops 6442450 | bytes 11534 | tf_op jit(solution)/shard_map/pallas_call | solution.py:257
  200.4 8.3 %collective-permute-done.24.refs_6_.refs_5_ = bf16[640,768]{1,0:T(8,128)(2,1)} collective-permute-done((bf16[640,768]{1,0:T(8,128)(2,1)S(1)}, bf16[640,768]{1,0:T(8,128)(2,1)}, u32[]{:S(2)}, u32[]{:S(2)}) %collective-permute-start.24) | collective-permute-done | bytes 983072 | tf_op jit(solution)/shard_map/ppermute | solution.py:16
  208.7 5.8 %shard_map.132.refs_2_.refs_4_.refs_3_ = bf16[2,640,768]{2,1,0:T(8,128)(2,1)} custom-call(bf16[2,640,768]{2,1,0:T(8,128)(2,1)} %shard_map.124.refs_0_.refs_4_, bf16[2,640,768]{2,1,0:T(8,128)(2,1)} %copy-done.5, f32[640,1]{1,0:T(8,128)} %reshape.109.refs_2_, bf16[1,640,768]{2,1,0:T(8,128)(2,1)} %shard_map.128.refs_5_.refs_3_, ...), custom_call_target="tpu_custom_call" | custom-call | tf_op jit(solution)/shard_map/pallas_call | solution.py:257
  216.1 5.8 %shard_map.131 = (bf16[2,2,128,1024]{3,2,1,0:T(8,128)(2,1)}, bf16[2,2,128,1024]{3,2,1,0:T(8,128)(2,1)}, bf16[2,2,128,1024]{3,2,1,0:T(8,128)(2,1)}, bf16[2,2,128,1024]{3,2,1,0:T(8,128)(2,1)}) custom-call(bf16[2,2,2,128,2048]{4,3,2,1,0:T(8,128)(2,1)} %bitcast.77, bf16[2,2,2,128,512]{4,3,2,1,0:T(8,128)(2,1)} %bitcast.78, ...), custom_call_target="tpu_custom_call" | custom-call | tf_op jit(solution)/shard_map/pallas_call | solution.py:257
  222.9 3.5 collective-permute-start.31
  226.3 33.6 %collective-permute-done.25.refs_3_.refs_5_.refs_4_ = bf16[2,640,768]{2,1,0:T(8,128)(2,1)} collective-permute-done((bf16[2,640,768]{2,1,0:T(8,128)(2,1)}, bf16[2,640,768]{2,1,0:T(8,128)(2,1)}, u32[]{:S(2)}, u32[]{:S(2)}) %collective-permute-start.25) | collective-permute-done | bytes 1966112 | tf_op jit(solution)/shard_map/ppermute | solution.py:16
  259.9 21.5 %shard_map.133 = (bf16[1024,2048]{1,0:T(8,128)(2,1)}, bf16[1024,768]{1,0:T(8,128)(2,1)}, bf16[1024,768]{1,0:T(8,128)(2,1)}, bf16[1024,512]{1,0:T(8,128)(2,1)}) custom-call(s32[1]{0:T(128)} %bitcast.refs_0_, s32[16,128,1]{2,1,0:T(8,128)} %copy.61.refs_1_, bf16[2,640,768]{2,1,0:T(8,128)(2,1)} %shard_map.132.refs_2_.refs_4_.refs_3_, ...), custom_call_target="tpu_custom_call" | custom-call | flops 12884901 | bytes 14680 | tf_op jit(solution)/shard_map/pallas_call | solution.py:257
  281.4 3.3 shard_map.134
  286.5 4.8 %collective-permute-done.30 = bf16[1024,512]{1,0:T(8,128)(2,1)} collective-permute-done((bf16[1024,512]{1,0:T(8,128)(2,1)S(1)}, bf16[1024,512]{1,0:T(8,128)(2,1)}, u32[]{:S(2)}, u32[]{:S(2)}) %collective-permute-start.30) | collective-permute-done | bytes 1048608 | tf_op jit(solution)/shard_map/ppermute | solution.py:16
  292.3 5.7 %shard_map.136 = (bf16[2,2,128,1024]{3,2,1,0:T(8,128)(2,1)}, bf16[2,2,128,1024]{3,2,1,0:T(8,128)(2,1)}, bf16[2,2,128,1024]{3,2,1,0:T(8,128)(2,1)}, bf16[2,2,128,1024]{3,2,1,0:T(8,128)(2,1)}) custom-call(bf16[2,2,2,128,2048]{4,3,2,1,0:T(8,128)(2,1)} %bitcast.75, bf16[2,2,2,128,768]{4,3,2,1,0:T(8,128)(2,1)} %bitcast.23.refs_1_, ...), custom_call_target="tpu_custom_call" | custom-call | tf_op jit(solution)/shard_map/pallas_call | solution.py:257
  298.0 12.4 %collective-permute-done.32.refs_2_.refs_6_ = bf16[640,768]{1,0:T(8,128)(2,1)} collective-permute-done((bf16[640,768]{1,0:T(8,128)(2,1)}, bf16[640,768]{1,0:T(8,128)(2,1)}, u32[]{:S(2)}, u32[]{:S(2)}) %collective-permute-start.32) | collective-permute-done | bytes 983072 | tf_op jit(solution)/shard_map/ppermute | solution.py:16
  312.1 10.3 %collective-permute-done.26.refs_1_ = bf16[2,128,1024]{2,1,0:T(8,128)(2,1)} collective-permute-done((bf16[2,128,1024]{2,1,0:T(8,128)(2,1)}, bf16[2,128,1024]{2,1,0:T(8,128)(2,1)}, u32[]{:S(2)}, u32[]{:S(2)}) %collective-permute-start.26) | collective-permute-done | bytes 524320 | tf_op jit(solution)/shard_map/ppermute | solution.py:16
  322.4 2.4 shard_map.138
  325.3 2.6 slice_bitcast_fusion
  327.8 1.5 collective-permute-start.38
  330.4 1.4 copy.65.refs_2_
  331.9 15.0 %shard_map.139.refs_2_ = f32[768,2048]{1,0:T(8,128)} custom-call(s32[1]{0:T(128)} %bitcast.refs_0_, s32[16,128,1]{2,1,0:T(8,128)} %copy.61.refs_1_, s32[16,128,1]{2,1,0:T(8,128)} %copy.65.refs_2_, bf16[640,768]{1,0:T(8,128)(2,1)} %shard_map.125.refs_4_.refs_2_.refs_3_, bf16[640,768]{1,0:T(8,128)(2,1)} %copy-done.6, ...), custom_call_target="tpu_custom_call" | custom-call | flops 6442450 | bytes 14680 | tf_op jit(solution)/shard_map/pallas_call | solution.py:257
  346.9 4.3 %collective-permute-done.33.refs_1_ = bf16[128,2048]{1,0:T(8,128)(2,1)} collective-permute-done((bf16[128,2048]{1,0:T(8,128)(2,1)}, bf16[128,2048]{1,0:T(8,128)(2,1)}, u32[]{:S(2)}, u32[]{:S(2)}) %collective-permute-start.33) | collective-permute-done | bytes 524320 | tf_op jit(solution)/shard_map/ppermute | solution.py:16
  351.2 2.0 shard_map.140.refs_4_
  353.3 2.6 collective-permute-done.35.refs_3_
  356.9 3.2 shard_map.141
  361.1 1.5 collective-permute-start.40
  362.6 14.7 %shard_map.142.refs_4_ = f32[2048,768]{1,0:T(8,128)} custom-call(s32[1]{0:T(128)} %bitcast.refs_0_, s32[16,128,1]{2,1,0:T(8,128)} %copy.61.refs_1_, s32[16,128,1]{2,1,0:T(8,128)} %copy.65.refs_2_, bf16[2,640,768]{2,1,0:T(8,128)(2,1)} %shard_map.132.refs_2_.refs_4_.refs_3_, bf16[2,640,768]{2,1,0:T(8,128)(2,1)} %collective-permute-done.25.refs_3_.refs_5_.refs_4_, ...), custom_call_target="tpu_custom_call" | custom-call | flops 6442450 | bytes 14680 | tf_op jit(solution)/shard_map/pallas_call | solution.py:257
  377.3 2.4 shard_map.143
  379.7 2.9 collective-permute-start.39
  382.5 2.0 collective-permute-done.40.refs_6_
  385.5 14.6 %shard_map.145 = f32[2048,768]{1,0:T(8,128)} custom-call(s32[1]{0:T(128)} %bitcast.refs_0_, s32[16,128,1]{2,1,0:T(8,128)} %copy.61.refs_1_, s32[16,128,1]{2,1,0:T(8,128)} %copy.65.refs_2_, bf16[2,640,768]{2,1,0:T(8,128)(2,1)} %shard_map.132.refs_2_.refs_4_.refs_3_, bf16[2,640,768]{2,1,0:T(8,128)(2,1)} %collective-permute-done.25.refs_3_.refs_5_.refs_4_, ...), custom_call_target="tpu_custom_call" | custom-call | flops 6442450 | bytes 14680 | tf_op jit(solution)/shard_map/pallas_call | solution.py:257
  400.1 5.3 %collective-permute-done.39.refs_1_ = bf16[128,2048]{1,0:T(8,128)(2,1)} collective-permute-done((bf16[128,2048]{1,0:T(8,128)(2,1)}, bf16[128,2048]{1,0:T(8,128)(2,1)}, u32[]{:S(2)}, u32[]{:S(2)}) %collective-permute-start.39) | collective-permute-done | bytes 524320 | tf_op jit(solution)/shard_map/ppermute | solution.py:16
  405.4 2.0 shard_map.144
  (110 shorter events, 27.5 us)
Async XLA Ops:
  3.2 28.7 %copy-start.9 = (bf16[1,1,1,128,1024]{4,3,2,1,0:T(8,128)(2,1)}, bf16[1,1,1,128,1024]{4,3,2,1,0:T(8,128)(2,1)S(1)}, u32[]{:S(2)}) copy-start(bf16[1,1,1,128,1024]{4,3,2,1,0:T(8,128)(2,1)S(1)} %get-tuple-element.91.refs_2_) | copy-start | bytes 786436
  3.3 28.7 %copy-start.7 = (bf16[1,1,1,128,1152]{4,3,2,1,0:T(8,128)(2,1)}, bf16[1,1,1,128,1152]{4,3,2,1,0:T(8,128)(2,1)S(1)}, u32[]{:S(2)}) copy-start(bf16[1,1,1,128,1152]{4,3,2,1,0:T(8,128)(2,1)S(1)} %pad_maximum_fusion.refs_0_) | copy-start | bytes 884740
  3.3 28.7 %collective-permute-start = (bf16[1,1,1,128,1152]{4,3,2,1,0:T(8,128)(2,1)S(1)}, bf16[1,1,1,128,1152]{4,3,2,1,0:T(8,128)(2,1)S(1)}, u32[]{:S(2)}, u32[]{:S(2)}) collective-permute-start(bf16[1,1,1,128,1152]{4,3,2,1,0:T(8,128)(2,1)S(1)} %pad_maximum_fusion.refs_0_), channel_id=1, source_target_pairs={{0,8},{1,9},{2,10},{3,11},{4,12},{5,13},{6,14},{7,15},{8,0},{9,1},... | collective-permute-start | bytes 884744 | tf_op jit(solution)/shard_map/ppermute | solution.py:16
  7.4 24.6 %collective-permute-start.1 = (bf16[1,1,1,128,1024]{4,3,2,1,0:T(8,128)(2,1)S(1)}, bf16[1,1,1,128,1024]{4,3,2,1,0:T(8,128)(2,1)S(1)}, u32[]{:S(2)}, u32[]{:S(2)}) collective-permute-start(bf16[1,1,1,128,1024]{4,3,2,1,0:T(8,128)(2,1)S(1)} %get-tuple-element.91.refs_2_), channel_id=1, source_target_pairs={{0,8},{1,9},{2,10},{3,11},{4,12},{5,13},{6,14},{7,15},{8,0},{9,1},... | collective-permute-start | bytes 786440 | tf_op jit(solution)/shard_map/ppermute | solution.py:16
  32.0 0.7 copy-start.16
  32.7 0.7 copy-start.15
  35.4 14.8 %collective-permute-start.2 = (bf16[2,1,1,128,1152]{4,3,2,1,0:T(8,128)(2,1)}, bf16[2,1,1,128,1152]{4,3,2,1,0:T(8,128)(2,1)S(1)}, u32[]{:S(2)}, u32[]{:S(2)}) collective-permute-start(bf16[2,1,1,128,1152]{4,3,2,1,0:T(8,128)(2,1)} %get-tuple-element.46.refs_0_), channel_id=1, source_target_pairs={{0,4},{1,5},{2,6},{3,7},{4,0},{5,1},{6,2},{7,3},{8,12},{9,13},{10,... | collective-permute-start | bytes 1769480 | tf_op jit(solution)/shard_map/ppermute | solution.py:16
  36.2 13.8 %collective-permute-start.3 = (bf16[2,1,1,128,1024]{4,3,2,1,0:T(8,128)(2,1)}, bf16[2,1,1,128,1024]{4,3,2,1,0:T(8,128)(2,1)S(1)}, u32[]{:S(2)}, u32[]{:S(2)}) collective-permute-start(bf16[2,1,1,128,1024]{4,3,2,1,0:T(8,128)(2,1)} %get-tuple-element.47.refs_2_), channel_id=1, source_target_pairs={{0,2},{1,3},{2,0},{3,1},{4,6},{5,7},{6,4},{7,5},{8,10},{9,11},{10,... | collective-permute-start | bytes 1572872 | tf_op jit(solution)/shard_map/ppermute | solution.py:16
  49.9 0.8 copy-start.14
  50.7 0.8 copy-start.13
  54.1 27.0 %collective-permute-start.4 = (bf16[2,2,1,128,1152]{4,3,2,1,0:T(8,128)(2,1)}, bf16[2,2,1,128,1152]{4,3,2,1,0:T(8,128)(2,1)S(1)}, u32[]{:S(2)}, u32[]{:S(2)}) collective-permute-start(bf16[2,2,1,128,1152]{4,3,2,1,0:T(8,128)(2,1)} %get-tuple-element.48.refs_0_), channel_id=1, source_target_pairs={{0,2},{1,3},{2,0},{3,1},{4,6},{5,7},{6,4},{7,5},{8,10},{9,11},{10,... | collective-permute-start | bytes 3538952 | tf_op jit(solution)/shard_map/ppermute | solution.py:16
  55.7 23.9 %collective-permute-start.5 = (bf16[2,1,2,128,1024]{4,3,2,1,0:T(8,128)(2,1)}, bf16[2,1,2,128,1024]{4,3,2,1,0:T(8,128)(2,1)}, u32[]{:S(2)}, u32[]{:S(2)}) collective-permute-start(bf16[2,1,2,128,1024]{4,3,2,1,0:T(8,128)(2,1)} %get-tuple-element.49.refs_2_), channel_id=1, source_target_pairs={{0,4},{1,5},{2,6},{3,7},{4,0},{5,1},{6,2},{7,3},{8,12},{9,13},{10,... | collective-permute-start | bytes 3145736 | tf_op jit(solution)/shard_map/ppermute | solution.py:16
  81.1 1.0 copy-start.8
  85.5 7.4 %collective-permute-start.6 = (bf16[8,128,1152]{2,1,0:T(8,128)(2,1)}, bf16[8,128,1152]{2,1,0:T(8,128)(2,1)S(1)}, u32[]{:S(2)}, u32[]{:S(2)}) collective-permute-start(bf16[8,128,1152]{2,1,0:T(8,128)(2,1)} %bitcast.43), channel_id=1, source_target_pairs={{0,1},{1,0},{2,3},{3,2},{4,5},{5,4},{6,7},{7,6},{8,9},{9,8},{10,11... | collective-permute-start | bytes 7077896 | tf_op jit(solution)/shard_map/ppermute | solution.py:16
  85.6 11.1 %collective-permute-start.7 = (bf16[8,128,1024]{2,1,0:T(8,128)(2,1)}, bf16[8,128,1024]{2,1,0:T(8,128)(2,1)}, u32[]{:S(2)}, u32[]{:S(2)}) collective-permute-start(bf16[8,128,1024]{2,1,0:T(8,128)(2,1)} %bitcast.51), channel_id=1, source_target_pairs={{0,1},{1,0},{2,3},{3,2},{4,5},{5,4},{6,7},{7,6},{8,9},{9,8},{10,11... | collective-permute-start | bytes 6291464 | tf_op jit(solution)/shard_map/ppermute | solution.py:16
  86.1 27.1 %collective-permute-start.8 = (bf16[1,1,1,128,2048]{4,3,2,1,0:T(8,128)(2,1)}, bf16[1,1,1,128,2048]{4,3,2,1,0:T(8,128)(2,1)}, u32[]{:S(2)}, u32[]{:S(2)}) collective-permute-start(bf16[1,1,1,128,2048]{4,3,2,1,0:T(8,128)(2,1)} %bitcast.12.refs_0_), channel_id=1, source_target_pairs={{0,8},{1,9},{2,10},{3,11},{4,12},{5,13},{6,14},{7,15},{8,0},{9,1},... | collective-permute-start | bytes 1572872 | tf_op jit(solution)/shard_map/ppermute | solution.py:16
  89.5 6.5 %copy-start.19 = (s32[16]{0:T(128)}, s32[16]{0:T(128)S(1)}, u32[]{:S(2)}) copy-start(s32[16]{0:T(128)S(1)} %fusion.7) | copy-start | bytes 196
  92.9 1.5 copy-start.1
  94.4 1.2 copy-start.2
  106.3 45.1 %collective-permute-start.9 = (bf16[2,640,768]{2,1,0:T(8,128)(2,1)}, bf16[2,640,768]{2,1,0:T(8,128)(2,1)S(1)}, u32[]{:S(2)}, u32[]{:S(2)}) collective-permute-start(bf16[2,640,768]{2,1,0:T(8,128)(2,1)} %shard_map.122.refs_2_), channel_id=1, source_target_pairs={{0,16},{16,0},{1,17},{17,1},{2,18},{18,2},{3,19},{19,3},{4,20},{20... | collective-permute-start | bytes 5898248 | tf_op jit(solution)/shard_map/ppermute | solution.py:16
  115.2 13.8 %collective-permute-start.11 = (bf16[2,1,1,128,1024]{4,3,2,1,0:T(8,128)(2,1)}, bf16[2,1,1,128,1024]{4,3,2,1,0:T(8,128)(2,1)}, u32[]{:S(2)}, u32[]{:S(2)}) collective-permute-start(bf16[2,1,1,128,1024]{4,3,2,1,0:T(8,128)(2,1)} %get-tuple-element.52.refs_8_.refs_0_), channel_id=1, source_target_pairs={{0,4},{1,5},{2,6},{3,7},{4,0},{5,1},{6,2},{7,3},{8,12},{9,13},{10,... | collective-permute-start | bytes 1572872 | tf_op jit(solution)/shard_map/ppermute | solution.py:16
  115.7 13.6 %collective-permute-start.12 = (bf16[2,1,1,128,1024]{4,3,2,1,0:T(8,128)(2,1)}, bf16[2,1,1,128,1024]{4,3,2,1,0:T(8,128)(2,1)}, u32[]{:S(2)}, u32[]{:S(2)}) collective-permute-start(bf16[2,1,1,128,1024]{4,3,2,1,0:T(8,128)(2,1)} %get-tuple-element.53.refs_2_), channel_id=1, source_target_pairs={{0,2},{1,3},{2,0},{3,1},{4,6},{5,7},{6,4},{7,5},{8,10},{9,11},{10,... | collective-permute-start | bytes 1572872 | tf_op jit(solution)/shard_map/ppermute | solution.py:16
  131.8 24.2 %collective-permute-start.13 = (bf16[2,2,1,128,1024]{4,3,2,1,0:T(8,128)(2,1)}, bf16[2,2,1,128,1024]{4,3,2,1,0:T(8,128)(2,1)}, u32[]{:S(2)}, u32[]{:S(2)}) collective-permute-start(bf16[2,2,1,128,1024]{4,3,2,1,0:T(8,128)(2,1)} %get-tuple-element.54.refs_0_), channel_id=1, source_target_pairs={{0,2},{1,3},{2,0},{3,1},{4,6},{5,7},{6,4},{7,5},{8,10},{9,11},{10,... | collective-permute-start | bytes 3145736 | tf_op jit(solution)/shard_map/ppermute | solution.py:16
  133.4 23.7 %collective-permute-start.14 = (bf16[2,1,2,128,1024]{4,3,2,1,0:T(8,128)(2,1)}, bf16[2,1,2,128,1024]{4,3,2,1,0:T(8,128)(2,1)}, u32[]{:S(2)}, u32[]{:S(2)}) collective-permute-start(bf16[2,1,2,128,1024]{4,3,2,1,0:T(8,128)(2,1)} %get-tuple-element.55.refs_2_), channel_id=1, source_target_pairs={{0,4},{1,5},{2,6},{3,7},{4,0},{5,1},{6,2},{7,3},{8,12},{9,13},{10,... | collective-permute-start | bytes 3145736 | tf_op jit(solution)/shard_map/ppermute | solution.py:16
  151.4 1.3 copy-start.5
  156.0 4.9 %copy-start.4 = (bf16[640,768]{1,0:T(8,128)(2,1)S(1)}, bf16[640,768]{1,0:T(8,128)(2,1)}, u32[]{:S(2)}) copy-start(bf16[640,768]{1,0:T(8,128)(2,1)} %shard_map.125.refs_4_.refs_2_.refs_3_) | copy-start | bytes 2949124
  160.4 5.5 %collective-permute-start.15 = (bf16[8,128,1024]{2,1,0:T(8,128)(2,1)}, bf16[8,128,1024]{2,1,0:T(8,128)(2,1)}, u32[]{:S(2)}, u32[]{:S(2)}) collective-permute-start(bf16[8,128,1024]{2,1,0:T(8,128)(2,1)} %bitcast.67), channel_id=1, source_target_pairs={{0,1},{1,0},{2,3},{3,2},{4,5},{5,4},{6,7},{7,6},{8,9},{9,8},{10,11... | collective-permute-start | bytes 6291464 | tf_op jit(solution)/shard_map/ppermute | solution.py:16
  160.4 7.5 %collective-permute-start.16 = (bf16[8,128,1024]{2,1,0:T(8,128)(2,1)}, bf16[8,128,1024]{2,1,0:T(8,128)(2,1)}, u32[]{:S(2)}, u32[]{:S(2)}) collective-permute-start(bf16[8,128,1024]{2,1,0:T(8,128)(2,1)} %bitcast.71), channel_id=1, source_target_pairs={{0,1},{1,0},{2,3},{3,2},{4,5},{5,4},{6,7},{7,6},{8,9},{9,8},{10,11... | collective-permute-start | bytes 6291464 | tf_op jit(solution)/shard_map/ppermute | solution.py:16
  160.9 24.6 %collective-permute-start.10 = (bf16[640,768]{1,0:T(8,128)(2,1)S(1)}, bf16[640,768]{1,0:T(8,128)(2,1)S(1)}, u32[]{:S(2)}, u32[]{:S(2)}) collective-permute-start(bf16[640,768]{1,0:T(8,128)(2,1)S(1)} %copy-done.4), channel_id=1, source_target_pairs={{0,16},{16,0},{1,17},{17,1},{2,18},{18,2},{3,19},{19,3},{4,20},{20... | collective-permute-start | bytes 2949128 | tf_op jit(solution)/shard_map/ppermute | solution.py:16
  162.4 46.3 %collective-permute-start.24 = (bf16[640,768]{1,0:T(8,128)(2,1)S(1)}, bf16[640,768]{1,0:T(8,128)(2,1)}, u32[]{:S(2)}, u32[]{:S(2)}) collective-permute-start(bf16[640,768]{1,0:T(8,128)(2,1)S(1)} %copy-done.4), channel_id=1, source_target_pairs={{0,8},{1,9},{2,10},{3,11},{4,12},{5,13},{6,14},{7,15},{8,0},{9,1},... | collective-permute-start | bytes 2949128 | tf_op jit(solution)/shard_map/ppermute | solution.py:16
  167.9 8.8 %copy-start.17 = (s32[16,128]{1,0:T(8,128)S(1)}, s32[16,128]{1,0:T(8,128)}, u32[]{:S(2)}) copy-start(s32[16,128]{1,0:T(8,128)} %get-tuple-element.96.refs_1_) | copy-start | bytes 24580
  175.2 33.5 %collective-permute-start.23 = (bf16[1,640,768]{2,1,0:T(8,128)(2,1)}, bf16[1,640,768]{2,1,0:T(8,128)(2,1)}, u32[]{:S(2)}, u32[]{:S(2)}) collective-permute-start(bf16[1,640,768]{2,1,0:T(8,128)(2,1)} %shard_map.129.refs_6_), channel_id=1, source_target_pairs={{0,16},{16,0},{1,17},{17,1},{2,18},{18,2},{3,19},{19,3},{4,20},{20... | collective-permute-start | bytes 2949128 | tf_op jit(solution)/shard_map/ppermute | solution.py:16
  185.5 0.9 copy-start.6
  199.8 15.3 %collective-permute-start.17 = (bf16[1024,512]{1,0:T(8,128)(2,1)}, bf16[1024,512]{1,0:T(8,128)(2,1)S(1)}, u32[]{:S(2)}, u32[]{:S(2)}) collective-permute-start(bf16[1024,512]{1,0:T(8,128)(2,1)} %get-tuple-element.59.refs_5_), channel_id=1, source_target_pairs={{0,1},{1,0},{2,3},{3,2},{4,5},{5,4},{6,7},{7,6},{8,9},{9,8},{10,11... | collective-permute-start | bytes 3145736 | tf_op jit(solution)/shard_map/ppermute | solution.py:16
  199.8 15.3 %collective-permute-start.18 = (bf16[1024,512]{1,0:T(8,128)(2,1)}, bf16[1024,512]{1,0:T(8,128)(2,1)}, u32[]{:S(2)}, u32[]{:S(2)}) collective-permute-start(bf16[1024,512]{1,0:T(8,128)(2,1)} %get-tuple-element.60), channel_id=1, source_target_pairs={{0,1},{1,0},{2,3},{3,2},{4,5},{5,4},{6,7},{7,6},{8,9},{9,8},{10,11... | collective-permute-start | bytes 3145736 | tf_op jit(solution)/shard_map/ppermute | solution.py:16
  200.3 14.8 %collective-permute-start.19 = (bf16[1024,512]{1,0:T(8,128)(2,1)}, bf16[1024,512]{1,0:T(8,128)(2,1)}, u32[]{:S(2)}, u32[]{:S(2)}) collective-permute-start(bf16[1024,512]{1,0:T(8,128)(2,1)} %get-tuple-element.61), channel_id=1, source_target_pairs={{0,1},{1,0},{2,3},{3,2},{4,5},{5,4},{6,7},{7,6},{8,9},{9,8},{10,11... | collective-permute-start | bytes 3145736 | tf_op jit(solution)/shard_map/ppermute | solution.py:16
  208.7 6.4 %collective-permute-start.20 = (bf16[1024,512]{1,0:T(8,128)(2,1)}, bf16[1024,512]{1,0:T(8,128)(2,1)}, u32[]{:S(2)}, u32[]{:S(2)}) collective-permute-start(bf16[1024,512]{1,0:T(8,128)(2,1)} %get-tuple-element.62), channel_id=1, source_target_pairs={{0,1},{1,0},{2,3},{3,2},{4,5},{5,4},{6,7},{7,6},{8,9},{9,8},{10,11... | collective-permute-start | bytes 3145736 | tf_op jit(solution)/shard_map/ppermute | solution.py:16
  214.5 45.4 %collective-permute-start.25 = (bf16[2,640,768]{2,1,0:T(8,128)(2,1)}, bf16[2,640,768]{2,1,0:T(8,128)(2,1)}, u32[]{:S(2)}, u32[]{:S(2)}) collective-permute-start(bf16[2,640,768]{2,1,0:T(8,128)(2,1)} %shard_map.132.refs_2_.refs_4_.refs_3_), channel_id=1, source_target_pairs={{0,16},{16,0},{1,17},{17,1},{2,18},{18,2},{3,19},{19,3},{4,20},{20... | collective-permute-start | bytes 5898248 | tf_op jit(solution)/shard_map/ppermute | solution.py:16
  215.1 1.0 copy-start.11
  216.0 6.8 %copy-start = (bf16[2,640,768]{2,1,0:T(8,128)(2,1)S(1)}, bf16[2,640,768]{2,1,0:T(8,128)(2,1)}, u32[]{:S(2)}) copy-start(bf16[2,640,768]{2,1,0:T(8,128)(2,1)} %shard_map.132.refs_2_.refs_4_.refs_3_) | copy-start | bytes 5898244
  221.9 59.5 %collective-permute-start.21 = (bf16[2,2,128,1024]{3,2,1,0:T(8,128)(2,1)}, bf16[2,2,128,1024]{3,2,1,0:T(8,128)(2,1)}, u32[]{:S(2)}, u32[]{:S(2)}) collective-permute-start(bf16[2,2,128,1024]{3,2,1,0:T(8,128)(2,1)} %get-tuple-element.64.refs_8_), channel_id=1, source_target_pairs={{0,2},{1,3},{2,0},{3,1},{4,6},{5,7},{6,4},{7,5},{8,10},{9,11},{10,... | collective-permute-start | bytes 3145736 | tf_op jit(solution)/shard_map/ppermute | solution.py:16
  222.5 58.9 %collective-permute-start.22 = (bf16[2,2,128,1024]{3,2,1,0:T(8,128)(2,1)}, bf16[2,2,128,1024]{3,2,1,0:T(8,128)(2,1)}, u32[]{:S(2)}, u32[]{:S(2)}) collective-permute-start(bf16[2,2,128,1024]{3,2,1,0:T(8,128)(2,1)} %get-tuple-element.66), channel_id=1, source_target_pairs={{0,4},{1,5},{2,6},{3,7},{4,0},{5,1},{6,2},{7,3},{8,12},{9,13},{10,... | collective-permute-start | bytes 3145736 | tf_op jit(solution)/shard_map/ppermute | solution.py:16
  222.9 88.3 %collective-permute-start.31 = (bf16[2,640,768]{2,1,0:T(8,128)(2,1)S(1)}, bf16[2,640,768]{2,1,0:T(8,128)(2,1)}, u32[]{:S(2)}, u32[]{:S(2)}) collective-permute-start(bf16[2,640,768]{2,1,0:T(8,128)(2,1)S(1)} %copy-done), channel_id=1, source_target_pairs={{0,8},{1,9},{2,10},{3,11},{4,12},{5,13},{6,14},{7,15},{8,0},{9,1},... | collective-permute-start | bytes 5898248 | tf_op jit(solution)/shard_map/ppermute | solution.py:16
  284.7 1.2 copy-start.18
  284.7 6.6 %collective-permute-start.29 = (bf16[1024,768]{1,0:T(8,128)(2,1)}, bf16[1024,768]{1,0:T(8,128)(2,1)}, u32[]{:S(2)}, u32[]{:S(2)}) collective-permute-start(bf16[1024,768]{1,0:T(8,128)(2,1)} %shard_map.135), channel_id=1, source_target_pairs={{0,1},{1,0},{2,3},{3,2},{4,5},{5,4},{6,7},{7,6},{8,9},{9,8},{10,11... | collective-permute-start | bytes 4718600 | tf_op jit(solution)/shard_map/ppermute | solution.py:16
  284.8 7.5 %collective-permute-start.28 = (bf16[1024,768]{1,0:T(8,128)(2,1)}, bf16[1024,768]{1,0:T(8,128)(2,1)}, u32[]{:S(2)}, u32[]{:S(2)}) collective-permute-start(bf16[1024,768]{1,0:T(8,128)(2,1)} %get-tuple-element.72), channel_id=1, source_target_pairs={{0,1},{1,0},{2,3},{3,2},{4,5},{5,4},{6,7},{7,6},{8,9},{9,8},{10,11... | collective-permute-start | bytes 4718600 | tf_op jit(solution)/shard_map/ppermute | solution.py:16
  285.9 5.4 %collective-permute-start.30 = (bf16[1024,512]{1,0:T(8,128)(2,1)S(1)}, bf16[1024,512]{1,0:T(8,128)(2,1)}, u32[]{:S(2)}, u32[]{:S(2)}) collective-permute-start(bf16[1024,512]{1,0:T(8,128)(2,1)S(1)} %copy-done.18), channel_id=1, source_target_pairs={{0,1},{1,0},{2,3},{3,2},{4,5},{5,4},{6,7},{7,6},{8,9},{9,8},{10,11... | collective-permute-start | bytes 3145736 | tf_op jit(solution)/shard_map/ppermute | solution.py:16
  285.9 24.5 %collective-permute-start.32 = (bf16[640,768]{1,0:T(8,128)(2,1)}, bf16[640,768]{1,0:T(8,128)(2,1)}, u32[]{:S(2)}, u32[]{:S(2)}) collective-permute-start(bf16[640,768]{1,0:T(8,128)(2,1)} %collective-permute-done.24.refs_6_.refs_5_), channel_id=1, source_target_pairs={{0,16},{16,0},{1,17},{17,1},{2,18},{18,2},{3,19},{19,3},{4,20},{20... | collective-permute-start | bytes 2949128 | tf_op jit(solution)/shard_map/ppermute | solution.py:16
  291.3 31.0 %collective-permute-start.26 = (bf16[2,128,1024]{2,1,0:T(8,128)(2,1)}, bf16[2,128,1024]{2,1,0:T(8,128)(2,1)}, u32[]{:S(2)}, u32[]{:S(2)}) collective-permute-start(bf16[2,128,1024]{2,1,0:T(8,128)(2,1)} %get-tuple-element.69.refs_1_), channel_id=1, source_target_pairs={{0,4},{1,5},{2,6},{3,7},{4,0},{5,1},{6,2},{7,3},{8,12},{9,13},{10,... | collective-permute-start | bytes 1572872 | tf_op jit(solution)/shard_map/ppermute | solution.py:16
  291.3 31.0 %collective-permute-start.27 = (bf16[2,128,1024]{2,1,0:T(8,128)(2,1)}, bf16[2,128,1024]{2,1,0:T(8,128)(2,1)}, u32[]{:S(2)}, u32[]{:S(2)}) collective-permute-start(bf16[2,128,1024]{2,1,0:T(8,128)(2,1)} %get-tuple-element.71), channel_id=1, source_target_pairs={{0,2},{1,3},{2,0},{3,1},{4,6},{5,7},{6,4},{7,5},{8,10},{9,11},{10,... | collective-permute-start | bytes 1572872 | tf_op jit(solution)/shard_map/ppermute | solution.py:16
  311.2 44.7 %collective-permute-start.35 = (bf16[2,2,128,1024]{3,2,1,0:T(8,128)(2,1)}, bf16[2,2,128,1024]{3,2,1,0:T(8,128)(2,1)S(1)}, u32[]{:S(2)}, u32[]{:S(2)}) collective-permute-start(bf16[2,2,128,1024]{3,2,1,0:T(8,128)(2,1)} %shard_map.137.refs_4_), channel_id=1, source_target_pairs={{0,4},{1,5},{2,6},{3,7},{4,0},{5,1},{6,2},{7,3},{8,12},{9,13},{10,... | collective-permute-start | bytes 3145736 | tf_op jit(solution)/shard_map/ppermute | solution.py:16
  311.2 44.7 %collective-permute-start.34 = (bf16[2,2,128,1024]{3,2,1,0:T(8,128)(2,1)}, bf16[2,2,128,1024]{3,2,1,0:T(8,128)(2,1)}, u32[]{:S(2)}, u32[]{:S(2)}) collective-permute-start(bf16[2,2,128,1024]{3,2,1,0:T(8,128)(2,1)} %get-tuple-element.79), channel_id=1, source_target_pairs={{0,2},{1,3},{2,0},{3,1},{4,6},{5,7},{6,4},{7,5},{8,10},{9,11},{10,... | collective-permute-start | bytes 3145736 | tf_op jit(solution)/shard_map/ppermute | solution.py:16
  324.8 5.2 %copy-start.3 = (f32[8,2,128,128]{3,2,1,0:T(8,128)S(1)}, f32[8,2,128,128]{3,2,1,0:T(8,128)}, u32[]{:S(2)}) copy-start(f32[8,2,128,128]{3,2,1,0:T(8,128)} %copy-done.2) | copy-start | bytes 3145732
  324.8 5.6 %copy-start.20 = (s32[16]{0:T(128)S(1)}, s32[16]{0:T(128)}, u32[]{:S(2)}) copy-start(s32[16]{0:T(128)} %copy-done.19) | copy-start | bytes 196
  324.8 26.5 %collective-permute-start.33 = (bf16[128,2048]{1,0:T(8,128)(2,1)}, bf16[128,2048]{1,0:T(8,128)(2,1)}, u32[]{:S(2)}, u32[]{:S(2)}) collective-permute-start(bf16[128,2048]{1,0:T(8,128)(2,1)} %get-tuple-element.77.refs_11_), channel_id=1, source_target_pairs={{0,8},{1,9},{2,10},{3,11},{4,12},{5,13},{6,14},{7,15},{8,0},{9,1},... | collective-permute-start | bytes 1572872 | tf_op jit(solution)/shard_map/ppermute | solution.py:16
  327.8 34.7 %collective-permute-start.38 = (bf16[640,768]{1,0:T(8,128)(2,1)}, bf16[640,768]{1,0:T(8,128)(2,1)}, u32[]{:S(2)}, u32[]{:S(2)}) collective-permute-start(bf16[640,768]{1,0:T(8,128)(2,1)} %get-tuple-element.90), channel_id=1, source_target_pairs={{0,16},{16,0},{1,17},{17,1},{2,18},{18,2},{3,19},{19,3},{4,20},{20... | collective-permute-start | bytes 2949128 | tf_op jit(solution)/shard_map/ppermute | solution.py:16
  355.9 1.0 copy-start.10
  360.1 17.2 %collective-permute-start.36 = (bf16[2,128,1024]{2,1,0:T(8,128)(2,1)}, bf16[2,128,1024]{2,1,0:T(8,128)(2,1)}, u32[]{:S(2)}, u32[]{:S(2)}) collective-permute-start(bf16[2,128,1024]{2,1,0:T(8,128)(2,1)} %get-tuple-element.82.refs_11_), channel_id=1, source_target_pairs={{0,4},{1,5},{2,6},{3,7},{4,0},{5,1},{6,2},{7,3},{8,12},{9,13},{10,... | collective-permute-start | bytes 1572872 | tf_op jit(solution)/shard_map/ppermute | solution.py:16
  360.1 17.2 %collective-permute-start.37 = (bf16[2,128,1024]{2,1,0:T(8,128)(2,1)}, bf16[2,128,1024]{2,1,0:T(8,128)(2,1)}, u32[]{:S(2)}, u32[]{:S(2)}) collective-permute-start(bf16[2,128,1024]{2,1,0:T(8,128)(2,1)} %get-tuple-element.84), channel_id=1, source_target_pairs={{0,2},{1,3},{2,0},{3,1},{4,6},{5,7},{6,4},{7,5},{8,10},{9,11},{10,... | collective-permute-start | bytes 1572872 | tf_op jit(solution)/shard_map/ppermute | solution.py:16
  361.1 23.4 %collective-permute-start.40 = (bf16[640,768]{1,0:T(8,128)(2,1)S(1)}, bf16[640,768]{1,0:T(8,128)(2,1)S(1)}, u32[]{:S(2)}, u32[]{:S(2)}) collective-permute-start(bf16[640,768]{1,0:T(8,128)(2,1)S(1)} %get-tuple-element.89), channel_id=1, source_target_pairs={{0,16},{16,0},{1,17},{17,1},{2,18},{18,2},{3,19},{19,3},{4,20},{20... | collective-permute-start | bytes 2949128 | tf_op jit(solution)/shard_map/ppermute | solution.py:16
  379.7 25.8 %collective-permute-start.39 = (bf16[128,2048]{1,0:T(8,128)(2,1)}, bf16[128,2048]{1,0:T(8,128)(2,1)}, u32[]{:S(2)}, u32[]{:S(2)}) collective-permute-start(bf16[128,2048]{1,0:T(8,128)(2,1)} %get-tuple-element.86.refs_11_), channel_id=1, source_target_pairs={{0,8},{1,9},{2,10},{3,11},{4,12},{5,13},{6,14},{7,15},{8,0},{9,1},... | collective-permute-start | bytes 1572872 | tf_op jit(solution)/shard_map/ppermute | solution.py:16
  384.5 1.0 copy-start.12
